TPU v7x, 32 devices: a whole 2x2x4 slice. The times are simulated.
32 devices in a mesh: dp: 8 (over y, x, core), seq: 4 (over z).
Axes of the slice: x: 2, y: 2, z: 4, core: 2. Of those that a mesh axis runs over, the one named last changes fastest.
Arguments:
- hidden_in: bfloat16 [8, 8, 128, 768], P('dp', 'seq'), may hold values from -6 to 6
- stretch_order: int32 [8], replicated, may hold values from 0 to 7, each once
- doc_lengths: int32 [8, 4], P('dp'), may hold values from 1 to 896, 1024 in all within a row
- attn_gain: bfloat16 [768], P(('dp', 'seq')), may hold values from 0.5 to 1.5
- attn_shift: bfloat16 [768], P(('dp', 'seq')), may hold values from -1 to 1
- feed_gain: bfloat16 [768], P(('dp', 'seq')), may hold values from 0.5 to 1.5
- feed_shift: bfloat16 [768], P(('dp', 'seq')), may hold values from -1 to 1
- qkv_weight: bfloat16 [768, 2304], P(('dp', 'seq')), may hold values from -0.21875 to 0.21875
- qkv_bias: bfloat16 [2304], P(('dp', 'seq')), may hold values from -1 to 1
- out_weight: bfloat16 [768, 768], P(('dp', 'seq')), may hold values from -1.75 to 1.75
- out_bias: bfloat16 [768], P(('dp', 'seq')), may hold values from -1 to 1
- up_weight: bfloat16 [768, 3072], P(('dp', 'seq')), may hold values from -0.21875 to 0.21875
- up_bias: bfloat16 [3072], P(('dp', 'seq')), may hold values from -1 to 1
- down_weight: bfloat16 [3072, 768], P(('dp', 'seq')), may hold values from -0.109375 to 0.109375
- down_bias: bfloat16 [768], P(('dp', 'seq')), may hold values from -1 to 1
- grad_out: bfloat16 [8, 8, 128, 768], P('dp', 'seq'), may hold values from -6 to 6
Outputs:
- hidden_out: bfloat16 [8, 8, 128, 768], P('dp', 'seq')
- grad_in: bfloat16 [8, 8, 128, 768], P('dp', 'seq')
- grad_attn_gain: float32 [768], P(('dp', 'seq'))
- grad_attn_shift: float32 [768], P(('dp', 'seq'))
- grad_feed_gain: float32 [768], P(('dp', 'seq'))
- grad_feed_shift: float32 [768], P(('dp', 'seq'))
- grad_qkv_weight: float32 [768, 2304], P(('dp', 'seq'))
- grad_qkv_bias: float32 [2304], P(('dp', 'seq'))
- grad_out_weight: float32 [768, 768], P(('dp', 'seq'))
- grad_out_bias: float32 [768], P(('dp', 'seq'))
- grad_up_weight: float32 [768, 3072], P(('dp', 'seq'))
- grad_up_bias: float32 [3072], P(('dp', 'seq'))
- grad_down_weight: float32 [3072, 768], P(('dp', 'seq'))
- grad_down_bias: float32 [768], P(('dp', 'seq'))
Inputs may be any that keep to these rules, and one draw needn't show every extreme that they name: `stretch_order`: each value 0 to 7 stands once. `doc_lengths`: each row sums to 1024, and its largest entry is exactly 896.
All inputs are finite; a program needn't handle non-finite values.
Results may differ from a plain program's by a relative error of at most 0.0095.
Values may be sent and summed in bfloat16 or wider, within the bound.
No kernel may reach another device: no remote copies, remote signals or barrier semaphores. Data moves between devices by JAX's collectives and lax.ppermute only.
A program may use at most 192 MiB of HBM per device.

v0:
```python
import math

import jax
import jax.numpy as jnp
from jax import lax
from jax.sharding import PartitionSpec as P

HD = 64
ROT = 16


eps = 1e-05
masked = -1e30


def layer_norm(rows, gain, shift):
    mean = jnp.mean(rows, axis=-1, keepdims=True)
    centred = rows - mean
    spread = jnp.mean(centred * centred, axis=-1, keepdims=True)
    return centred * lax.rsqrt(spread + eps) * gain + shift


def frequencies():
    return jnp.power(10000.0, -2.0 * jnp.arange(ROT // 2, dtype=jnp.float32) / ROT)


def rotate(heads, cosine, sine):
    half_rot = ROT // 2
    first = heads[..., :half_rot]
    second = heads[..., half_rot:ROT]
    return jnp.concatenate(
        [first * cosine - second * sine, second * cosine + first * sine, heads[..., ROT:]], axis=-1
    )


def doc_ids(positions, ends):
    return jnp.sum((positions[None, :, None] >= ends[:, None, :]).astype(jnp.int32), axis=-1)


def times_transposed(left, right):
    return lax.dot_general(
        left, right, (((1,), (1,)), ((), ())), preferred_element_type=jnp.float32
    )


def inner_rows(left, right):
    return lax.dot_general(
        left, right, (((0,), (0,)), ((), ())), preferred_element_type=jnp.float32
    )


def per_device(
    hidden_in,
    stretch_order,
    doc_lengths,
    attn_gain,
    attn_shift,
    feed_gain,
    feed_shift,
    qkv_weight,
    qkv_bias,
    out_weight,
    out_bias,
    up_weight,
    up_bias,
    down_weight,
    down_bias,
    grad_out,
):
    whole = (
        lax.all_gather(attn_gain, ("dp", "seq"), axis=0, tiled=True),
        lax.all_gather(attn_shift, ("dp", "seq"), axis=0, tiled=True),
        lax.all_gather(feed_gain, ("dp", "seq"), axis=0, tiled=True),
        lax.all_gather(feed_shift, ("dp", "seq"), axis=0, tiled=True),
        lax.all_gather(qkv_weight, ("dp", "seq"), axis=0, tiled=True),
        lax.all_gather(qkv_bias, ("dp", "seq"), axis=0, tiled=True),
        lax.all_gather(out_weight, ("dp", "seq"), axis=0, tiled=True),
        lax.all_gather(out_bias, ("dp", "seq"), axis=0, tiled=True),
        lax.all_gather(up_weight, ("dp", "seq"), axis=0, tiled=True),
        lax.all_gather(up_bias, ("dp", "seq"), axis=0, tiled=True),
        lax.all_gather(down_weight, ("dp", "seq"), axis=0, tiled=True),
        lax.all_gather(down_bias, ("dp", "seq"), axis=0, tiled=True),
    )
    seqs, blocks_own, half, width = hidden_in.shape
    heads = width // HD
    hidden_units = whole[8].shape[1]
    ratio = hidden_units // width
    queries = blocks_own * half
    count = seqs * queries
    scale_qk = 1.0 / math.sqrt(HD)
    lane = lax.axis_index("seq")
    offsets = jnp.arange(half, dtype=jnp.int32)
    own_blocks = lax.dynamic_slice_in_dim(stretch_order, lane * blocks_own, blocks_own)
    own_pos = (own_blocks[:, None] * half + offsets[None, :]).reshape(queries)
    ends = jnp.cumsum(doc_lengths, axis=1)[:, :-1]
    own_doc = doc_ids(own_pos, ends)
    angle = own_pos.astype(jnp.float32)[:, None] * frequencies()[None, :]
    cosine = jnp.cos(angle)[None, :, None, :]
    sine = jnp.sin(angle)[None, :, None, :]

    def allowed_of(key_pos, key_doc):
        causal = key_pos[None, None, None, :] <= own_pos[None, None, :, None]
        same = key_doc[:, None, None, :] == own_doc[:, None, :, None]
        return causal & same

    rows = hidden_in.astype(jnp.float32).reshape(count, width)
    normed_first, pull_first = jax.vjp(
        layer_norm, rows, whole[0].astype(jnp.float32), whole[1].astype(jnp.float32)
    )
    normed_second, pull_second = jax.vjp(
        layer_norm, rows, whole[2].astype(jnp.float32), whole[3].astype(jnp.float32)
    )
    first_low = normed_first.astype(jnp.bfloat16)
    second_low = normed_second.astype(jnp.bfloat16)
    mixed = jnp.dot(first_low, whole[4], preferred_element_type=jnp.float32) + whole[5].astype(
        jnp.float32
    )
    mixed = mixed.reshape(seqs, queries, 3, heads, HD)
    query = rotate(mixed[:, :, 0], cosine, sine).astype(jnp.bfloat16)
    key_own = (
        rotate(mixed[:, :, 1], cosine, sine)
        .astype(jnp.bfloat16)
        .reshape(seqs, blocks_own, half, width)
    )
    value_own = mixed[:, :, 2].astype(jnp.bfloat16).reshape(seqs, blocks_own, half, width)
    top = jnp.full((seqs, heads, queries), masked, jnp.float32)
    key_piece = lax.all_gather(key_own, "seq", axis=1, tiled=True)
    value_piece = lax.all_gather(value_own, "seq", axis=1, tiled=True)
    blocks = key_piece.shape[1]
    key_pos = (stretch_order[:, None] * half + offsets[None, :]).reshape(blocks * half)
    allowed = allowed_of(key_pos, doc_ids(key_pos, ends))
    keys = key_piece.reshape(seqs, blocks * half, heads, HD)
    values = value_piece.reshape(seqs, blocks * half, heads, HD)
    scores = (
        jnp.einsum("sqhd,skhd->shqk", query, keys, preferred_element_type=jnp.float32) * scale_qk
    )
    scores = jnp.where(allowed, scores, masked)
    new_top = jnp.maximum(top, jnp.max(scores, axis=-1))
    weights = jnp.where(allowed, jnp.exp(scores - new_top[..., None]), 0.0)
    total = jnp.sum(weights, axis=-1)
    accum = jnp.einsum(
        "shqk,skhd->shqd", weights.astype(jnp.bfloat16), values, preferred_element_type=jnp.float32
    )
    top, total, accum = (new_top, total, accum)
    logsum = top + jnp.log(total)
    heads_rows = jnp.transpose(accum / total[..., None], (0, 2, 1, 3))
    heads_low = heads_rows.reshape(count, width).astype(jnp.bfloat16)
    attended = jnp.dot(heads_low, whole[6], preferred_element_type=jnp.float32) + whole[7].astype(
        jnp.float32
    )
    inner = jnp.dot(second_low, whole[8], preferred_element_type=jnp.float32) + whole[9].astype(
        jnp.float32
    )
    active, pull_gelu = jax.vjp(lambda v: jax.nn.gelu(v, approximate=False), inner)
    active_low = active.astype(jnp.bfloat16)
    fed = jnp.dot(active_low, whole[10], preferred_element_type=jnp.float32) + whole[11].astype(
        jnp.float32
    )
    hidden_out = (rows + attended + fed).astype(jnp.bfloat16).reshape(hidden_in.shape)
    params_back = (
        lax.all_gather(attn_gain, ("dp", "seq"), axis=0, tiled=True),
        lax.all_gather(attn_shift, ("dp", "seq"), axis=0, tiled=True),
        lax.all_gather(feed_gain, ("dp", "seq"), axis=0, tiled=True),
        lax.all_gather(feed_shift, ("dp", "seq"), axis=0, tiled=True),
        lax.all_gather(qkv_weight, ("dp", "seq"), axis=0, tiled=True),
        lax.all_gather(qkv_bias, ("dp", "seq"), axis=0, tiled=True),
        lax.all_gather(out_weight, ("dp", "seq"), axis=0, tiled=True),
        lax.all_gather(out_bias, ("dp", "seq"), axis=0, tiled=True),
        lax.all_gather(up_weight, ("dp", "seq"), axis=0, tiled=True),
        lax.all_gather(up_bias, ("dp", "seq"), axis=0, tiled=True),
        lax.all_gather(down_weight, ("dp", "seq"), axis=0, tiled=True),
        lax.all_gather(down_bias, ("dp", "seq"), axis=0, tiled=True),
    )
    upstream_low = grad_out.reshape(count, width)
    upstream = upstream_low.astype(jnp.float32)
    grad_bias_out = jnp.sum(upstream, axis=0)
    grad_active = times_transposed(upstream_low, params_back[10])
    (grad_inner,) = pull_gelu(grad_active)
    inner_low = grad_inner.astype(jnp.bfloat16)
    grad_up_bias = jnp.sum(grad_inner, axis=0)
    grad_second = times_transposed(inner_low, params_back[8])
    grad_heads = times_transposed(upstream_low, params_back[6])
    heads_grad_low = grad_heads.astype(jnp.bfloat16).reshape(seqs, queries, heads, HD)
    delta = jnp.transpose(
        jnp.sum(heads_grad_low.astype(jnp.float32) * heads_rows, axis=-1), (0, 2, 1)
    )
    key_all, value_all = (
        lax.all_gather(key_own, "seq", axis=1, tiled=True),
        lax.all_gather(value_own, "seq", axis=1, tiled=True),
    )
    blocks_all = key_all.shape[1]

    def backstep(grad_query, block):
        keys = lax.dynamic_slice_in_dim(key_all, block, 1, axis=1).reshape(seqs, half, heads, HD)
        values = lax.dynamic_slice_in_dim(value_all, block, 1, axis=1).reshape(
            seqs, half, heads, HD
        )
        key_pos = lax.dynamic_slice_in_dim(stretch_order, block, 1) * half + offsets
        allowed = allowed_of(key_pos, doc_ids(key_pos, ends))
        scores = (
            jnp.einsum("sqhd,skhd->shqk", query, keys, preferred_element_type=jnp.float32)
            * scale_qk
        )
        probs = jnp.where(allowed, jnp.exp(scores - logsum[..., None]), 0.0)
        grad_probs = jnp.einsum(
            "sqhd,skhd->shqk", heads_grad_low, values, preferred_element_type=jnp.float32
        )
        grad_scores = (probs * (grad_probs - delta[..., None]) * scale_qk).astype(jnp.bfloat16)
        grad_query = grad_query + jnp.einsum(
            "shqk,skhd->sqhd", grad_scores, keys, preferred_element_type=jnp.float32
        )
        key_term = jnp.einsum(
            "shqk,sqhd->skhd", grad_scores, query, preferred_element_type=jnp.float32
        )
        value_term = jnp.einsum(
            "shqk,sqhd->skhd",
            probs.astype(jnp.bfloat16),
            heads_grad_low,
            preferred_element_type=jnp.float32,
        )
        return (
            grad_query,
            (key_term.reshape(seqs, half, width), value_term.reshape(seqs, half, width)),
        )

    grad_query, (grad_keys, grad_values) = lax.scan(
        backstep,
        jnp.zeros((seqs, queries, heads, HD), jnp.float32),
        jnp.arange(blocks_all, dtype=jnp.int32),
    )
    key_part, value_part = (
        lax.psum_scatter(
            grad_keys.astype(jnp.bfloat16), "seq", scatter_dimension=0, tiled=True
        ).astype(jnp.float32),
        lax.psum_scatter(
            grad_values.astype(jnp.bfloat16), "seq", scatter_dimension=0, tiled=True
        ).astype(jnp.float32),
    )
    key_sum = jnp.transpose(key_part, (1, 0, 2, 3))
    value_sum = jnp.transpose(value_part, (1, 0, 2, 3))
    query_back = rotate(grad_query, cosine, -sine).reshape(count, width)
    key_back = rotate(key_sum.reshape(seqs, queries, heads, HD), cosine, -sine).reshape(
        count, width
    )
    grad_mixed = jnp.concatenate([query_back, key_back, value_sum.reshape(count, width)], axis=1)
    mixed_low = grad_mixed.astype(jnp.bfloat16)
    grad_qkv_bias = jnp.sum(grad_mixed, axis=0)
    grad_first = times_transposed(mixed_low, params_back[4])
    rows_first, gain_first, shift_first = pull_first(grad_first)
    rows_second, gain_second, shift_second = pull_second(grad_second)
    grad_in = (upstream + rows_first + rows_second).astype(jnp.bfloat16).reshape(hidden_in.shape)
    factor = 1.0 / math.sqrt(count * lax.axis_size("dp") * lax.axis_size("seq"))
    small_columns = jnp.stack(
        [gain_first, shift_first, gain_second, shift_second, grad_bias_out], axis=1
    )
    qkv_bias_rows = grad_qkv_bias.reshape(width, 3)
    up_bias_rows = grad_up_bias.reshape(width, ratio)
    part_qkv = inner_rows(first_low, mixed_low)
    part_out = inner_rows(heads_low, upstream_low)
    part_up = inner_rows(second_low, inner_low)
    part_down = inner_rows(active_low, upstream_low).reshape(
        lax.axis_size(("dp", "seq")) * qkv_weight.shape[0], ratio * width
    )
    owned = lax.psum_scatter(
        jnp.concatenate(
            [part_qkv, part_out, part_up, part_down, small_columns, qkv_bias_rows, up_bias_rows],
            axis=1,
        )
        * factor,
        ("dp", "seq"),
        scatter_dimension=0,
        tiled=True,
    )
    own_rows = owned.shape[0]
    edge_out = 3 * width
    edge_up = edge_out + width
    edge_down = edge_up + hidden_units
    edge_small = edge_down + hidden_units
    edge_qkvb = edge_small + 5
    edge_upb = edge_qkvb + 3
    grad_qkv_own = owned[:, :edge_out]
    grad_out_own = owned[:, edge_out:edge_up]
    grad_up_own = owned[:, edge_up:edge_down]
    grad_down_own = owned[:, edge_down:edge_small].reshape(own_rows * ratio, width)
    grad_bias_own = owned[:, edge_small + 4]
    grad_qkvb_own = owned[:, edge_qkvb:edge_upb].reshape(own_rows * 3)
    grad_upb_own = owned[:, edge_upb : edge_upb + ratio].reshape(own_rows * ratio)
    return (
        hidden_out,
        grad_in,
        owned[:, edge_small],
        owned[:, edge_small + 1],
        owned[:, edge_small + 2],
        owned[:, edge_small + 3],
        grad_qkv_own,
        grad_qkvb_own,
        grad_out_own,
        grad_bias_own,
        grad_up_own,
        grad_upb_own,
        grad_down_own,
        grad_bias_own,
    )


def solution(mesh):
    in_specs = (
        P("dp", "seq", None, None),
        P(),
        P("dp", None),
        P(("dp", "seq")),
        P(("dp", "seq")),
        P(("dp", "seq")),
        P(("dp", "seq")),
        P(("dp", "seq"), None),
        P(("dp", "seq")),
        P(("dp", "seq"), None),
        P(("dp", "seq")),
        P(("dp", "seq"), None),
        P(("dp", "seq")),
        P(("dp", "seq"), None),
        P(("dp", "seq")),
        P("dp", "seq", None, None),
    )
    out_specs = (
        P("dp", "seq", None, None),
        P("dp", "seq", None, None),
        P(("dp", "seq")),
        P(("dp", "seq")),
        P(("dp", "seq")),
        P(("dp", "seq")),
        P(("dp", "seq"), None),
        P(("dp", "seq")),
        P(("dp", "seq"), None),
        P(("dp", "seq")),
        P(("dp", "seq"), None),
        P(("dp", "seq")),
        P(("dp", "seq"), None),
        P(("dp", "seq")),
    )
    return jax.shard_map(
        per_device, mesh=mesh, in_specs=in_specs, out_specs=out_specs, check_vma=False
    )
```

profile of v0, /device:TPU:0, one launch (start us, length us, event | category | flops | bytes accessed | tf_op | source)
XLA Modules:
  0.0 959.7 jit_solution(11660358668159368766)
XLA Ops:
  15.5 42.9 %all-reduce.9 = (bf16[768]{0:T(1024)(128)(2,1)S(1)}, bf16[768]{0:T(1024)(128)(2,1)S(1)}, bf16[3072]{0:T(1024)(128)(2,1)}, bf16[768]{0:T(1024)(128)(2,1)}, bf16[7...) all-reduce(bf16[768]{0:T(1024)(128)(2,1)S(1)} %dynamic-update-slice, ...), channel_id=1, replica_groups=mesh['dp'=8,'seq'=4] {'dp','seq'}, use_global_device_ids=true, to_apply=%add.5 | all-reduce | flops 9984 | bytes 39936
  65.6 8.2 all-gather.7.cloned.1.call-done
  73.8 4.5 convolution_add_fusion
  89.2 40.3 %all-gather.13.cloned.1.call-done = bf16[768,768]{1,0:T(8,128)(2,1)} async-done(((bf16[24,768]{1,0:T(8,128)(2,1)}), bf16[768,768]{1,0:T(8,128)(2,1)}) %all-gather.13.cloned.1.call-update) | async-done | bytes 1179664 | tf_op jit(solution)/shard_map/all_gather | solution.py:77
  135.2 32.5 %all-gather.9.cloned.1.call-done = bf16[1,8,128,768]{3,2,0,1:T(8,128)(2,1)} async-done(((bf16[1,2,128,768]{3,2,0,1:T(8,128)(2,1)}), bf16[1,8,128,768]{3,2,0,1:T(8,128)(2,1)}) %all-gather.9.cloned.1.call-update) | async-done | bytes 1572880 | tf_op jit(solution)/shard_map/all_gather | solution.py:127
  172.0 7.2 fusion.15
  179.2 25.9 %all-gather.11.cloned.1.call-done = bf16[1,8,128,768]{3,2,0,1:T(8,128)(2,1)} async-done(((bf16[1,2,128,768]{3,2,0,1:T(8,128)(2,1)}), bf16[1,8,128,768]{3,2,0,1:T(8,128)(2,1)}) %all-gather.11.cloned.1.call-update) | async-done | bytes 1572880 | tf_op jit(solution)/shard_map/all_gather | solution.py:128
  205.1 2.1 copy.103
  209.4 8.8 fusion.16
  218.8 5.5 multiply_reduce_fusion.4
  224.8 141.6 %while.15 = (s32[]{:T(128)}, f32[1,256,12,64]{1,3,2,0:T(8,128)S(1)}, bf16[8,1,128,768]{2,3,1,0:T(8,128)(2,1)}, bf16[8,1,128,768]{3,2,0,1:T(8,128)(2,1)}, s32[8]{...) while((s32[]{:T(128)}, ...), condition=%wide.region_10.11_spmd.clone, body=%wide.region_8.10_spmd.clone.sunk | while | flops 255296896 | bytes 14841673 | solution.py:226
  369.2 5.7 convolution_add_fusion.1
  375.2 11.4 %fusion.66 = (f32[3072]{0:T(1024)S(1)}, bf16[256,3072]{1,0:T(8,128)(2,1)}, f32[256,3072]{1,0:T(8,128)S(1)}) fusion(f32[256,3072]{1,0:T(8,128)} %convolution_add_fusion.1, bf16[256,768]{1,0:T(8,128)(2,1)S(1)} %bitcast.225, bf16[3072,768]{1,0:T(8,128)(2,1)} %all-gather.17.cloned.1.call-done), kind=kOutput, calls=%fused_computation.147 | convolution fusion | flops 1265366016 | bytes 12988416 | tf_op jit(solution)/shard_map/dot_general | solution.py:41
  387.2 5.1 fusion.72
  392.3 11.5 %reshape.849 = f32[768,3072]{1,0:T(8,128)} reshape(f32[3072,768]{1,0:T(8,128)} %fusion.72) | data formatting | bytes 18874368 | tf_op jit(solution)/shard_map/reshape | solution.py:261
  405.0 5.3 fusion.40
  410.3 5.1 fusion.38
  419.5 17.9 %reduce-scatter.3.cloned.1.call-done = bf16[2,1,128,768]{2,3,1,0:T(8,128)(2,1)} async-done(((bf16[8,1,128,768]{2,3,1,0:T(8,128)(2,1)}), bf16[2,1,128,768]{2,3,1,0:T(8,128)(2,1)}) %reduce-scatter.3.cloned.1.call-update) | async-done | bytes 393232 | tf_op jit(solution)/shard_map/reduce_scatter | solution.py:232
  437.4 2.3 copy.107
  442.9 4.1 fusion.58
  456.1 31.9 %concatenate.49 = f32[768,9228]{1,0:T(8,128)} concatenate(f32[768,2304]{1,0:T(8,128)} %fusion.58, f32[768,768]{1,0:T(8,128)S(1)} %copy-done.5, f32[768,3072]{1,0:T(8,128)} %fusion.38, f32[768,3072]{1,0:T(8,128)} %reshape.849, f32[768,1]{1,0:T(8,128)} %stack.20, f32[768,1]{1,0:T(8,128)} %stack.21, f32[768,1]{1,0:T(8,128)} %stack.22, f32[768,1]{1,0:T(8,128)} %stack.23, ...), dimensions={1} | concatenate | bytes 56696832 | tf_op jit(solution)/shard_map/concatenate | solution.py:265
  488.0 20.9 %broadcast_multiply_fusion = f32[768,9228]{1,0:T(8,128)} fusion(f32[768,9228]{1,0:T(8,128)} %concatenate.49), kind=kLoop, calls=%fused_computation.24 | loop fusion | flops 7087104 | bytes 56696832 | tf_op jit(solution)/shard_map/mul | solution.py:265
  510.3 3.8 convolution_add_fusion.3
  516.9 425.3 %all-reduce.12.cloned.1.call-done = f32[768,9228]{1,0:T(8,128)} async-done(((f32[768,9228]{1,0:T(8,128)}), f32[768,9228]{1,0:T(8,128)}) %all-reduce.12.cloned.1.call-update) | async-done | bytes 28348432
  (369 shorter events, 195.6 us)
Async XLA Ops:
  7.2 66.6 %all-gather.7.cloned.1.call-start = ((), (), s32[]{:S(2)}) async-start(), calls=%async_computation.2 | async-start | bytes 3649536 | tf_op jit(solution)/shard_map/all_gather | solution.py:75
  7.9 121.6 %all-gather.13.cloned.1.call-start = ((), (), s32[]{:S(2)}) async-start(), calls=%async_computation.5 | async-start | bytes 1216512 | tf_op jit(solution)/shard_map/all_gather | solution.py:77
  8.7 159.0 %all-gather.9.cloned.1.call-start = ((), (), s32[]{:S(2)}) async-start(), calls=%async_computation.3 | async-start | bytes 1966080 | tf_op jit(solution)/shard_map/all_gather | solution.py:127
  58.4 15.4 %copy-start.27 = (f32[768]{0:T(1024)}, f32[768]{0:T(1024)S(1)}, u32[]{:S(2)}) copy-start(f32[768]{0:T(1024)S(1)} %convert_element_type.174) | copy-start | bytes 9220
  59.6 14.2 %copy-start.29 = (f32[768]{0:T(1024)}, f32[768]{0:T(1024)S(1)}, u32[]{:S(2)}) copy-start(f32[768]{0:T(1024)S(1)} %convert_element_type.185) | copy-start | bytes 9220
  60.8 12.9 %copy-start.32 = (f32[256]{0:T(256)}, f32[256]{0:T(256)S(1)}, u32[]{:S(2)}) copy-start(f32[256]{0:T(256)S(1)} %get-tuple-element.299) | copy-start | bytes 3076
  62.1 11.7 %copy-start.34 = (f32[256]{0:T(256)}, f32[256]{0:T(256)S(1)}, u32[]{:S(2)}) copy-start(f32[256]{0:T(256)S(1)} %bitcast_rsqrt_fusion) | copy-start | bytes 3076
  63.6 17.0 %copy-start.25 = (f32[256,8]{0,1:T(8,128)}, f32[256,8]{0,1:T(8,128)S(1)}, u32[]{:S(2)}) copy-start(f32[256,8]{0,1:T(8,128)S(1)} %get-tuple-element.298) | copy-start | bytes 24580
  65.6 12.7 %copy-start.16 = (bf16[256,768]{1,0:T(8,128)(2,1)}, bf16[256,768]{1,0:T(8,128)(2,1)S(1)}, u32[]{:S(2)}) copy-start(bf16[256,768]{1,0:T(8,128)(2,1)S(1)} %get-tuple-element.288) | copy-start | bytes 1179652
  82.1 47.4 %copy-start.3 = (bf16[1,2,128,768]{3,2,1,0:T(8,128)(2,1)S(1)}, bf16[1,2,128,768]{3,2,1,0:T(8,128)(2,1)}, u32[]{:S(2)}) copy-start(bf16[1,2,128,768]{3,2,1,0:T(8,128)(2,1)} %param.33) | copy-start | bytes 1179652
  83.3 121.8 %all-gather.11.cloned.1.call-start = ((), (), s32[]{:S(2)}) async-start(), calls=%async_computation.4 | async-start | bytes 1966080 | tf_op jit(solution)/shard_map/all_gather | solution.py:128
  83.4 50.9 %copy-start.23 = (bf16[1,256,12,8]{1,3,2,0:T(8,128)(2,1)S(1)}, bf16[1,256,12,8]{1,3,2,0:T(8,128)(2,1)}, u32[]{:S(2)}) copy-start(bf16[1,256,12,8]{1,3,2,0:T(8,128)(2,1)} %get-tuple-element.282) | copy-start | bytes 147460
  83.4 50.9 %copy-start.24 = (bf16[1,256,12,8]{1,3,2,0:T(8,128)(2,1)S(1)}, bf16[1,256,12,8]{1,3,2,0:T(8,128)(2,1)}, u32[]{:S(2)}) copy-start(bf16[1,256,12,8]{1,3,2,0:T(8,128)(2,1)} %get-tuple-element.283) | copy-start | bytes 147460
  84.6 284.5 %all-gather.15.cloned.1.call-start = ((), (), s32[]{:S(2)}) async-start(), calls=%async_computation.6 | async-start | bytes 4866048 | tf_op jit(solution)/shard_map/all_gather | solution.py:79
  85.2 289.9 %all-gather.17.cloned.1.call-start = ((), (), s32[]{:S(2)}) async-start(), calls=%async_computation.7 | async-start | bytes 4866048 | tf_op jit(solution)/shard_map/all_gather | solution.py:81
  85.8 332.3 %reduce-scatter.5.cloned.1.call-start = ((), (), s32[]{:S(2)}) async-start(), calls=%async_computation.9 | async-start | bytes 1966080 | tf_op jit(solution)/shard_map/reduce_scatter | solution.py:235
  135.2 36.8 %copy-start.22 = (bf16[256,12,48]{0,2,1:T(8,128)(2,1)S(1)}, bf16[256,12,48]{0,2,1:T(8,128)(2,1)}, u32[]{:S(2)}) copy-start(bf16[256,12,48]{0,2,1:T(8,128)(2,1)} %slice_bitcast_fusion.3) | copy-start | bytes 884740
  209.4 9.4 copy-start
  366.4 71.0 %reduce-scatter.3.cloned.1.call-start = ((), (), s32[]{:S(2)}) async-start(), calls=%async_computation.8 | async-start | bytes 1966080 | tf_op jit(solution)/shard_map/reduce_scatter | solution.py:232
  374.9 567.3 %all-reduce.12.cloned.1.call-start = ((), (), s32[]{:S(2)}) async-start(), calls=%async_computation.10 | async-start | bytes 57409536
  375.2 11.4 %copy-start.13 = (f32[256,3072]{1,0:T(8,128)S(1)}, f32[256,3072]{1,0:T(8,128)}, u32[]{:S(2)}) copy-start(f32[256,3072]{1,0:T(8,128)} %convolution_add_fusion.1) | copy-start | bytes 9437188
  418.1 23.4 %copy-start.26 = (f32[256,8]{0,1:T(8,128)S(1)}, f32[256,8]{0,1:T(8,128)}, u32[]{:S(2)}) copy-start(f32[256,8]{0,1:T(8,128)} %copy-done.25) | copy-start | bytes 24580
  418.1 23.4 %copy-start.31 = (f32[256,8]{0,1:T(8,128)S(1)}, f32[256,8]{0,1:T(8,128)}, u32[]{:S(2)}) copy-start(f32[256,8]{0,1:T(8,128)} %get-tuple-element.296) | copy-start | bytes 24580
  449.3 6.8 copy-start.5
  (41 other events, 156.9 us)
Sparse Core Ops, SparseCore 0:
  10.8 62.9 all-gather.6
  76.6 52.8 all-gather.12
  131.6 36.0 all-gather.8
  169.1 35.9 all-gather.10
  207.8 62.4 all-gather.14
  272.9 62.3 all-gather.16
  366.5 34.1 reduce-scatter.4
  403.0 34.2 reduce-scatter.2
  509.0 433.1 all-reduce.11
where the time goes:
time: 964 us; the launch traced here: 960 us
  waiting for transfers between devices  553 us (57%)
  local copies, waits for them, and re-layouts  149 us (15%)
  matrix products  111 us (12%)
  other arithmetic  67.9 us (7%)
  blocking collectives  42.9 us (4%)
  loops' own time  21.5 us (2%)
  between operations  14.5 us (2%)
    unnamed x10, waiting for transfers between devices  428 us
    unnamed x1, blocking collectives  42.9 us
    all_gather x1, waiting for transfers between devices, per_device(): lax.all_gather(out_weight, ('dp', 'seq'), axis=0, tiled=True)  40.3 us
    all_gather x1, waiting for transfers between devices, per_device(): key_piece = lax.all_gather(key_own, 'seq', axis=1, tiled=True)  32.5 us
    concatenate x1, local copies, waits for them, and re-layouts, per_device(): jnp.concatenate([part_qkv, part_out, part_up, part_down, small_columns, q...  31.9 us
    all_gather x1, waiting for transfers between devices, per_device(): value_piece = lax.all_gather(value_own, 'seq', axis=1, tiled=True)  25.9 us
    another operation x1, loops' own time, per_device(): lax.scan(backstep, jnp.zeros((seqs, queries, heads, HD), jnp.float32), jn...  21.5 us
    mul x1, other arithmetic, per_device(): jnp.concatenate([part_qkv, part_out, part_up, part_down, small_columns, q...  20.9 us
  transfers between devices with their start and end apart: 9, of which 6 were waited for; matrix products, arithmetic and copies ran while one was open for 25% of the time, Pallas kernels for 0%

commit v1 on v0

--- a/solution.py
+++ b/solution.py
@@ -3,6 +3,8 @@
 import jax
 import jax.numpy as jnp
 from jax import lax
+from jax.experimental import pallas as pl
+from jax.experimental.pallas import tpu as pltpu
 from jax.sharding import PartitionSpec as P
 
 HD = 64
@@ -49,7 +51,7 @@
     )
 
 
-def per_device(
+def per_device_split(
     hidden_in,
     stretch_order,
     doc_lengths,
@@ -303,6 +305,502 @@
     )
 
 
+f32 = jnp.float32
+bf16 = jnp.bfloat16
+
+
+def whole_block(shape):
+    return pl.BlockSpec(shape, lambda *_: (0,) * len(shape))
+
+
+def normalise(rows):
+    centred = rows - jnp.mean(rows, axis=-1, keepdims=True)
+    spread = jnp.mean(centred * centred, axis=-1, keepdims=True)
+    return centred * lax.rsqrt(spread + eps)
+
+
+def turn(upright, cosine, sine):
+    half_rot = ROT // 2
+    first = upright[:half_rot]
+    second = upright[half_rot:ROT]
+    return [first * cosine - second * sine, second * cosine + first * sine, upright[ROT:]]
+
+
+def product(left, right, left_dim=1, right_dim=0):
+    return lax.dot_general(
+        left, right, (((left_dim,), (right_dim,)), ((), ())), preferred_element_type=f32
+    )
+
+
+def front_kernel(
+    x_ref, vec_ref, bias_ref, cos_ref, sin_ref, up_ref, down_ref, attn_ref,
+    n1_ref, n2_ref, act_ref, slope_ref, fed_ref, upright_ref, rows_ref,
+):
+    hat = normalise(x_ref[...].astype(f32))
+    vec = vec_ref[...]
+    n1 = (hat * vec[0:1] + vec[1:2]).astype(bf16)
+    n2 = (hat * vec[2:3] + vec[3:4]).astype(bf16)
+    n1_ref[...] = n1
+    n2_ref[...] = n2
+    width = upright_ref.shape[0]
+    mixed = product(n1, attn_ref[:, :width]) + bias_ref[...]
+    upright = mixed.T
+    cosine, sine = cos_ref[...], sin_ref[...]
+    part = width // 3
+    pieces = []
+    for start in range(0, part, HD):
+        pieces += [v * HD**-0.5 for v in turn(upright[start : start + HD], cosine, sine)]
+    for start in range(part, 2 * part, HD):
+        pieces += turn(upright[start : start + HD], cosine, sine)
+    upright = jnp.concatenate(pieces + [upright[2 * part :]], axis=0)
+    upright_ref[...] = upright.astype(bf16)
+    mixed = upright.T.astype(bf16)
+    for j in range(width // HD):
+        rows_ref[j] = mixed[:, j * HD : (j + 1) * HD]
+    inner = product(n2, up_ref[...]) + vec[4:5]
+    phi = 0.5 + 0.5 * lax.erf(inner * math.sqrt(0.5))
+    active = (inner * phi).astype(bf16)
+    act_ref[...] = active
+    bell = jnp.exp(inner * inner * -0.5) * (1.0 / math.sqrt(2.0 * math.pi))
+    slope_ref[...] = (phi + inner * bell).astype(bf16)
+    fed_ref[...] = product(active, down_ref[...])
+
+
+def attend_kernel(
+    span_ref, place_ref, key_ref, query_ref, value_ref, fed_ref, out_ref,
+    soft_ref, inv_ref, heads_ref, sum_ref, bias_ref,
+):
+    head = pl.program_id(1)
+
+    @pl.when(head == 0)
+    def _():
+        place = place_ref[...]
+        ok = (place <= span_ref[0:1]) & (place >= span_ref[1:2])
+        bias_ref[...] = jnp.where(ok, 0.0, masked)
+
+    scores = product(key_ref[head], query_ref[...]) + bias_ref[...]
+    weights = jnp.exp(scores - jnp.max(scores, axis=0, keepdims=True))
+    inverse = 1.0 / jnp.sum(weights, axis=0, keepdims=True)
+    soft = weights.astype(bf16)
+    soft_ref[0] = soft
+    inv_ref[0] = jnp.broadcast_to(inverse, inv_ref.shape[1:])
+    spot = pl.ds(pl.multiple_of(head * HD, HD), HD)
+    heads_ref[spot, :] = (product(value_ref[...], soft) * inverse).astype(bf16)
+
+    @pl.when(head == pl.num_programs(1) - 1)
+    def _():
+        sum_ref[...] = (fed_ref[...] + product(heads_ref[...], out_ref[...], 0, 0)).astype(bf16)
+
+
+def feed_back_kernel(
+    dy_ref, x_ref, act_ref, slope_ref, n2_ref, vec_ref, up_ref, down_ref,
+    scaled_ref, gup_ref, gdown_ref, sums_ref, acc_up, acc_down,
+):
+    step = pl.program_id(0)
+
+    @pl.when(step == 0)
+    def _():
+        acc_up[...] = jnp.zeros_like(acc_up)
+        acc_down[...] = jnp.zeros_like(acc_down)
+        sums_ref[...] = jnp.zeros_like(sums_ref)
+
+    dy = dy_ref[...]
+    grad_inner = product(dy, down_ref[...], 1, 1) * slope_ref[...].astype(f32)
+    low = grad_inner.astype(bf16)
+    grad = product(low, up_ref[...], 1, 1)
+    hat = normalise(x_ref[...].astype(f32))
+    scaled_ref[...] = grad * vec_ref[2:3]
+    sums_ref[0:1] += jnp.sum(grad * hat, axis=0, keepdims=True)
+    sums_ref[1:2] += jnp.sum(grad, axis=0, keepdims=True)
+    sums_ref[2:3] += jnp.sum(grad_inner, axis=0, keepdims=True)
+    acc_up[...] += product(n2_ref[...], low, 0, 0)
+    acc_down[...] += product(act_ref[...], dy, 0, 0)
+
+    @pl.when(step == pl.num_programs(0) - 1)
+    def _():
+        gup_ref[...] = acc_up[...].astype(bf16)
+        gdown_ref[...] = acc_down[...].astype(bf16)
+
+
+def attend_back_kernel(
+    dy_ref, out_ref, heads_ref, inv_ref, soft_ref, value_ref, key_ref, query_ref, cos_ref, sin_ref,
+    gquery_ref, gkey_ref, gvalue_ref, gout_ref, held_ref,
+):
+    step, head = pl.program_id(0), pl.program_id(1)
+
+    @pl.when((step == 0) & (head == 0))
+    def _():
+        gkey_ref[...] = jnp.zeros_like(gkey_ref)
+        gvalue_ref[...] = jnp.zeros_like(gvalue_ref)
+        gout_ref[...] = jnp.zeros_like(gout_ref)
+
+    @pl.when(head == 0)
+    def _():
+        dy = dy_ref[...]
+        held_ref[...] = product(out_ref[...], dy, 1, 1).astype(bf16).astype(f32)
+        gout_ref[...] += product(heads_ref[...], dy)
+
+    spot = pl.ds(pl.multiple_of(head * HD, HD), HD)
+    lifted = held_ref[spot, :] * inv_ref[0, 0:1]
+    delta = jnp.sum(lifted * heads_ref[spot, :].astype(f32), axis=0, keepdims=True)
+    lifted_rows = lifted.T.astype(bf16)
+    soft = soft_ref[0]
+    grad_soft = product(value_ref[head], lifted.astype(bf16))
+    grad_scores = (soft.astype(f32) * (grad_soft - delta)).astype(bf16)
+    gvalue_ref[head] += product(soft, lifted_rows)
+    gkey_ref[head] += product(grad_scores, query_ref[0])
+    back = product(key_ref[...], grad_scores) * HD**-0.5
+    gquery_ref[spot, :] = jnp.concatenate(turn(back, cos_ref[...], -sin_ref[...]), axis=0)
+
+
+def rear_kernel(
+    gquery_ref, gkey_ref, gvalue_ref, cos_ref, sin_ref, n1_ref, x_ref, scaled_ref, vec_ref, attn_ref,
+    total_ref, gattn_ref, sums_ref, gbias_ref, acc_ref,
+):
+    step = pl.program_id(0)
+
+    @pl.when(step == 0)
+    def _():
+        acc_ref[...] = jnp.zeros_like(acc_ref)
+        sums_ref[...] = jnp.zeros_like(sums_ref)
+        gbias_ref[...] = jnp.zeros_like(gbias_ref)
+
+    cosine, sine = cos_ref[...], sin_ref[...]
+    pieces = [gquery_ref[...]]
+    for j in range(gkey_ref.shape[0]):
+        pieces += turn(gkey_ref[j].T, cosine, -sine)
+    pieces += [gvalue_ref[j].T for j in range(gvalue_ref.shape[0])]
+    mixed = jnp.concatenate(pieces, axis=0).T
+    gbias_ref[0:1] += jnp.sum(mixed, axis=0, keepdims=True)
+    low = mixed.astype(bf16)
+    grad = product(low, attn_ref[:, : low.shape[1]], 1, 1)
+    hat = normalise(x_ref[...].astype(f32))
+    total_ref[...] = (grad * vec_ref[0:1] + scaled_ref[...]).astype(bf16)
+    sums_ref[0:1] += jnp.sum(grad * hat, axis=0, keepdims=True)
+    sums_ref[1:2] += jnp.sum(grad, axis=0, keepdims=True)
+    acc_ref[...] += product(n1_ref[...], low, 0, 0)
+
+    @pl.when(step == pl.num_programs(0) - 1)
+    def _():
+        gattn_ref[...] = acc_ref[...].astype(bf16)
+
+
+VMEM = 56 * 1024 * 1024
+
+
+def call(kernel, grid, ins, outs, scratch=()):
+    arrays, in_specs = zip(*ins)
+    shapes, out_specs = zip(*outs)
+    return pl.pallas_call(
+        kernel,
+        grid=grid,
+        in_specs=list(in_specs),
+        out_specs=list(out_specs),
+        out_shape=list(shapes),
+        scratch_shapes=list(scratch),
+        compiler_params=pltpu.CompilerParams(vmem_limit_bytes=VMEM),
+    )(*arrays)
+
+
+def shift(block, amount, ranks):
+    return lax.ppermute(block, "seq", [(k, (k + amount) % ranks) for k in range(ranks)])
+
+
+def swap(block, mask):
+    return lax.ppermute(block, "dp", [(k, k ^ mask) for k in range(8)])
+
+
+def gather_dp(piece):
+    half = piece.shape[0] // 2
+    place = lax.axis_index("dp")
+    by_x, by_y = swap(piece, 2), swap(piece, 4)
+    three = jnp.stack([piece, by_x, by_y])
+    other = swap(three, 1)
+    corner = jnp.concatenate([swap(by_x[:half], 4), swap(by_y[half:], 2)])
+    far = swap(corner, 1)
+    whole = jnp.zeros((8,) + piece.shape, piece.dtype)
+    for mask, part in (
+        (0, piece), (2, by_x), (4, by_y), (1, other[0]), (3, other[1]), (5, other[2]),
+        (6, corner), (7, far),
+    ):
+        whole = lax.dynamic_update_slice(whole, part[None], (place ^ mask, 0, 0))
+    return whole.reshape(8 * piece.shape[0], piece.shape[1])
+
+
+def per_device_heads(
+    hidden_in,
+    stretch_order,
+    doc_lengths,
+    attn_gain,
+    attn_shift,
+    feed_gain,
+    feed_shift,
+    qkv_weight,
+    qkv_bias,
+    out_weight,
+    out_bias,
+    up_weight,
+    up_bias,
+    down_weight,
+    down_bias,
+    grad_out,
+):
+    ranks, groups = lax.axis_size("seq"), lax.axis_size("dp")
+    rank = lax.axis_index("seq")
+    blocks_own, half, width = hidden_in.shape[1:]
+    own = blocks_own * half
+    count = ranks * own
+    share = qkv_weight.shape[0]
+    piece = share * ranks
+    cols = width // ranks
+    heads = cols // HD
+    hidden = up_weight.shape[1] // ranks
+    ratio = up_weight.shape[1] // width
+    mixed_cols = 3 * cols
+    edge = hidden + width + mixed_cols
+
+    small = jnp.concatenate(
+        [attn_gain[:, None], attn_shift[:, None], feed_gain[:, None], feed_shift[:, None],
+         out_bias[:, None], down_bias[:, None], qkv_bias.reshape(share, 3),
+         up_bias.reshape(share, ratio)], axis=1,
+    )
+    small = jnp.pad(small, ((0, 0), (0, 128 - small.shape[1])))
+    by_rank = jnp.concatenate(
+        [
+            up_weight.reshape(share, ranks, hidden),
+            jnp.transpose(qkv_weight.reshape(share, 3, ranks, cols), (0, 2, 1, 3)).reshape(
+                share, ranks, mixed_cols
+            ),
+            jnp.broadcast_to(small[:, None], (share, ranks, 128)),
+        ],
+        axis=2,
+    )
+    by_rank = jnp.transpose(by_rank, (1, 0, 2))
+    spread = ranks * groups
+    rows_piece = jnp.concatenate([down_weight, out_weight.reshape(piece, cols)], axis=1)
+    rows_piece = lax.ppermute(
+        rows_piece, ("dp", "seq"),
+        [(k, (k % groups) * ranks + k // groups) for k in range(spread)],
+    )
+    landed = jnp.zeros((ranks,) + by_rank.shape[1:], bf16)
+    for r in range(ranks):
+        sent = lax.dynamic_index_in_dim(by_rank, (rank + r) % ranks, 0)
+        got = shift(sent, r, ranks) if r else sent
+        landed = lax.dynamic_update_slice(landed, got, ((rank - r) % ranks, 0, 0))
+    landed = landed.reshape(piece, -1)
+    weights = gather_dp(
+        jnp.concatenate(
+            [
+                landed[:, :hidden],
+                rows_piece[:, :width],
+                landed[:, hidden : hidden + mixed_cols],
+                rows_piece[:, width:],
+                landed[:, hidden + mixed_cols :],
+            ],
+            axis=1,
+        )
+    )
+    vectors = weights[:, edge + cols : edge + cols + 6 + 3 + ratio].astype(f32)
+    up_bias_own = lax.dynamic_slice_in_dim(vectors[:, 9:].reshape(-1), rank * hidden, hidden)
+    qkv_bias_own = lax.dynamic_index_in_dim(
+        vectors[:, 6:9].reshape(3, ranks, cols), rank, 1, keepdims=False
+    ).reshape(1, mixed_cols)
+    vec = jnp.stack(
+        [vectors[:, 0], vectors[:, 1], vectors[:, 2], vectors[:, 3], up_bias_own]
+        + [jnp.zeros(width, f32)] * 3
+    )
+    out_own = weights[:, edge : edge + cols].reshape(cols, width)
+
+    x_own = hidden_in.reshape(own, width)
+    dy_own = grad_out.reshape(own, width)
+    x_all = jnp.concatenate([x_own] + [shift(x_own, r, ranks) for r in range(1, ranks)])
+    dy_all = jnp.concatenate([dy_own] + [shift(dy_own, r, ranks) for r in range(1, ranks)])
+
+    owners = (rank - jnp.arange(ranks, dtype=jnp.int32)) % ranks
+    blocks = stretch_order.reshape(ranks, blocks_own)[owners].reshape(-1)
+    place = (blocks[:, None] * half + jnp.arange(half, dtype=jnp.int32)[None]).reshape(count)
+    ends = jnp.cumsum(doc_lengths[0])[:-1]
+    first = jnp.max(jnp.where(place[:, None] >= ends[None], ends[None], 0), axis=1)
+    span = jnp.concatenate([place[None], first[None], jnp.zeros((6, count), jnp.int32)])
+    angle = frequencies()[:, None] * place.astype(f32)[None]
+    cosine, sine = jnp.cos(angle), jnp.sin(angle)
+
+    tile = lambda w: pl.BlockSpec((own, w), lambda t, *_: (t, 0))
+    upright_tile = lambda n: pl.BlockSpec((n, own), lambda t, *_: (0, t))
+    column = lambda j: pl.BlockSpec((width, width), lambda *_: (0, j))
+    shape = jax.ShapeDtypeStruct
+    angles = [(cosine, upright_tile(ROT // 2)), (sine, upright_tile(ROT // 2))]
+
+    n1, n2, active, slope, fed, upright, rows = call(
+        front_kernel,
+        (ranks,),
+        [(x_all, tile(width)), (vec, whole_block((8, width))),
+         (qkv_bias_own, whole_block((1, mixed_cols)))] + angles
+        + [(weights, column(0)), (weights, column(1)), (weights, column(2))],
+        [(shape((count, width), bf16), tile(width)), (shape((count, width), bf16), tile(width)),
+         (shape((count, hidden), bf16), tile(hidden)), (shape((count, hidden), bf16), tile(hidden)),
+         (shape((count, width), f32), tile(width)),
+         (shape((mixed_cols, count), bf16), upright_tile(mixed_cols)),
+         (shape((3 * heads, count, HD), bf16),
+          pl.BlockSpec((3 * heads, own, HD), lambda t: (0, t, 0)))],
+    )
+
+    all_heads = lambda j: pl.BlockSpec((heads, count, HD), lambda *_: (j, 0, 0))
+    soft_spec = pl.BlockSpec((1, count, own), lambda t, h: (h, 0, t))
+    inv_spec = pl.BlockSpec((1, 8, own), lambda t, h: (h, 0, t))
+    soft, inverse, heads_low, part_out = call(
+        attend_kernel,
+        (ranks, heads),
+        [(span, upright_tile(8)), (place[:, None], whole_block((count, 1))),
+         (rows, all_heads(1)), (upright, pl.BlockSpec((HD, own), lambda t, h: (h, t))),
+         (upright, pl.BlockSpec((HD, count), lambda t, h: (2 * heads + h, 0))),
+         (fed, tile(width)), (out_own, whole_block((cols, width)))],
+        [(shape((heads, count, count), bf16), soft_spec),
+         (shape((heads, 8, count), f32), inv_spec),
+         (shape((cols, count), bf16), upright_tile(cols)),
+         (shape((count, width), bf16), tile(width))],
+        [pltpu.VMEM((count, own), f32)],
+    )
+
+    def give_back(parts):
+        parts = parts.reshape(ranks, own, width)
+        total = parts[0].astype(f32)
+        for r in range(1, ranks):
+            total = total + shift(parts[r], -r, ranks).astype(f32)
+        return total
+
+    hidden_out = (
+        x_own.astype(f32) + (vectors[:, 4] + vectors[:, 5])[None] + give_back(part_out)
+    ).astype(bf16)
+
+    scaled, part_up, part_down, feed_sums = call(
+        feed_back_kernel,
+        (ranks,),
+        [(dy_all, tile(width)), (x_all, tile(width)), (active, tile(hidden)),
+         (slope, tile(hidden)), (n2, tile(width)), (vec, whole_block((8, width))),
+         (weights, column(0)), (weights, column(1))],
+        [(shape((count, width), f32), tile(width)),
+         (shape((width, hidden), bf16), whole_block((width, hidden))),
+         (shape((hidden, width), bf16), whole_block((hidden, width))),
+         (shape((8, width), f32), whole_block((8, width)))],
+        [pltpu.VMEM((width, hidden), f32), pltpu.VMEM((hidden, width), f32)],
+    )
+    feed_part = lax.psum_scatter(
+        jnp.concatenate([part_up, part_down], axis=1), "dp", scatter_dimension=0, tiled=True
+    )
+
+    gquery, gkey, gvalue, part_proj = call(
+        attend_back_kernel,
+        (ranks, heads),
+        [(dy_all, tile(width)), (out_own, whole_block((cols, width))),
+         (heads_low, upright_tile(cols)), (inverse, inv_spec), (soft, soft_spec),
+         (rows, all_heads(2)), (upright, pl.BlockSpec((HD, count), lambda t, h: (heads + h, 0))),
+         (rows, pl.BlockSpec((1, own, HD), lambda t, h: (h, t, 0)))] + angles,
+        [(shape((cols, count), f32), upright_tile(cols)),
+         (shape((heads, count, HD), f32), whole_block((heads, count, HD))),
+         (shape((heads, count, HD), f32), whole_block((heads, count, HD))),
+         (shape((cols, width), f32), whole_block((cols, width)))],
+        [pltpu.VMEM((cols, own), f32)],
+    )
+
+    head_tile = pl.BlockSpec((heads, own, HD), lambda t: (0, t, 0))
+    total, part_attn, attn_sums, attn_bias = call(
+        rear_kernel,
+        (ranks,),
+        [(gquery, upright_tile(cols)), (gkey, head_tile), (gvalue, head_tile)] + angles
+        + [(n1, tile(width)), (x_all, tile(width)), (scaled, tile(width)),
+           (vec, whole_block((8, width))), (weights, column(2))],
+        [(shape((count, width), bf16), tile(width)),
+         (shape((width, mixed_cols), bf16), whole_block((width, mixed_cols))),
+         (shape((8, width), f32), whole_block((8, width))),
+         (shape((8, mixed_cols), f32), whole_block((8, mixed_cols)))],
+        [pltpu.VMEM((width, mixed_cols), f32)],
+    )
+
+    dy = dy_own.astype(f32)
+    grad = give_back(total)
+    rows_own = x_own.astype(f32)
+    centred = rows_own - jnp.mean(rows_own, axis=-1, keepdims=True)
+    rstd = lax.rsqrt(jnp.mean(centred * centred, axis=-1, keepdims=True) + eps)
+    hat = centred * rstd
+    grad_in = dy + rstd * (
+        grad
+        - jnp.mean(grad, axis=-1, keepdims=True)
+        - hat * jnp.mean(grad * hat, axis=-1, keepdims=True)
+    )
+
+    qkv_bias_part = lax.dynamic_update_slice(
+        jnp.zeros((3, ranks, cols), f32), attn_bias[0].reshape(3, 1, cols), (0, rank, 0)
+    )
+    up_bias_part = lax.dynamic_update_slice(
+        jnp.zeros(ranks * hidden, f32), feed_sums[2], (rank * hidden,)
+    )
+    small_part = jnp.concatenate(
+        [
+            jnp.stack(
+                [attn_sums[0], attn_sums[1], feed_sums[0], feed_sums[1], jnp.sum(dy, axis=0)],
+                axis=1,
+            ),
+            qkv_bias_part.reshape(width, 3),
+            up_bias_part.reshape(width, ratio),
+        ],
+        axis=1,
+    ).astype(bf16)
+    attn_part = lax.psum_scatter(
+        jnp.concatenate(
+            [
+                part_attn,
+                part_proj.astype(bf16).reshape(width, cols),
+                jnp.pad(small_part, ((0, 0), (0, 128 - small_part.shape[1]))),
+            ],
+            axis=1,
+        ),
+        "dp",
+        scatter_dimension=0,
+        tiled=True,
+    )
+    factor = 1.0 / math.sqrt(count * groups)
+
+    def exchange(parts):
+        parts = parts.reshape(ranks, share, parts.shape[1])
+        return lax.all_to_all(parts, "seq", 0, 0, tiled=True).astype(f32)
+
+    def to_owner(parts):
+        home = [((k % groups) * ranks + k // groups, k) for k in range(spread)]
+        return lax.ppermute(parts, ("dp", "seq"), home).astype(f32) * factor
+
+    up_own = jnp.transpose(exchange(feed_part[:, :hidden]), (1, 0, 2)) * factor
+    down_own = to_owner(feed_part[:, hidden:])
+    rest = exchange(
+        jnp.concatenate([attn_part[:, :mixed_cols], attn_part[:, mixed_cols + cols :]], axis=1)
+    )
+    qkv_own = rest[:, :, :mixed_cols].reshape(ranks, share, 3, cols) * factor
+    small_own = jnp.sum(rest[:, :, mixed_cols:], axis=0) * factor
+    proj_own = to_owner(attn_part[:, mixed_cols : mixed_cols + cols]).reshape(share, width)
+    return (
+        hidden_out.reshape(hidden_in.shape),
+        grad_in.astype(bf16).reshape(hidden_in.shape),
+        small_own[:, 0],
+        small_own[:, 1],
+        small_own[:, 2],
+        small_own[:, 3],
+        jnp.transpose(qkv_own, (1, 2, 0, 3)).reshape(share, 3 * width),
+        small_own[:, 5:8].reshape(share * 3),
+        proj_own,
+        small_own[:, 4],
+        up_own.reshape(share, ranks * hidden),
+        small_own[:, 8 : 8 + ratio].reshape(share * ratio),
+        down_own,
+        small_own[:, 4],
+    )
+
+
+def per_device(hidden_in, *rest):
+    heads = hidden_in.shape[-1] // HD
+    fits = heads % lax.axis_size("seq") == 0 and lax.axis_size("dp") == 8
+    return (per_device_heads if fits else per_device_split)(hidden_in, *rest)
+
+
 def solution(mesh):
     in_specs = (
         P("dp", "seq", None, None),

time: 964 us -> 321 us (0.33)
  waiting for transfers between devices: 553 us -> 96.7 us
  matrix products: 111 us -> 0 us
  local copies, waits for them, and re-layouts: 149 us -> 38.5 us
  starting transfers between devices: 0.76 us -> 89.6 us
  Pallas kernels: 0 us -> 63 us
  other arithmetic: 67.9 us -> 16.6 us
  blocking collectives: 42.9 us -> 0 us
  loops' own time: 21.5 us -> 0 us
    unnamed x10 -> x2, waiting for transfers between devices: 428 us -> 0.03 us
    dot_general x54 -> x0, matrix products: 111 us -> none  [the longest x4 19.9 us: times_transposed(): lax.dot_general(left, right, (((1,), (1,)), ((), ())), preferred_element_...]
    all_gather x6 -> x0, waiting for transfers between devices: 107 us -> none  [the longest x1 40.3 us: per_device(): lax.all_gather(out_weight, ('dp', 'seq'), axis=0, tiled=True)]
    ppermute x0 -> x24, waiting for transfers between devices: none -> 85.3 us  [the longest x15 75.4 us: shift(): lax.ppermute(block, 'seq', [(k, (k + amount) % ranks) for k in range(rank...]
    ppermute x0 -> x24, starting transfers between devices: none -> 76.7 us  [the longest x15 67.1 us: shift(): lax.ppermute(block, 'seq', [(k, (k + amount) % ranks) for k in range(rank...]
    pallas_call x0 -> x5, Pallas kernels: none -> 63 us  [call(): pl.pallas_call(kernel, grid=grid, in_specs=list(in_specs), out_specs=list...]
    unnamed x1 -> x0, blocking collectives: 42.9 us -> none
    dynamic_slice x40 -> x2, local copies, waits for them, and re-layouts: 35.2 us -> 0.1 us  [the longest x1 0.08 us: per_device_heads(): lax.dynamic_slice_in_dim(vectors[:, 9:].reshape(-1), rank * hidden, hidden)]
  transfers between devices with their start and end apart: 9 -> 28, of which waited for: 6 -> 14; matrix products, arithmetic and copies ran while one was open for 25% -> 10% of each run, Pallas kernels for 0% -> 0%
where the time goes in v1:
time: 321 us; the launch traced here: 319 us
  waiting for transfers between devices  96.7 us (30%)
  starting transfers between devices  89.6 us (28%)
  Pallas kernels  63 us (20%)
  local copies, waits for them, and re-layouts  38.5 us (12%)
  other arithmetic  16.6 us (5%)
  between operations  14.8 us (5%)
    ppermute x15, waiting for transfers between devices, shift(): lax.ppermute(block, 'seq', [(k, (k + amount) % ranks) for k in range(rank...  75.4 us
    ppermute x15, starting transfers between devices, shift(): lax.ppermute(block, 'seq', [(k, (k + amount) % ranks) for k in range(rank...  67.1 us
    pallas_call x5, Pallas kernels, call(): pl.pallas_call(kernel, grid=grid, in_specs=list(in_specs), out_specs=list...  63 us
    all_to_all x2, starting transfers between devices, exchange(): return lax.all_to_all(parts, 'seq', 0, 0, tiled=True).astype(f32)  12.8 us
    all_to_all x2, waiting for transfers between devices, exchange(): return lax.all_to_all(parts, 'seq', 0, 0, tiled=True).astype(f32)  11.3 us
    ppermute x6, waiting for transfers between devices, swap(): return lax.ppermute(block, 'dp', [(k, k ^ mask) for k in range(8)])  9.87 us
    ppermute x6, starting transfers between devices, swap(): return lax.ppermute(block, 'dp', [(k, k ^ mask) for k in range(8)])  7.59 us
  transfers between devices with their start and end apart: 28, of which 14 were waited for; matrix products, arithmetic and copies ran while one was open for 10% of the time, Pallas kernels for 0%

profile of v1, /device:TPU:0, one launch (start us, length us, event | category | flops | bytes accessed | tf_op | source)
XLA Modules:
  0.0 319.2 jit_solution(2113793285021377014)
XLA Ops:
  7.3 3.1 collective-permute-start.10
  30.0 11.1 %collective-permute-done = bf16[1,24,1472]{2,1,0:T(8,128)(2,1)S(1)} collective-permute-done((bf16[1,24,1472]{2,1,0:T(8,128)(2,1)S(1)}, bf16[1,24,1472]{2,1,0:T(8,128)(2,1)S(1)}, u32[]{:S(2)}, u32[]{:S(2)}) %collective-permute-start) | collective-permute-done | bytes 70688 | tf_op jit(solution)/shard_map/ppermute | solution.py:506
  41.1 10.7 %collective-permute-done.1 = bf16[1,24,1472]{2,1,0:T(8,128)(2,1)S(1)} collective-permute-done((bf16[1,24,1472]{2,1,0:T(8,128)(2,1)S(1)}, bf16[1,24,1472]{2,1,0:T(8,128)(2,1)S(1)}, u32[]{:S(2)}, u32[]{:S(2)}) %collective-permute-start.1) | collective-permute-done | bytes 70688 | tf_op jit(solution)/shard_map/ppermute | solution.py:506
  56.3 19.0 %collective-permute-start.17 = (bf16[256,768]{1,0:T(8,128)(2,1)S(1)}, bf16[256,768]{1,0:T(8,128)(2,1)}, u32[]{:S(2)}, u32[]{:S(2)}) collective-permute-start(bf16[256,768]{1,0:T(8,128)(2,1)S(1)} %bitcast.87), channel_id=1, source_target_pairs={{0,2},{1,3},{2,0},{3,1},{4,6},{5,7},{6,4},{7,5},{8,10},{9,11},{10,... | collective-permute-start | bytes 1179656 | tf_op jit(solution)/shard_map/ppermute | solution.py:506
  75.4 8.5 %collective-permute-start.18 = (bf16[256,768]{1,0:T(8,128)(2,1)S(1)}, bf16[256,768]{1,0:T(8,128)(2,1)S(1)}, u32[]{:S(2)}, u32[]{:S(2)}) collective-permute-start(bf16[256,768]{1,0:T(8,128)(2,1)S(1)} %bitcast.88), channel_id=1, source_target_pairs={{0,3},{1,0},{2,1},{3,2},{4,7},{5,4},{6,5},{7,6},{8,11},{9,8},{10,9... | collective-permute-start | bytes 1179656 | tf_op jit(solution)/shard_map/ppermute | solution.py:506
  85.8 7.7 %collective-permute-done.18 = bf16[256,768]{1,0:T(8,128)(2,1)S(1)} collective-permute-done((bf16[256,768]{1,0:T(8,128)(2,1)S(1)}, bf16[256,768]{1,0:T(8,128)(2,1)S(1)}, u32[]{:S(2)}, u32[]{:S(2)}) %collective-permute-start.18) | collective-permute-done | bytes 393248 | tf_op jit(solution)/shard_map/ppermute | solution.py:506
  96.8 7.1 %collective-permute-start.6 = (bf16[3,96,2432]{2,1,0:T(8,128)(2,1)S(1)}, bf16[3,96,2432]{2,1,0:T(8,128)(2,1)S(1)}, u32[]{:S(2)}, u32[]{:S(2)}) collective-permute-start(bf16[3,96,2432]{2,1,0:T(8,128)(2,1)S(1)} %pad_maximum_fusion.3), channel_id=1, source_target_pairs={{0,4},{4,0},{8,12},{12,8},{16,20},{20,16},{24,28},{28,24},{1,5},{5... | collective-permute-start | bytes 4202504 | tf_op jit(solution)/shard_map/ppermute | solution.py:510
  104.3 7.4 %collective-permute-done.7 = bf16[48,2432]{1,0:T(8,128)(2,1)S(1)} collective-permute-done((bf16[48,2432]{1,0:T(8,128)(2,1)S(1)}, bf16[48,2432]{1,0:T(8,128)(2,1)S(1)}, u32[]{:S(2)}, u32[]{:S(2)}) %collective-permute-start.7) | collective-permute-done | bytes 233504 | tf_op jit(solution)/shard_map/ppermute | solution.py:510
  117.7 10.0 %shard_map.263 = (bf16[1024,768]{1,0:T(8,128)(2,1)}, bf16[1024,768]{1,0:T(8,128)(2,1)}, bf16[1024,768]{1,0:T(8,128)(2,1)}, bf16[1024,768]{1,0:T(8,128)(2,1)}, f3...) custom-call(bf16[1024,768]{1,0:T(8,128)(2,1)} %pad_maximum_fusion.1.x_ref, ...), custom_call_target="tpu_custom_call" | custom-call | tf_op jit(solution)/shard_map/pallas_call | solution.py:494
  127.8 11.3 %shard_map.266 = (f32[1024,768]{1,0:T(8,128)}, bf16[768,768]{1,0:T(8,128)(2,1)}, bf16[768,768]{1,0:T(8,128)(2,1)}, f32[8,768]{1,0:T(8,128)}) custom-call(bf16[1024,768]{1,0:T(8,128)(2,1)} %pad_maximum_fusion.2.dy_ref, bf16[1024,768]{1,0:T(8,128)(2,1)} %pad_maximum_fusion.1.x_ref, bf16[1024,768]{1,0:T(8,128)(2,1)} %get-tuple-element.48.act_ref, ...), custom_call_target="tpu_custom_call" | custom-call | tf_op jit(solution)/shard_map/pallas_call | solution.py:494
  141.7 15.8 %shard_map.264 = (bf16[3,1024,1024]{2,1,0:T(8,128)(2,1)}, f32[3,8,1024]{2,1,0:T(8,128)}, bf16[192,1024]{1,0:T(8,128)(2,1)}, bf16[1024,768]{1,0:T(8,128)(2,1)}) custom-call(s32[8,1024]{1,0:T(8,128)} %add_add_fusion.span_ref, s32[1024,1]{1,0:T(8,128)} %copy.95.place_ref, bf16[9,1024,64]{2,1,0:T(8,128)(2,1)} %get-tuple-element.37.key_ref.value_ref.query_ref, ...), custom_call_target="tpu_custom_call" | custom-call | tf_op jit(solution)/shard_map/pallas_call | solution.py:494
  157.5 16.2 %shard_map.265 = (f32[192,1024]{1,0:T(8,128)}, f32[3,1024,64]{2,1,0:T(8,128)}, f32[3,1024,64]{2,1,0:T(8,128)}, f32[192,768]{1,0:T(8,128)}) custom-call(bf16[1024,768]{1,0:T(8,128)(2,1)} %pad_maximum_fusion.2.dy_ref, bf16[192,768]{1,0:T(8,128)(2,1)} %reshape.332.out_ref, bf16[192,1024]{1,0:T(8,128)(2,1)} %get-tuple-element.41.heads_ref, ...), custom_call_target="tpu_custom_call" | custom-call | tf_op jit(solution)/shard_map/pallas_call | solution.py:494
  173.7 9.6 %shard_map.267 = (bf16[1024,768]{1,0:T(8,128)(2,1)}, bf16[768,576]{1,0:T(8,128)(2,1)}, f32[8,768]{1,0:T(8,128)}, f32[8,576]{1,0:T(8,128)}) custom-call(f32[192,1024]{1,0:T(8,128)} %get-tuple-element.44.gquery_ref, f32[3,1024,64]{2,1,0:T(8,128)} %get-tuple-element.45.gkey_ref, f32[3,1024,64]{2,1,0:T(8,128)} %get-tuple-element.46.gvalue_ref, ...), custom_call_target="tpu_custom_call" | custom-call | tf_op jit(solution)/shard_map/pallas_call | solution.py:494
  193.9 2.7 fusion.1
  199.8 5.3 %collective-permute-start.19 = (bf16[256,768]{1,0:T(8,128)(2,1)S(1)}, bf16[256,768]{1,0:T(8,128)(2,1)S(1)}, u32[]{:S(2)}, u32[]{:S(2)}) collective-permute-start(bf16[256,768]{1,0:T(8,128)(2,1)S(1)} %get-tuple-element.72), channel_id=1, source_target_pairs={{0,3},{1,0},{2,1},{3,2},{4,7},{5,4},{6,5},{7,6},{8,11},{9,8},{10,9... | collective-permute-start | bytes 1179656 | tf_op jit(solution)/shard_map/ppermute | solution.py:506
  206.0 3.9 %collective-permute-start.13 = (bf16[256,768]{1,0:T(8,128)(2,1)S(1)}, bf16[256,768]{1,0:T(8,128)(2,1)S(1)}, u32[]{:S(2)}, u32[]{:S(2)}) collective-permute-start(bf16[256,768]{1,0:T(8,128)(2,1)S(1)} %get-tuple-element.75), channel_id=1, source_target_pairs={{0,3},{1,0},{2,1},{3,2},{4,7},{5,4},{6,5},{7,6},{8,11},{9,8},{10,9... | collective-permute-start | bytes 1179656 | tf_op jit(solution)/shard_map/ppermute | solution.py:506
  210.1 4.5 %collective-permute-done.19 = bf16[256,768]{1,0:T(8,128)(2,1)S(1)} collective-permute-done((bf16[256,768]{1,0:T(8,128)(2,1)S(1)}, bf16[256,768]{1,0:T(8,128)(2,1)S(1)}, u32[]{:S(2)}, u32[]{:S(2)}) %collective-permute-start.19) | collective-permute-done | bytes 393248 | tf_op jit(solution)/shard_map/ppermute | solution.py:506
  214.6 18.7 %collective-permute-start.15 = (bf16[256,768]{1,0:T(8,128)(2,1)S(1)}, bf16[256,768]{1,0:T(8,128)(2,1)S(1)}, u32[]{:S(2)}, u32[]{:S(2)}) collective-permute-start(bf16[256,768]{1,0:T(8,128)(2,1)S(1)} %get-tuple-element.76), channel_id=1, source_target_pairs={{0,1},{1,2},{2,3},{3,0},{4,5},{5,6},{6,7},{7,4},{8,9},{9,10},{10,1... | collective-permute-start | bytes 1179656 | tf_op jit(solution)/shard_map/ppermute | solution.py:506
  233.3 24.7 %collective-permute-done.20 = bf16[256,768]{1,0:T(8,128)(2,1)S(1)} collective-permute-done((bf16[256,768]{1,0:T(8,128)(2,1)S(1)}, bf16[256,768]{1,0:T(8,128)(2,1)S(1)}, u32[]{:S(2)}, u32[]{:S(2)}) %collective-permute-start.20) | collective-permute-done | bytes 393248 | tf_op jit(solution)/shard_map/ppermute | solution.py:506
  258.5 15.6 %collective-permute-done.14 = bf16[256,768]{1,0:T(8,128)(2,1)S(1)} collective-permute-done((bf16[256,768]{1,0:T(8,128)(2,1)S(1)}, bf16[256,768]{1,0:T(8,128)(2,1)S(1)}, u32[]{:S(2)}, u32[]{:S(2)}) %collective-permute-start.14) | collective-permute-done | bytes 393248 | tf_op jit(solution)/shard_map/ppermute | solution.py:506
  279.6 7.2 %all-to-all-start = ((bf16[4,24,704]{2,1,0:T(8,128)(2,1)}), bf16[4,24,704]{2,1,0:T(8,128)(2,1)S(1)}, u32[]{:S(2)}, u32[]{:S(2)}) async-start(bf16[4,24,704]{2,1,0:T(8,128)(2,1)} %bitcast.31), calls=%async_computation.1 | async-start | bytes 294912 | tf_op jit(solution)/shard_map/all_to_all | solution.py:766
  287.5 5.2 %all-to-all-done = bf16[4,24,704]{2,1,0:T(8,128)(2,1)S(1)} async-done(((bf16[4,24,704]{2,1,0:T(8,128)(2,1)}), bf16[4,24,704]{2,1,0:T(8,128)(2,1)S(1)}, u32[]{:S(2)}, u32[]{:S(2)}) %all-to-all-start) | async-done | bytes 135200 | tf_op jit(solution)/shard_map/all_to_all | solution.py:766
  298.7 5.6 %all-to-all-start.1 = ((bf16[4,24,768]{2,1,0:T(8,128)(2,1)}), bf16[4,24,768]{2,1,0:T(8,128)(2,1)S(1)}, u32[]{:S(2)}, u32[]{:S(2)}) async-start(bf16[4,24,768]{2,1,0:T(8,128)(2,1)} %bitcast.33), calls=%async_computation.3 | async-start | bytes 294912 | tf_op jit(solution)/shard_map/all_to_all | solution.py:766
  305.0 6.1 %all-to-all-done.1 = bf16[4,24,768]{2,1,0:T(8,128)(2,1)S(1)} async-done(((bf16[4,24,768]{2,1,0:T(8,128)(2,1)}), bf16[4,24,768]{2,1,0:T(8,128)(2,1)S(1)}, u32[]{:S(2)}, u32[]{:S(2)}) %all-to-all-start.1) | async-done | bytes 147488 | tf_op jit(solution)/shard_map/all_to_all | solution.py:766
  (206 shorter events, 67.3 us)
Async XLA Ops:
  7.2 268.3 %reduce-scatter.3.cloned.1.call-start = ((), (), s32[]{:S(2)}) async-start(), calls=%async_computation.4 | async-start | bytes 1548288 | tf_op jit(solution)/shard_map/reduce_scatter | solution.py:749
  7.3 68.2 %collective-permute-start.10 = (bf16[256,768]{1,0:T(8,128)(2,1)}, bf16[256,768]{1,0:T(8,128)(2,1)S(1)}, u32[]{:S(2)}, u32[]{:S(2)}) collective-permute-start(bf16[256,768]{1,0:T(8,128)(2,1)} %bitcast.81), channel_id=1, source_target_pairs={{0,1},{1,2},{2,3},{3,0},{4,5},{5,6},{6,7},{7,4},{8,9},{9,10},{10,1... | collective-permute-start | bytes 1179656 | tf_op jit(solution)/shard_map/ppermute | solution.py:506
  10.3 73.6 %collective-permute-start.11 = (bf16[256,768]{1,0:T(8,128)(2,1)}, bf16[256,768]{1,0:T(8,128)(2,1)S(1)}, u32[]{:S(2)}, u32[]{:S(2)}) collective-permute-start(bf16[256,768]{1,0:T(8,128)(2,1)} %bitcast.82), channel_id=1, source_target_pairs={{0,2},{1,3},{2,0},{3,1},{4,6},{5,7},{6,4},{7,5},{8,10},{9,11},{10,... | collective-permute-start | bytes 1179656 | tf_op jit(solution)/shard_map/ppermute | solution.py:506
  12.9 71.1 %collective-permute-start.12 = (bf16[256,768]{1,0:T(8,128)(2,1)}, bf16[256,768]{1,0:T(8,128)(2,1)S(1)}, u32[]{:S(2)}, u32[]{:S(2)}) collective-permute-start(bf16[256,768]{1,0:T(8,128)(2,1)} %bitcast.83), channel_id=1, source_target_pairs={{0,3},{1,0},{2,1},{3,2},{4,7},{5,4},{6,5},{7,6},{8,11},{9,8},{10,9... | collective-permute-start | bytes 1179656 | tf_op jit(solution)/shard_map/ppermute | solution.py:506
  23.9 17.2 %collective-permute-start = (bf16[1,24,1472]{2,1,0:T(8,128)(2,1)S(1)}, bf16[1,24,1472]{2,1,0:T(8,128)(2,1)S(1)}, u32[]{:S(2)}, u32[]{:S(2)}) collective-permute-start(bf16[1,24,1472]{2,1,0:T(8,128)(2,1)S(1)} %bitcast.101), channel_id=1, source_target_pairs={{0,1},{1,2},{2,3},{3,0},{4,5},{5,6},{6,7},{7,4},{8,9},{9,10},{10,1... | collective-permute-start | bytes 211976 | tf_op jit(solution)/shard_map/ppermute | solution.py:506
  24.6 27.3 %collective-permute-start.1 = (bf16[1,24,1472]{2,1,0:T(8,128)(2,1)S(1)}, bf16[1,24,1472]{2,1,0:T(8,128)(2,1)S(1)}, u32[]{:S(2)}, u32[]{:S(2)}) collective-permute-start(bf16[1,24,1472]{2,1,0:T(8,128)(2,1)S(1)} %bitcast.100), channel_id=1, source_target_pairs={{0,2},{1,3},{2,0},{3,1},{4,6},{5,7},{6,4},{7,5},{8,10},{9,11},{10,... | collective-permute-start | bytes 211976 | tf_op jit(solution)/shard_map/ppermute | solution.py:506
  41.1 12.5 %collective-permute-start.2 = (bf16[1,24,1472]{2,1,0:T(8,128)(2,1)S(1)}, bf16[1,24,1472]{2,1,0:T(8,128)(2,1)S(1)}, u32[]{:S(2)}, u32[]{:S(2)}) collective-permute-start(bf16[1,24,1472]{2,1,0:T(8,128)(2,1)S(1)} %bitcast.102), channel_id=1, source_target_pairs={{0,3},{1,0},{2,1},{3,2},{4,7},{5,4},{6,5},{7,6},{8,11},{9,8},{10,9... | collective-permute-start | bytes 211976 | tf_op jit(solution)/shard_map/ppermute | solution.py:506
  53.6 32.2 %collective-permute-start.16 = (bf16[256,768]{1,0:T(8,128)(2,1)S(1)}, bf16[256,768]{1,0:T(8,128)(2,1)S(1)}, u32[]{:S(2)}, u32[]{:S(2)}) collective-permute-start(bf16[256,768]{1,0:T(8,128)(2,1)S(1)} %bitcast.86), channel_id=1, source_target_pairs={{0,1},{1,2},{2,3},{3,0},{4,5},{5,6},{6,7},{7,4},{8,9},{9,10},{10,1... | collective-permute-start | bytes 1179656 | tf_op jit(solution)/shard_map/ppermute | solution.py:506
  56.3 29.6 %collective-permute-start.17 = (bf16[256,768]{1,0:T(8,128)(2,1)S(1)}, bf16[256,768]{1,0:T(8,128)(2,1)}, u32[]{:S(2)}, u32[]{:S(2)}) collective-permute-start(bf16[256,768]{1,0:T(8,128)(2,1)S(1)} %bitcast.87), channel_id=1, source_target_pairs={{0,2},{1,3},{2,0},{3,1},{4,6},{5,7},{6,4},{7,5},{8,10},{9,11},{10,... | collective-permute-start | bytes 1179656 | tf_op jit(solution)/shard_map/ppermute | solution.py:506
  75.4 18.1 %collective-permute-start.18 = (bf16[256,768]{1,0:T(8,128)(2,1)S(1)}, bf16[256,768]{1,0:T(8,128)(2,1)S(1)}, u32[]{:S(2)}, u32[]{:S(2)}) collective-permute-start(bf16[256,768]{1,0:T(8,128)(2,1)S(1)} %bitcast.88), channel_id=1, source_target_pairs={{0,3},{1,0},{2,1},{3,2},{4,7},{5,4},{6,5},{7,6},{8,11},{9,8},{10,9... | collective-permute-start | bytes 1179656 | tf_op jit(solution)/shard_map/ppermute | solution.py:506
  84.0 12.6 %collective-permute-start.4 = (bf16[96,2432]{1,0:T(8,128)(2,1)S(1)}, bf16[96,2432]{1,0:T(8,128)(2,1)S(1)}, u32[]{:S(2)}, u32[]{:S(2)}) collective-permute-start(bf16[96,2432]{1,0:T(8,128)(2,1)S(1)} %concatenate.40), channel_id=1, source_target_pairs={{0,8},{4,12},{8,0},{12,4},{16,24},{20,28},{24,16},{28,20},{1,9},{5... | collective-permute-start | bytes 1400840 | tf_op jit(solution)/shard_map/ppermute | solution.py:510
  84.0 12.7 %collective-permute-start.5 = (bf16[96,2432]{1,0:T(8,128)(2,1)S(1)}, bf16[96,2432]{1,0:T(8,128)(2,1)S(1)}, u32[]{:S(2)}, u32[]{:S(2)}) collective-permute-start(bf16[96,2432]{1,0:T(8,128)(2,1)S(1)} %concatenate.40), channel_id=1, source_target_pairs={{0,16},{4,20},{8,24},{12,28},{16,0},{20,4},{24,8},{28,12},{1,17},{... | collective-permute-start | bytes 1400840 | tf_op jit(solution)/shard_map/ppermute | solution.py:510
  96.8 15.0 %collective-permute-start.6 = (bf16[3,96,2432]{2,1,0:T(8,128)(2,1)S(1)}, bf16[3,96,2432]{2,1,0:T(8,128)(2,1)S(1)}, u32[]{:S(2)}, u32[]{:S(2)}) collective-permute-start(bf16[3,96,2432]{2,1,0:T(8,128)(2,1)S(1)} %pad_maximum_fusion.3), channel_id=1, source_target_pairs={{0,4},{4,0},{8,12},{12,8},{16,20},{20,16},{24,28},{28,24},{1,5},{5... | collective-permute-start | bytes 4202504 | tf_op jit(solution)/shard_map/ppermute | solution.py:510
  196.6 96.3 %reduce-scatter.5.cloned.1.call-start = ((), (), s32[]{:S(2)}) async-start(), calls=%async_computation.5 | async-start | bytes 2654208 | tf_op jit(solution)/shard_map/reduce_scatter | solution.py:688
  199.8 14.9 %collective-permute-start.19 = (bf16[256,768]{1,0:T(8,128)(2,1)S(1)}, bf16[256,768]{1,0:T(8,128)(2,1)S(1)}, u32[]{:S(2)}, u32[]{:S(2)}) collective-permute-start(bf16[256,768]{1,0:T(8,128)(2,1)S(1)} %get-tuple-element.72), channel_id=1, source_target_pairs={{0,3},{1,0},{2,1},{3,2},{4,7},{5,4},{6,5},{7,6},{8,11},{9,8},{10,9... | collective-permute-start | bytes 1179656 | tf_op jit(solution)/shard_map/ppermute | solution.py:506
  205.0 53.0 %collective-permute-start.20 = (bf16[256,768]{1,0:T(8,128)(2,1)S(1)}, bf16[256,768]{1,0:T(8,128)(2,1)S(1)}, u32[]{:S(2)}, u32[]{:S(2)}) collective-permute-start(bf16[256,768]{1,0:T(8,128)(2,1)S(1)} %get-tuple-element.74), channel_id=1, source_target_pairs={{0,2},{1,3},{2,0},{3,1},{4,6},{5,7},{6,4},{7,5},{8,10},{9,11},{10,... | collective-permute-start | bytes 1179656 | tf_op jit(solution)/shard_map/ppermute | solution.py:506
  205.9 52.1 %collective-permute-start.21 = (bf16[256,768]{1,0:T(8,128)(2,1)S(1)}, bf16[256,768]{1,0:T(8,128)(2,1)S(1)}, u32[]{:S(2)}, u32[]{:S(2)}) collective-permute-start(bf16[256,768]{1,0:T(8,128)(2,1)S(1)} %get-tuple-element.73), channel_id=1, source_target_pairs={{0,1},{1,2},{2,3},{3,0},{4,5},{5,6},{6,7},{7,4},{8,9},{9,10},{10,1... | collective-permute-start | bytes 1179656 | tf_op jit(solution)/shard_map/ppermute | solution.py:506
  206.0 52.4 %collective-permute-start.13 = (bf16[256,768]{1,0:T(8,128)(2,1)S(1)}, bf16[256,768]{1,0:T(8,128)(2,1)S(1)}, u32[]{:S(2)}, u32[]{:S(2)}) collective-permute-start(bf16[256,768]{1,0:T(8,128)(2,1)S(1)} %get-tuple-element.75), channel_id=1, source_target_pairs={{0,3},{1,0},{2,1},{3,2},{4,7},{5,4},{6,5},{7,6},{8,11},{9,8},{10,9... | collective-permute-start | bytes 1179656 | tf_op jit(solution)/shard_map/ppermute | solution.py:506
  209.9 64.1 %collective-permute-start.14 = (bf16[256,768]{1,0:T(8,128)(2,1)S(1)}, bf16[256,768]{1,0:T(8,128)(2,1)S(1)}, u32[]{:S(2)}, u32[]{:S(2)}) collective-permute-start(bf16[256,768]{1,0:T(8,128)(2,1)S(1)} %get-tuple-element.77), channel_id=1, source_target_pairs={{0,2},{1,3},{2,0},{3,1},{4,6},{5,7},{6,4},{7,5},{8,10},{9,11},{10,... | collective-permute-start | bytes 1179656 | tf_op jit(solution)/shard_map/ppermute | solution.py:506
  214.6 59.4 %collective-permute-start.15 = (bf16[256,768]{1,0:T(8,128)(2,1)S(1)}, bf16[256,768]{1,0:T(8,128)(2,1)S(1)}, u32[]{:S(2)}, u32[]{:S(2)}) collective-permute-start(bf16[256,768]{1,0:T(8,128)(2,1)S(1)} %get-tuple-element.76), channel_id=1, source_target_pairs={{0,1},{1,2},{2,3},{3,0},{4,5},{5,6},{6,7},{7,4},{8,9},{9,10},{10,1... | collective-permute-start | bytes 1179656 | tf_op jit(solution)/shard_map/ppermute | solution.py:506
  276.5 10.3 %collective-permute-start.22 = (bf16[96,192]{1,0:T(8,128)(2,1)S(1)}, bf16[96,192]{1,0:T(8,128)(2,1)S(1)}, u32[]{:S(2)}, u32[]{:S(2)}) collective-permute-start(bf16[96,192]{1,0:T(8,128)(2,1)S(1)} %slice.245), channel_id=1, source_target_pairs={{0,0},{4,1},{8,2},{12,3},{16,4},{20,5},{24,6},{28,7},{1,8},{5,9},{... | collective-permute-start | bytes 110600 | tf_op jit(solution)/shard_map/ppermute | solution.py:770
  279.6 13.2 %all-to-all-start = ((bf16[4,24,704]{2,1,0:T(8,128)(2,1)}), bf16[4,24,704]{2,1,0:T(8,128)(2,1)S(1)}, u32[]{:S(2)}, u32[]{:S(2)}) async-start(bf16[4,24,704]{2,1,0:T(8,128)(2,1)} %bitcast.31), calls=%async_computation.1 | async-start | bytes 294912 | tf_op jit(solution)/shard_map/all_to_all | solution.py:766
  294.6 9.6 %collective-permute-start.23 = (bf16[96,768]{1,0:T(8,128)(2,1)S(1)}, bf16[96,768]{1,0:T(8,128)(2,1)S(1)}, u32[]{:S(2)}, u32[]{:S(2)}) collective-permute-start(bf16[96,768]{1,0:T(8,128)(2,1)S(1)} %get-tuple-element.80), channel_id=1, source_target_pairs={{0,0},{4,1},{8,2},{12,3},{16,4},{20,5},{24,6},{28,7},{1,8},{5,9},{... | collective-permute-start | bytes 442376 | tf_op jit(solution)/shard_map/ppermute | solution.py:770
  298.7 12.4 %all-to-all-start.1 = ((bf16[4,24,768]{2,1,0:T(8,128)(2,1)}), bf16[4,24,768]{2,1,0:T(8,128)(2,1)S(1)}, u32[]{:S(2)}, u32[]{:S(2)}) async-start(bf16[4,24,768]{2,1,0:T(8,128)(2,1)} %bitcast.33), calls=%async_computation.3 | async-start | bytes 294912 | tf_op jit(solution)/shard_map/all_to_all | solution.py:766
  (17 other events, 172.7 us)
Sparse Core Ops, SparseCore 0:
  196.7 39.7 reduce-scatter.2
  240.3 42.4 reduce-scatter.4

commit v2 on v1

--- a/solution.py
+++ b/solution.py
@@ -1,3 +1,4 @@
+import functools
 import math
 
 import jax
@@ -332,10 +333,114 @@
     )
 
 
+def places(owners, per, base, index):
+    lanes = lax.broadcasted_iota(jnp.int32, (LANES, index.shape[1]), 0)
+    rows = lax.broadcasted_iota(jnp.int32, (owners, index.shape[1]), 0)
+    return rows == index // per, (lanes == base + index % per).astype(bf16)
+
+
+def vector_maps(rank, share, ranks, cols, hidden, ratio):
+    line = lambda n: lax.broadcasted_iota(jnp.int32, (1, n), 1)
+    width = ranks * cols
+    part = line(3 * cols)
+    maps = [(share, j * share, line(width)) for j in range(6)]
+    maps.append((3 * share, 6 * share, part // cols * width + rank * cols + part % cols))
+    held = ratio * share
+    unit = line(hidden)
+    maps.append((held, 9 * share, (unit // held * ranks + rank) * held + unit % held))
+    return maps
+
+
+def pack_kernel(rank_ref, up_ref, qkv_ref, out_ref, *refs, vectors, held):
+    outs = refs[vectors:]
+    ranks = len(outs) - 1
+    rank = rank_ref[0]
+    up, qkv = up_ref[...], qkv_ref[...]
+    width = qkv.shape[1] // 3
+    cols = width // ranks
+    share = up.shape[0]
+    line = jnp.concatenate([ref[...][None].astype(f32) for ref in refs[:vectors]], axis=1)
+    line = jnp.pad(line, ((0, 0), (0, LANES - line.shape[1])))
+    lines = [line[:, j : j + 128] for j in range(0, LANES, 128)]
+    small = jnp.concatenate(lines + [jnp.zeros((share - len(lines), 128), f32)]).astype(bf16)
+    for t in range(ranks):
+        block = jnp.concatenate(
+            [up[:, at : at + held] for at in range(t * held, up.shape[1], ranks * held)]
+            + [qkv[:, j * width + t * cols : j * width + (t + 1) * cols] for j in range(3)]
+            + [small],
+            axis=1,
+        )
+        for r in range(ranks):
+
+            @pl.when((rank + r) % ranks == t)
+            def _():
+                outs[r][...] = block
+
+    out = out_ref[...].astype(f32)
+    flat = jnp.concatenate([out[:, j * cols : (j + 1) * cols] for j in range(ranks)], axis=0)
+    outs[-1][...] = flat.astype(bf16)
+
+
+def land_kernel(rank_ref, *refs, hidden):
+    ranks = len(refs) - 3
+    rank = rank_ref[0]
+    blocks = [ref[...].astype(f32) for ref in refs[:ranks]]
+    ordered = []
+    for t in range(ranks):
+        picked = blocks[0]
+        for r in range(1, ranks):
+            picked = jnp.where((rank - r + ranks) % ranks == t, blocks[r], picked)
+        ordered.append(picked)
+    landed = jnp.concatenate(ordered, axis=0).astype(bf16)
+    tail = landed.shape[1] - 128
+    refs[-1][...] = jnp.concatenate(
+        [landed[:, :hidden], refs[ranks][...], landed[:, hidden:tail], refs[ranks + 1][...],
+         landed[:, tail:]], axis=1,
+    )
+
+
+def store_at(refs, step, block):
+    for at, ref in enumerate(refs):
+
+        @pl.when(step == at)
+        def _():
+            ref[...] = block
+
+
 def front_kernel(
-    x_ref, vec_ref, bias_ref, cos_ref, sin_ref, up_ref, down_ref, attn_ref,
-    n1_ref, n2_ref, act_ref, slope_ref, fed_ref, upright_ref, rows_ref,
+    rank_ref, x_ref, small_ref, cos_ref, sin_ref, up_ref, down_ref, attn_ref,
+    n1_ref, n2_ref, act_ref, slope_ref, fed_ref, upright_ref, rows_ref, vec_ref, own_out_ref, bias_ref,
+    *, ranks, ratio,
 ):
+    width, part3 = n1_ref.shape[1], upright_ref.shape[0]
+    cols, hidden = part3 // 3, act_ref.shape[1]
+    owners = ranks * 8
+    share = width // owners
+
+    @pl.when(pl.program_id(0) == 0)
+    def _():
+        table = small_ref[...].astype(f32).reshape(owners, share, 128)
+        table = jnp.concatenate([table[:, j, :] for j in range(LANES // 128)], axis=1).astype(bf16)
+        vectors = []
+        for per, base, index in vector_maps(rank_ref[0], share, ranks, cols, hidden, ratio):
+            rows, lanes = places(owners, per, base, index)
+            spread = jnp.where(rows, product(table, lanes), 0.0)
+            vectors.append(jnp.sum(spread, axis=0, keepdims=True))
+        bias_ref[...] = vectors[6]
+        vec_ref[...] = jnp.concatenate(
+            vectors[:4] + [vectors[7], vectors[4] + vectors[5], jnp.zeros((2, width), f32)], axis=0
+        )
+        flat = attn_ref[:, part3:].astype(f32)
+        rebuilt = []
+        for d in range(8):
+            start = d * share * ranks
+            rebuilt.append(
+                jnp.concatenate(
+                    [flat[start + j * share : start + (j + 1) * share] for j in range(ranks)], axis=1
+                )
+            )
+        own_out_ref[...] = jnp.concatenate(rebuilt, axis=0).astype(bf16)
+
     hat = normalise(x_ref[...].astype(f32))
     vec = vec_ref[...]
     n1 = (hat * vec[0:1] + vec[1:2]).astype(bf16)
@@ -368,8 +473,9 @@
 
 def attend_kernel(
     span_ref, place_ref, key_ref, query_ref, value_ref, fed_ref, out_ref,
-    soft_ref, inv_ref, heads_ref, sum_ref, bias_ref,
+    soft_ref, inv_ref, heads_ref, *refs,
 ):
+    *sum_refs, bias_ref = refs
     head = pl.program_id(1)
 
     @pl.when(head == 0)
@@ -389,12 +495,14 @@
 
     @pl.when(head == pl.num_programs(1) - 1)
     def _():
-        sum_ref[...] = (fed_ref[...] + product(heads_ref[...], out_ref[...], 0, 0)).astype(bf16)
+        part = (fed_ref[...] + product(heads_ref[...], out_ref[...], 0, 0)).astype(bf16)
+        store_at(sum_refs, pl.program_id(0), part)
 
 
 def feed_back_kernel(
-    dy_ref, x_ref, act_ref, slope_ref, n2_ref, vec_ref, up_ref, down_ref,
-    scaled_ref, gup_ref, gdown_ref, sums_ref, acc_up, acc_down,
+    dy_ref, x_ref, act_ref, slope_ref, n2_ref, vec_ref, up_ref, down_ref, heads_ref,
+    scaled_ref, grads_ref, sums_ref, acc_up, acc_down, acc_out,
+    *, ranks,
 ):
     step = pl.program_id(0)
 
@@ -402,7 +510,9 @@
     def _():
         acc_up[...] = jnp.zeros_like(acc_up)
         acc_down[...] = jnp.zeros_like(acc_down)
+        acc_out[...] = jnp.zeros_like(acc_out)
         sums_ref[...] = jnp.zeros_like(sums_ref)
+        sums_ref[3:4] = jnp.sum(dy_ref[...].astype(f32), axis=0, keepdims=True)
 
     dy = dy_ref[...]
     grad_inner = product(dy, down_ref[...], 1, 1) * slope_ref[...].astype(f32)
@@ -415,16 +525,26 @@
     sums_ref[2:3] += jnp.sum(grad_inner, axis=0, keepdims=True)
     acc_up[...] += product(n2_ref[...], low, 0, 0)
     acc_down[...] += product(act_ref[...], dy, 0, 0)
+    acc_out[...] += product(heads_ref[...], dy)
 
     @pl.when(step == pl.num_programs(0) - 1)
     def _():
-        gup_ref[...] = acc_up[...].astype(bf16)
-        gdown_ref[...] = acc_down[...].astype(bf16)
+        cols = acc_out.shape[0]
+        share = cols // 8
+        flat = []
+        for d in range(8):
+            rows = acc_out[d * share : (d + 1) * share]
+            flat += [rows[:, j * cols : (j + 1) * cols] for j in range(ranks)]
+        flat = jnp.concatenate(flat, axis=0)
+        edge = acc_up.shape[1]
+        grads_ref[:, :edge] = acc_up[...].astype(bf16)
+        grads_ref[:, edge : edge + acc_down.shape[1]] = acc_down[...].astype(bf16)
+        grads_ref[:, edge + acc_down.shape[1] :] = flat.astype(bf16)
 
 
 def attend_back_kernel(
     dy_ref, out_ref, heads_ref, inv_ref, soft_ref, value_ref, key_ref, query_ref, cos_ref, sin_ref,
-    gquery_ref, gkey_ref, gvalue_ref, gout_ref, held_ref,
+    gquery_ref, gkey_ref, gvalue_ref, held_ref,
 ):
     step, head = pl.program_id(0), pl.program_id(1)
 
@@ -432,13 +552,10 @@
     def _():
         gkey_ref[...] = jnp.zeros_like(gkey_ref)
         gvalue_ref[...] = jnp.zeros_like(gvalue_ref)
-        gout_ref[...] = jnp.zeros_like(gout_ref)
 
     @pl.when(head == 0)
     def _():
-        dy = dy_ref[...]
-        held_ref[...] = product(out_ref[...], dy, 1, 1).astype(bf16).astype(f32)
-        gout_ref[...] += product(heads_ref[...], dy)
+        held_ref[...] = product(out_ref[...], dy_ref[...], 1, 1).astype(bf16).astype(f32)
 
     spot = pl.ds(pl.multiple_of(head * HD, HD), HD)
     lifted = held_ref[spot, :] * inv_ref[0, 0:1]
@@ -454,9 +571,11 @@
 
 
 def rear_kernel(
-    gquery_ref, gkey_ref, gvalue_ref, cos_ref, sin_ref, n1_ref, x_ref, scaled_ref, vec_ref, attn_ref,
-    total_ref, gattn_ref, sums_ref, gbias_ref, acc_ref,
+    spot_ref, gquery_ref, gkey_ref, gvalue_ref, cos_ref, sin_ref, n1_ref, x_ref, scaled_ref, vec_ref,
+    attn_ref, feed_ref, *refs, ranks, ratio,
 ):
+    total_refs, grads_ref = refs[:ranks], refs[ranks]
+    acc_ref, sums_ref, gbias_ref, small_ref = refs[-4:]
     step = pl.program_id(0)
 
     @pl.when(step == 0)
@@ -475,45 +594,113 @@
     low = mixed.astype(bf16)
     grad = product(low, attn_ref[:, : low.shape[1]], 1, 1)
     hat = normalise(x_ref[...].astype(f32))
-    total_ref[...] = (grad * vec_ref[0:1] + scaled_ref[...]).astype(bf16)
+    store_at(total_refs, step, (grad * vec_ref[0:1] + scaled_ref[...]).astype(bf16))
     sums_ref[0:1] += jnp.sum(grad * hat, axis=0, keepdims=True)
     sums_ref[1:2] += jnp.sum(grad, axis=0, keepdims=True)
     acc_ref[...] += product(n1_ref[...], low, 0, 0)
 
     @pl.when(step == pl.num_programs(0) - 1)
     def _():
-        gattn_ref[...] = acc_ref[...].astype(bf16)
-
-
+        width, part3 = acc_ref.shape
+        cols, owners = part3 // 3, small_ref.shape[0]
+        share = width // owners
+        feed = feed_ref[...]
+        vectors = [sums_ref[0:1], sums_ref[1:2], feed[0:1], feed[1:2], feed[3:4], None]
+        vectors += [gbias_ref[0:1], feed[2:3]]
+        maps = vector_maps(spot_ref[0], share, ranks, cols, feed.shape[1], ratio)
+        table = jnp.zeros((owners, LANES), f32)
+        for vector, (per, base, index) in zip(vectors, maps):
+            if vector is not None:
+                rows, lanes = places(owners, per, base, index)
+                table += product(jnp.where(rows, vector, 0.0).astype(bf16), lanes, 1, 1)
+        small_ref[...] = jnp.zeros_like(small_ref)
+        for j in range(LANES // 128):
+            small_ref[:, j, :] = table[:, j * 128 : (j + 1) * 128]
+        small = small_ref[...].reshape(width, 128)
+        grads_ref[...] = jnp.concatenate([acc_ref[...], small], axis=1).astype(bf16)
+
+
+def finish_kernel(
+    rank_ref, *refs, factor, hidden,
+):
+    qkv_ref, up_ref, proj_ref, down_ref, *small_refs = refs[-11:]
+    down_in, proj_in, refs = refs[-13], refs[-12], refs[:-13]
+    ranks, rank = len(refs), rank_ref[0]
+    blocks = [ref[...].astype(f32) * factor for ref in refs]
+    share, width = proj_ref.shape
+    cols = width // ranks
+    small = jnp.zeros((share, 128), f32)
+    for t in range(ranks):
+        picked = blocks[0]
+        for r in range(1, ranks):
+            picked = jnp.where((rank - r + ranks) % ranks == t, blocks[r], picked)
+        for at in range(0, hidden, down_ref.shape[0]):
+            where = at * ranks + t * down_ref.shape[0]
+            up_ref[:, where : where + down_ref.shape[0]] = picked[:, at : at + down_ref.shape[0]]
+        for j in range(3):
+            at = j * width + t * cols
+            qkv_ref[:, at : at + cols] = picked[:, hidden + j * cols : hidden + (j + 1) * cols]
+        small += picked[:, hidden + 3 * cols :]
+    down_ref[...] = down_in[...].astype(f32) * factor
+    rows = proj_in[...].astype(f32) * factor
+    proj_ref[...] = jnp.concatenate(
+        [rows[j * share : (j + 1) * share] for j in range(ranks)], axis=1
+    )
+    line = jnp.concatenate([small[j : j + 1] for j in range(LANES // 128)], axis=1)
+    at = 0
+    for j, ref in enumerate(small_refs):
+        if j == 5:
+            at += share
+        ref[...] = line[0, at : at + ref.shape[0]]
+        at += ref.shape[0]
+
+
+LANES = 384
 VMEM = 56 * 1024 * 1024
 
 
-def call(kernel, grid, ins, outs, scratch=()):
+SMEM = pl.BlockSpec(memory_space=pltpu.SMEM)
+
+
+def call(kernel, grid, ins, outs, scratch=(), cost=1, first=()):
     arrays, in_specs = zip(*ins)
     shapes, out_specs = zip(*outs)
     return pl.pallas_call(
         kernel,
-        grid=grid,
-        in_specs=list(in_specs),
-        out_specs=list(out_specs),
+        grid_spec=pltpu.PrefetchScalarGridSpec(
+            num_scalar_prefetch=len(first),
+            grid=grid,
+            in_specs=list(in_specs),
+            out_specs=list(out_specs),
+            scratch_shapes=list(scratch),
+        ),
         out_shape=list(shapes),
-        scratch_shapes=list(scratch),
         compiler_params=pltpu.CompilerParams(vmem_limit_bytes=VMEM),
-    )(*arrays)
+        cost_estimate=pl.CostEstimate(flops=cost * 10**9, bytes_accessed=0, transcendentals=0),
+    )(*first, *arrays)
+
+
+def after(value, *others):
+    return lax.optimization_barrier((value,) + others)[0]
 
 
 def shift(block, amount, ranks):
     return lax.ppermute(block, "seq", [(k, (k + amount) % ranks) for k in range(ranks)])
 
 
+def around(blocks, sign, ranks):
+    order = sorted(range(1, ranks), key=lambda r: abs(ranks - 2 * r))
+    got = {r: shift(blocks[r - 1], sign * r, ranks) for r in order}
+    return [got[r] for r in range(1, ranks)]
+
+
 def swap(block, mask):
     return lax.ppermute(block, "dp", [(k, k ^ mask) for k in range(8)])
 
 
-def gather_dp(piece):
+def gather_dp(piece, by_x, by_y):
     half = piece.shape[0] // 2
     place = lax.axis_index("dp")
-    by_x, by_y = swap(piece, 2), swap(piece, 4)
     three = jnp.stack([piece, by_x, by_y])
     other = swap(three, 1)
     corner = jnp.concatenate([swap(by_x[:half], 4), swap(by_y[half:], 2)])
@@ -525,6 +712,11 @@
     ):
         whole = lax.dynamic_update_slice(whole, part[None], (place ^ mask, 0, 0))
     return whole.reshape(8 * piece.shape[0], piece.shape[1])
+
+
+def scatter_dp(parts):
+    parts = lax.all_to_all(parts.reshape(8, -1, parts.shape[1]), "dp", 0, 0, tiled=True)
+    return jnp.sum(parts.astype(f32), axis=0).astype(bf16)
 
 
 def per_device_heads(
@@ -559,62 +751,42 @@
     mixed_cols = 3 * cols
     edge = hidden + width + mixed_cols
 
-    small = jnp.concatenate(
-        [attn_gain[:, None], attn_shift[:, None], feed_gain[:, None], feed_shift[:, None],
-         out_bias[:, None], down_bias[:, None], qkv_bias.reshape(share, 3),
-         up_bias.reshape(share, ratio)], axis=1,
-    )
-    small = jnp.pad(small, ((0, 0), (0, 128 - small.shape[1])))
-    by_rank = jnp.concatenate(
-        [
-            up_weight.reshape(share, ranks, hidden),
-            jnp.transpose(qkv_weight.reshape(share, 3, ranks, cols), (0, 2, 1, 3)).reshape(
-                share, ranks, mixed_cols
-            ),
-            jnp.broadcast_to(small[:, None], (share, ranks, 128)),
-        ],
-        axis=2,
-    )
-    by_rank = jnp.transpose(by_rank, (1, 0, 2))
+    small = [attn_gain, attn_shift, feed_gain, feed_shift, out_bias, down_bias, qkv_bias, up_bias]
+    shape = jax.ShapeDtypeStruct
+    spot = jnp.stack([rank, lax.axis_index("dp")])
+    sent = (share, hidden + mixed_cols + 128)
+    *packed, out_piece = call(
+        functools.partial(pack_kernel, vectors=len(small), held=ratio * share),
+        (1,),
+        [(spot, SMEM)]
+        + [(a, whole_block(a.shape)) for a in (up_weight, qkv_weight, out_weight, *small)],
+        [(shape(sent, bf16), whole_block(sent))] * ranks
+        + [(shape((piece, cols), bf16), whole_block((piece, cols)))],
+    )
     spread = ranks * groups
-    rows_piece = jnp.concatenate([down_weight, out_weight.reshape(piece, cols)], axis=1)
-    rows_piece = lax.ppermute(
-        rows_piece, ("dp", "seq"),
+    out_piece = lax.ppermute(
+        out_piece, ("dp", "seq"),
         [(k, (k % groups) * ranks + k // groups) for k in range(spread)],
     )
-    landed = jnp.zeros((ranks,) + by_rank.shape[1:], bf16)
-    for r in range(ranks):
-        sent = lax.dynamic_index_in_dim(by_rank, (rank + r) % ranks, 0)
-        got = shift(sent, r, ranks) if r else sent
-        landed = lax.dynamic_update_slice(landed, got, ((rank - r) % ranks, 0, 0))
-    landed = landed.reshape(piece, -1)
-    weights = gather_dp(
-        jnp.concatenate(
-            [
-                landed[:, :hidden],
-                rows_piece[:, :width],
-                landed[:, hidden : hidden + mixed_cols],
-                rows_piece[:, width:],
-                landed[:, hidden + mixed_cols :],
-            ],
-            axis=1,
-        )
-    )
-    vectors = weights[:, edge + cols : edge + cols + 6 + 3 + ratio].astype(f32)
-    up_bias_own = lax.dynamic_slice_in_dim(vectors[:, 9:].reshape(-1), rank * hidden, hidden)
-    qkv_bias_own = lax.dynamic_index_in_dim(
-        vectors[:, 6:9].reshape(3, ranks, cols), rank, 1, keepdims=False
-    ).reshape(1, mixed_cols)
-    vec = jnp.stack(
-        [vectors[:, 0], vectors[:, 1], vectors[:, 2], vectors[:, 3], up_bias_own]
-        + [jnp.zeros(width, f32)] * 3
-    )
-    out_own = weights[:, edge : edge + cols].reshape(cols, width)
+    landed = packed[:1] + around(packed[1:], 1, ranks)
+    total_cols = edge + cols + 128
+    (weight_piece,) = call(
+        functools.partial(land_kernel, hidden=hidden),
+        (1,),
+        [(spot, SMEM)] + [(a, whole_block(a.shape)) for a in (*landed, down_weight, out_piece)],
+        [(shape((piece, total_cols), bf16), whole_block((piece, total_cols)))],
+    )
+    by_x, by_y = swap(weight_piece, 2), swap(weight_piece, 4)
+    weights = gather_dp(weight_piece, by_x, by_y)
 
     x_own = hidden_in.reshape(own, width)
     dy_own = grad_out.reshape(own, width)
-    x_all = jnp.concatenate([x_own] + [shift(x_own, r, ranks) for r in range(1, ranks)])
-    dy_all = jnp.concatenate([dy_own] + [shift(dy_own, r, ranks) for r in range(1, ranks)])
+    x_go = after(x_own, *landed)
+    x_near = after(x_own, by_x, by_y)
+    x_sent = [x_go] * (ranks - 2) + [x_near]
+    x_all = jnp.concatenate([x_own] + around(x_sent, 1, ranks))
+    dy_go = after(dy_own, x_all, weights)
+    dy_all = jnp.concatenate([dy_own] + around([dy_go] * (ranks - 1), 1, ranks))
 
     owners = (rank - jnp.arange(ranks, dtype=jnp.int32)) % ranks
     blocks = stretch_order.reshape(ranks, blocks_own)[owners].reshape(-1)
@@ -628,68 +800,67 @@
     tile = lambda w: pl.BlockSpec((own, w), lambda t, *_: (t, 0))
     upright_tile = lambda n: pl.BlockSpec((n, own), lambda t, *_: (0, t))
     column = lambda j: pl.BlockSpec((width, width), lambda *_: (0, j))
-    shape = jax.ShapeDtypeStruct
     angles = [(cosine, upright_tile(ROT // 2)), (sine, upright_tile(ROT // 2))]
 
-    n1, n2, active, slope, fed, upright, rows = call(
-        front_kernel,
+    n1, n2, active, slope, fed, upright, rows, vec, out_own = call(
+        functools.partial(front_kernel, ranks=ranks, ratio=ratio),
         (ranks,),
-        [(x_all, tile(width)), (vec, whole_block((8, width))),
-         (qkv_bias_own, whole_block((1, mixed_cols)))] + angles
+        [(spot, SMEM), (x_all, tile(width)),
+         (weights, pl.BlockSpec((width, 128), lambda t: (0, (edge + cols) // 128)))] + angles
         + [(weights, column(0)), (weights, column(1)), (weights, column(2))],
         [(shape((count, width), bf16), tile(width)), (shape((count, width), bf16), tile(width)),
          (shape((count, hidden), bf16), tile(hidden)), (shape((count, hidden), bf16), tile(hidden)),
          (shape((count, width), f32), tile(width)),
          (shape((mixed_cols, count), bf16), upright_tile(mixed_cols)),
          (shape((3 * heads, count, HD), bf16),
-          pl.BlockSpec((3 * heads, own, HD), lambda t: (0, t, 0)))],
+          pl.BlockSpec((3 * heads, own, HD), lambda t: (0, t, 0))),
+         (shape((8, width), f32), whole_block((8, width))),
+         (shape((cols, width), bf16), whole_block((cols, width)))],
+        [pltpu.VMEM((1, mixed_cols), f32)],
+        cost=10,
     )
 
     all_heads = lambda j: pl.BlockSpec((heads, count, HD), lambda *_: (j, 0, 0))
-    soft_spec = pl.BlockSpec((1, count, own), lambda t, h: (h, 0, t))
-    inv_spec = pl.BlockSpec((1, 8, own), lambda t, h: (h, 0, t))
-    soft, inverse, heads_low, part_out = call(
+    soft_spec = pl.BlockSpec((1, count, own), lambda t, h, *_: (h, 0, t))
+    inv_spec = pl.BlockSpec((1, 8, own), lambda t, h, *_: (h, 0, t))
+    soft, inverse, heads_low, *part_out = call(
         attend_kernel,
         (ranks, heads),
         [(span, upright_tile(8)), (place[:, None], whole_block((count, 1))),
-         (rows, all_heads(1)), (upright, pl.BlockSpec((HD, own), lambda t, h: (h, t))),
-         (upright, pl.BlockSpec((HD, count), lambda t, h: (2 * heads + h, 0))),
+         (rows, all_heads(1)), (upright, pl.BlockSpec((HD, own), lambda t, h, *_: (h, t))),
+         (upright, pl.BlockSpec((HD, count), lambda t, h, *_: (2 * heads + h, 0))),
          (fed, tile(width)), (out_own, whole_block((cols, width)))],
         [(shape((heads, count, count), bf16), soft_spec),
          (shape((heads, 8, count), f32), inv_spec),
-         (shape((cols, count), bf16), upright_tile(cols)),
-         (shape((count, width), bf16), tile(width))],
+         (shape((cols, count), bf16), upright_tile(cols))]
+        + [(shape((own, width), bf16), whole_block((own, width)))] * ranks,
         [pltpu.VMEM((count, own), f32)],
-    )
-
-    def give_back(parts):
-        parts = parts.reshape(ranks, own, width)
-        total = parts[0].astype(f32)
-        for r in range(1, ranks):
-            total = total + shift(parts[r], -r, ranks).astype(f32)
-        return total
-
-    hidden_out = (
-        x_own.astype(f32) + (vectors[:, 4] + vectors[:, 5])[None] + give_back(part_out)
-    ).astype(bf16)
-
-    scaled, part_up, part_down, feed_sums = call(
-        feed_back_kernel,
+        cost=16,
+    )
+
+    dy_all = after(dy_all, heads_low)
+    scaled, grads_feed, feed_sums = call(
+        functools.partial(feed_back_kernel, ranks=ranks),
         (ranks,),
         [(dy_all, tile(width)), (x_all, tile(width)), (active, tile(hidden)),
          (slope, tile(hidden)), (n2, tile(width)), (vec, whole_block((8, width))),
-         (weights, column(0)), (weights, column(1))],
+         (weights, column(0)), (weights, column(1)), (heads_low, upright_tile(cols))],
         [(shape((count, width), f32), tile(width)),
-         (shape((width, hidden), bf16), whole_block((width, hidden))),
-         (shape((hidden, width), bf16), whole_block((hidden, width))),
+         (shape((width, edge - mixed_cols + cols), bf16),
+          whole_block((width, edge - mixed_cols + cols))),
          (shape((8, width), f32), whole_block((8, width)))],
-        [pltpu.VMEM((width, hidden), f32), pltpu.VMEM((hidden, width), f32)],
-    )
-    feed_part = lax.psum_scatter(
-        jnp.concatenate([part_up, part_down], axis=1), "dp", scatter_dimension=0, tiled=True
-    )
-
-    gquery, gkey, gvalue, part_proj = call(
+        [pltpu.VMEM((width, hidden), f32), pltpu.VMEM((hidden, width), f32),
+         pltpu.VMEM((cols, width), f32)],
+        cost=12,
+    )
+    feed_part = scatter_dp(grads_feed)
+
+    far = [r for r in range(1, ranks) if 2 * r == ranks]
+    near = [r for r in range(1, ranks) if r not in far]
+    out_parts = part_out[:1] + [shift(part_out[r], -r, ranks) for r in near]
+    heads_low = after(heads_low, scaled, *out_parts)
+    far_parts = [shift(after(part_out[r], scaled), -r, ranks) for r in far]
+    gquery, gkey, gvalue = call(
         attend_back_kernel,
         (ranks, heads),
         [(dy_all, tile(width)), (out_own, whole_block((cols, width))),
@@ -698,27 +869,38 @@
          (rows, pl.BlockSpec((1, own, HD), lambda t, h: (h, t, 0)))] + angles,
         [(shape((cols, count), f32), upright_tile(cols)),
          (shape((heads, count, HD), f32), whole_block((heads, count, HD))),
-         (shape((heads, count, HD), f32), whole_block((heads, count, HD))),
-         (shape((cols, width), f32), whole_block((cols, width)))],
+         (shape((heads, count, HD), f32), whole_block((heads, count, HD)))],
         [pltpu.VMEM((cols, own), f32)],
-    )
+        cost=16,
+    )
+    gquery = after(gquery, *far_parts)
+    out_sum = sum(part.astype(f32) for part in out_parts + far_parts)
+    hidden_out = (x_own.astype(f32) + vec[5:6] + out_sum).astype(bf16)
 
     head_tile = pl.BlockSpec((heads, own, HD), lambda t: (0, t, 0))
-    total, part_attn, attn_sums, attn_bias = call(
-        rear_kernel,
+    *total, grads_attn = call(
+        functools.partial(rear_kernel, ranks=ranks, ratio=ratio),
         (ranks,),
-        [(gquery, upright_tile(cols)), (gkey, head_tile), (gvalue, head_tile)] + angles
+        [(spot, SMEM), (gquery, upright_tile(cols)), (gkey, head_tile), (gvalue, head_tile)]
+        + angles
         + [(n1, tile(width)), (x_all, tile(width)), (scaled, tile(width)),
-           (vec, whole_block((8, width))), (weights, column(2))],
-        [(shape((count, width), bf16), tile(width)),
-         (shape((width, mixed_cols), bf16), whole_block((width, mixed_cols))),
-         (shape((8, width), f32), whole_block((8, width))),
-         (shape((8, mixed_cols), f32), whole_block((8, mixed_cols)))],
-        [pltpu.VMEM((width, mixed_cols), f32)],
+           (vec, whole_block((8, width))), (weights, column(2)),
+           (feed_sums, whole_block((8, width)))],
+        [(shape((own, width), bf16), whole_block((own, width)))] * ranks
+        + [(shape((width, mixed_cols + 128), bf16), whole_block((width, mixed_cols + 128)))],
+        [pltpu.VMEM((width, mixed_cols), f32), pltpu.VMEM((8, width), f32),
+         pltpu.VMEM((8, mixed_cols), f32), pltpu.VMEM((spread, share, 128), f32)],
+        cost=11,
     )
 
     dy = dy_own.astype(f32)
-    grad = give_back(total)
+    grad_parts = total[:1] + around(total[1:], -1, ranks)
+    attn_part = scatter_dp(after(grads_attn, feed_part))
+    parts = jnp.concatenate([feed_part[:, :hidden], attn_part], axis=1)
+    parts = parts.reshape(ranks, share, parts.shape[1])
+    parts = [lax.dynamic_index_in_dim(parts, (rank + r) % ranks, 0, False) for r in range(ranks)]
+    parts = parts[:1] + around([after(p, *grad_parts) for p in parts[1:]], 1, ranks)
+    grad = sum(part.astype(f32) for part in grad_parts)
     rows_own = x_own.astype(f32)
     centred = rows_own - jnp.mean(rows_own, axis=-1, keepdims=True)
     rstd = lax.rsqrt(jnp.mean(centred * centred, axis=-1, keepdims=True) + eps)
@@ -729,69 +911,30 @@
         - hat * jnp.mean(grad * hat, axis=-1, keepdims=True)
     )
 
-    qkv_bias_part = lax.dynamic_update_slice(
-        jnp.zeros((3, ranks, cols), f32), attn_bias[0].reshape(3, 1, cols), (0, rank, 0)
-    )
-    up_bias_part = lax.dynamic_update_slice(
-        jnp.zeros(ranks * hidden, f32), feed_sums[2], (rank * hidden,)
-    )
-    small_part = jnp.concatenate(
-        [
-            jnp.stack(
-                [attn_sums[0], attn_sums[1], feed_sums[0], feed_sums[1], jnp.sum(dy, axis=0)],
-                axis=1,
-            ),
-            qkv_bias_part.reshape(width, 3),
-            up_bias_part.reshape(width, ratio),
-        ],
-        axis=1,
-    ).astype(bf16)
-    attn_part = lax.psum_scatter(
-        jnp.concatenate(
-            [
-                part_attn,
-                part_proj.astype(bf16).reshape(width, cols),
-                jnp.pad(small_part, ((0, 0), (0, 128 - small_part.shape[1]))),
-            ],
-            axis=1,
-        ),
-        "dp",
-        scatter_dimension=0,
-        tiled=True,
-    )
     factor = 1.0 / math.sqrt(count * groups)
-
-    def exchange(parts):
-        parts = parts.reshape(ranks, share, parts.shape[1])
-        return lax.all_to_all(parts, "seq", 0, 0, tiled=True).astype(f32)
-
-    def to_owner(parts):
-        home = [((k % groups) * ranks + k // groups, k) for k in range(spread)]
-        return lax.ppermute(parts, ("dp", "seq"), home).astype(f32) * factor
-
-    up_own = jnp.transpose(exchange(feed_part[:, :hidden]), (1, 0, 2)) * factor
-    down_own = to_owner(feed_part[:, hidden:])
-    rest = exchange(
-        jnp.concatenate([attn_part[:, :mixed_cols], attn_part[:, mixed_cols + cols :]], axis=1)
-    )
-    qkv_own = rest[:, :, :mixed_cols].reshape(ranks, share, 3, cols) * factor
-    small_own = jnp.sum(rest[:, :, mixed_cols:], axis=0) * factor
-    proj_own = to_owner(attn_part[:, mixed_cols : mixed_cols + cols]).reshape(share, width)
+    home = [((k % groups) * ranks + k // groups, k) for k in range(spread)]
+    proj_part = lax.ppermute(feed_part[:, hidden + width :], ("dp", "seq"), home)
+    down_part = feed_part[:, hidden : hidden + width]
+    results = [(share, 3 * width), (share, ranks * hidden), (share, width), (piece, width)]
+    results += [(share,)] * 5 + [(3 * share,), (ratio * share,)]
+    qkv_own, up_own, proj_own, down_own, *small_own = call(
+        functools.partial(finish_kernel, factor=factor, hidden=hidden),
+        (1,),
+        [(spot, SMEM)] + [(a, whole_block(a.shape)) for a in (*parts, down_part, proj_part)],
+        [(shape(size, f32), whole_block(size)) for size in results],
+    )
     return (
         hidden_out.reshape(hidden_in.shape),
         grad_in.astype(bf16).reshape(hidden_in.shape),
-        small_own[:, 0],
-        small_own[:, 1],
-        small_own[:, 2],
-        small_own[:, 3],
-        jnp.transpose(qkv_own, (1, 2, 0, 3)).reshape(share, 3 * width),
-        small_own[:, 5:8].reshape(share * 3),
+        *small_own[:4],
+        qkv_own,
+        small_own[5],
         proj_own,
-        small_own[:, 4],
-        up_own.reshape(share, ranks * hidden),
-        small_own[:, 8 : 8 + ratio].reshape(share * ratio),
+        small_own[4],
+        up_own,
+        small_own[6],
         down_own,
-        small_own[:, 4],
+        small_own[4],
     )
 
 

time: 321 us -> 218 us (0.68)
  waiting for transfers between devices: 96.7 us -> 60.4 us
  local copies, waits for them, and re-layouts: 38.5 us -> 7.19 us
  starting transfers between devices: 89.6 us -> 61.3 us
  between operations: 14.8 us -> 1.1 us
  Pallas kernels: 63 us -> 74.8 us
  other arithmetic: 16.6 us -> 11.8 us
    ppermute x15 -> x18, waiting for transfers between devices: 75.4 us -> 47 us  [shift(): lax.ppermute(block, 'seq', [(k, (k + amount) % ranks) for k in range(rank...]
    ppermute x15 -> x18, starting transfers between devices: 67.1 us -> 41.7 us  [shift(): lax.ppermute(block, 'seq', [(k, (k + amount) % ranks) for k in range(rank...]
    reshape x20 -> x0, local copies, waits for them, and re-layouts: 12.3 us -> none  [the longest x2 1.14 us: per_device_heads(): qkv_weight.reshape(share, 3, ranks, cols)]
    pallas_call x5 -> x8, Pallas kernels: 63 us -> 74.8 us  [call(): pl.pallas_call(kernel, grid_spec=pltpu.PrefetchScalarGridSpec(num_scalar_...]
    all_to_all x2, waiting for transfers between devices: 11.3 us -> 0.01 us  [scatter_dp(): lax.all_to_all(parts.reshape(8, -1, parts.shape[1]), 'dp', 0, 0, tiled=True)]
    concatenate x6 -> x3, other arithmetic: 8.6 us -> 2.53 us  [the longest x1 1.26 us: per_device_heads(): dy_all = jnp.concatenate([dy_own] + around([dy_go] * (ranks - 1), 1, ranks))]
    slice x19 -> x3, local copies, waits for them, and re-layouts: 7.49 us -> 1.51 us  [the longest x1 0.82 us: per_device_heads(): hidden_out = (x_own.astype(f32) + vec[5:6] + out_sum).astype(bf16)]
    another operation x17 -> x0, local copies, waits for them, and re-layouts: 5.62 us -> none  [the longest x7 4.24 us: per_device_heads(): jnp.stack([attn_sums[0], attn_sums[1], feed_sums[0], feed_sums[1], jnp.su...]
  transfers between devices with their start and end apart: 28 -> 28, of which waited for: 14 -> 10; matrix products, arithmetic and copies ran while one was open for 10% -> 7% of each run, Pallas kernels for 0% -> 32%
where the time goes in v2:
time: 218 us; the launch traced here: 217 us
  Pallas kernels  74.8 us (34%)
  starting transfers between devices  61.3 us (28%)
  waiting for transfers between devices  60.4 us (28%)
  other arithmetic  11.8 us (5%)
  local copies, waits for them, and re-layouts  7.19 us (3%)
    pallas_call x8, Pallas kernels, call(): pl.pallas_call(kernel, grid_spec=pltpu.PrefetchScalarGridSpec(num_scalar_...  74.8 us
    ppermute x18, waiting for transfers between devices, shift(): lax.ppermute(block, 'seq', [(k, (k + amount) % ranks) for k in range(rank...  47 us
    ppermute x18, starting transfers between devices, shift(): lax.ppermute(block, 'seq', [(k, (k + amount) % ranks) for k in range(rank...  41.7 us
    ppermute x6, waiting for transfers between devices, swap(): return lax.ppermute(block, 'dp', [(k, k ^ mask) for k in range(8)])  13.4 us
    ppermute x6, starting transfers between devices, swap(): return lax.ppermute(block, 'dp', [(k, k ^ mask) for k in range(8)])  9 us
    all_to_all x2, starting transfers between devices, scatter_dp(): lax.all_to_all(parts.reshape(8, -1, parts.shape[1]), 'dp', 0, 0, tiled=True)  7.87 us
  transfers between devices with their start and end apart: 28, of which 10 were waited for; matrix products, arithmetic and copies ran while one was open for 7% of the time, Pallas kernels for 32%

profile of v2, /device:TPU:0, one launch (start us, length us, event | category | flops | bytes accessed | tf_op | source)
XLA Modules:
  0.0 216.6 jit_solution(18017416542656391094)
XLA Ops:
  1.3 2.2 %shard_map.263 = (bf16[24,1472]{1,0:T(8,128)(2,1)}, bf16[24,1472]{1,0:T(8,128)(2,1)}, bf16[24,1472]{1,0:T(8,128)(2,1)}, bf16[24,1472]{1,0:T(8,128)(2,1)}, bf16[96,192]{1,0:T(8,128)(2,1)}) custom-call(s32[2]{0:T(128)} %pad_add_fusion.rank_ref.spot_ref, bf16[24,3072]{1,0:T(8,128)(2,1)} %up_ref.1, bf16[24,2304]{1,0:T(8,128)(2,1)} %qkv_ref.1, ...), custom_call_target="tpu_custom_call" | custom-call | flops 1000000000 | tf_op jit(solution)/shard_map/pallas_call | solution.py:668
  3.5 3.0 %collective-permute-start = (bf16[24,1472]{1,0:T(8,128)(2,1)}, bf16[24,1472]{1,0:T(8,128)(2,1)S(1)}, u32[]{:S(2)}, u32[]{:S(2)}) collective-permute-start(bf16[24,1472]{1,0:T(8,128)(2,1)} %get-tuple-element.69), channel_id=1, source_target_pairs={{0,1},{1,2},{2,3},{3,0},{4,5},{5,6},{6,7},{7,4},{8,9},{9,10},{10,1... | collective-permute-start | bytes 211976 | tf_op jit(solution)/shard_map/ppermute | solution.py:688
  6.5 2.6 %collective-permute-start.1 = (bf16[24,1472]{1,0:T(8,128)(2,1)}, bf16[24,1472]{1,0:T(8,128)(2,1)S(1)}, u32[]{:S(2)}, u32[]{:S(2)}) collective-permute-start(bf16[24,1472]{1,0:T(8,128)(2,1)} %get-tuple-element.70), channel_id=1, source_target_pairs={{0,2},{1,3},{2,0},{3,1},{4,6},{5,7},{6,4},{7,5},{8,10},{9,11},{10,... | collective-permute-start | bytes 211976 | tf_op jit(solution)/shard_map/ppermute | solution.py:688
  18.5 5.2 %collective-permute-start.6 = (bf16[96,2432]{1,0:T(8,128)(2,1)}, bf16[96,2432]{1,0:T(8,128)(2,1)S(1)}, u32[]{:S(2)}, u32[]{:S(2)}) collective-permute-start(bf16[96,2432]{1,0:T(8,128)(2,1)} %shard_map.264), channel_id=1, source_target_pairs={{0,8},{4,12},{8,0},{12,4},{16,24},{20,28},{24,16},{28,20},{1,9},{5... | collective-permute-start | bytes 1400840 | tf_op jit(solution)/shard_map/ppermute | solution.py:698
  27.2 6.2 %collective-permute-done.6 = bf16[96,2432]{1,0:T(8,128)(2,1)S(1)} collective-permute-done((bf16[96,2432]{1,0:T(8,128)(2,1)}, bf16[96,2432]{1,0:T(8,128)(2,1)S(1)}, u32[]{:S(2)}, u32[]{:S(2)}) %collective-permute-start.6) | collective-permute-done | bytes 466976 | tf_op jit(solution)/shard_map/ppermute | solution.py:698
  37.4 5.8 %collective-permute-done.10 = bf16[48,2432]{1,0:T(8,128)(2,1)S(1)} collective-permute-done((bf16[48,2432]{1,0:T(8,128)(2,1)S(1)}, bf16[48,2432]{1,0:T(8,128)(2,1)S(1)}, u32[]{:S(2)}, u32[]{:S(2)}) %collective-permute-start.10) | collective-permute-done | bytes 233504 | tf_op jit(solution)/shard_map/ppermute | solution.py:698
  43.3 2.3 %collective-permute-start.8 = (bf16[256,768]{1,0:T(8,128)(2,1)S(1)}, bf16[256,768]{1,0:T(8,128)(2,1)S(1)}, u32[]{:S(2)}, u32[]{:S(2)}) collective-permute-start(bf16[256,768]{1,0:T(8,128)(2,1)S(1)} %bitcast.50), channel_id=1, source_target_pairs={{0,3},{1,0},{2,1},{3,2},{4,7},{5,4},{6,5},{7,6},{8,11},{9,8},{10,9... | collective-permute-start | bytes 1179656 | tf_op jit(solution)/shard_map/ppermute | solution.py:688
  45.7 7.6 %collective-permute-done.4 = bf16[256,768]{1,0:T(8,128)(2,1)S(1)} collective-permute-done((bf16[256,768]{1,0:T(8,128)(2,1)S(1)}, bf16[256,768]{1,0:T(8,128)(2,1)S(1)}, u32[]{:S(2)}, u32[]{:S(2)}) %collective-permute-start.4) | collective-permute-done | bytes 393248 | tf_op jit(solution)/shard_map/ppermute | solution.py:688
  53.3 7.3 %collective-permute-done.8 = bf16[256,768]{1,0:T(8,128)(2,1)S(1)} collective-permute-done((bf16[256,768]{1,0:T(8,128)(2,1)S(1)}, bf16[256,768]{1,0:T(8,128)(2,1)S(1)}, u32[]{:S(2)}, u32[]{:S(2)}) %collective-permute-start.8) | collective-permute-done | bytes 393248 | tf_op jit(solution)/shard_map/ppermute | solution.py:688
  63.5 2.6 %collective-permute-start.17 = (bf16[256,768]{1,0:T(8,128)(2,1)S(1)}, bf16[256,768]{1,0:T(8,128)(2,1)S(1)}, u32[]{:S(2)}, u32[]{:S(2)}) collective-permute-start(bf16[256,768]{1,0:T(8,128)(2,1)S(1)} %bitcast.65), channel_id=1, source_target_pairs={{0,3},{1,0},{2,1},{3,2},{4,7},{5,4},{6,5},{7,6},{8,11},{9,8},{10,9... | collective-permute-start | bytes 1179656 | tf_op jit(solution)/shard_map/ppermute | solution.py:688
  66.1 11.4 %shard_map.265 = (bf16[1024,768]{1,0:T(8,128)(2,1)}, bf16[1024,768]{1,0:T(8,128)(2,1)}, bf16[1024,768]{1,0:T(8,128)(2,1)}, bf16[1024,768]{1,0:T(8,128)(2,1)}, f3...) custom-call(s32[2]{0:T(128)} %pad_add_fusion.rank_ref.spot_ref, ...), custom_call_target="tpu_custom_call" | custom-call | flops 10000000000 | tf_op jit(solution)/shard_map/pallas_call | solution.py:668
  77.5 16.4 %shard_map.266 = (bf16[3,1024,1024]{2,1,0:T(8,128)(2,1)}, f32[3,8,1024]{2,1,0:T(8,128)}, bf16[192,1024]{1,0:T(8,128)(2,1)}, bf16[256,768]{1,0:T(8,128)(2,1)}, bf...) custom-call(s32[8,1024]{1,0:T(8,128)} %add_add_fusion.span_ref, ...), custom_call_target="tpu_custom_call" | custom-call | flops 16000000000 | tf_op jit(solution)/shard_map/pallas_call | solution.py:668
  97.3 11.9 %shard_map.267 = (f32[1024,768]{1,0:T(8,128)}, bf16[768,1728]{1,0:T(8,128)(2,1)}, f32[8,768]{1,0:T(8,128)}) custom-call(bf16[1024,768]{1,0:T(8,128)(2,1)} %pad_maximum_fusion.1.dy_ref, bf16[1024,768]{1,0:T(8,128)(2,1)} %pad_maximum_fusion.x_ref, bf16[1024,768]{1,0:T(8,128)(2,1)} %get-tuple-element.87.act_ref, bf16[1024,768]{1,0:T(8,128)(2,1)} %get-tuple-element.88.slope_ref, ...), custom_call_target="tpu_custom_call" | custom-call | flops 12000000000 | tf_op jit(solution)/shard_map/pallas_call | solution.py:668
  109.1 4.2 %collective-permute-start.18 = (bf16[256,768]{1,0:T(8,128)(2,1)}, bf16[256,768]{1,0:T(8,128)(2,1)}, u32[]{:S(2)}, u32[]{:S(2)}) collective-permute-start(bf16[256,768]{1,0:T(8,128)(2,1)} %get-tuple-element.91), channel_id=1, source_target_pairs={{0,2},{1,3},{2,0},{3,1},{4,6},{5,7},{6,4},{7,5},{8,10},{9,11},{10,... | collective-permute-start | bytes 1179656 | tf_op jit(solution)/shard_map/ppermute | solution.py:688
  114.5 3.8 %all-to-all-start = ((bf16[8,96,1728]{2,1,0:T(8,128)(2,1)}), bf16[8,96,1728]{2,1,0:T(8,128)(2,1)S(1)}, u32[]{:S(2)}, u32[]{:S(2)}) async-start(bf16[8,96,1728]{2,1,0:T(8,128)(2,1)} %bitcast.61), calls=%async_computation | async-start | bytes 5505024 | tf_op jit(solution)/shard_map/all_to_all | solution.py:718
  118.3 15.7 %shard_map.268 = (f32[192,1024]{1,0:T(8,128)}, f32[3,1024,64]{2,1,0:T(8,128)}, f32[3,1024,64]{2,1,0:T(8,128)}) custom-call(bf16[1024,768]{1,0:T(8,128)(2,1)} %pad_maximum_fusion.1.dy_ref, bf16[192,768]{1,0:T(8,128)(2,1)} %get-tuple-element.79.out_ref, bf16[192,1024]{1,0:T(8,128)(2,1)} %get-tuple-element.92.heads_ref, ...), custom_call_target="tpu_custom_call" | custom-call | flops 16000000000 | tf_op jit(solution)/shard_map/pallas_call | solution.py:668
  134.0 12.9 %shard_map.269 = (bf16[256,768]{1,0:T(8,128)(2,1)}, bf16[256,768]{1,0:T(8,128)(2,1)}, bf16[256,768]{1,0:T(8,128)(2,1)}, bf16[256,768]{1,0:T(8,128)(2,1)}, bf16[768,704]{1,0:T(8,128)(2,1)}) custom-call(s32[2]{0:T(128)} %pad_add_fusion.rank_ref.spot_ref, f32[192,1024]{1,0:T(8,128)} %get-tuple-element.96.gquery_ref, f32[3,1024,64]{2,1,0:T(8,128)} %get-tuple-element.97.gkey_ref, ...), custom_call_target="tpu_custom_call" | custom-call | flops 11000000512 | tf_op jit(solution)/shard_map/pallas_call | solution.py:668
  146.9 5.9 %collective-permute-start.19 = (bf16[256,768]{1,0:T(8,128)(2,1)}, bf16[256,768]{1,0:T(8,128)(2,1)}, u32[]{:S(2)}, u32[]{:S(2)}) collective-permute-start(bf16[256,768]{1,0:T(8,128)(2,1)} %get-tuple-element.102), channel_id=1, source_target_pairs={{0,3},{1,0},{2,1},{3,2},{4,7},{5,4},{6,5},{7,6},{8,11},{9,8},{10,9... | collective-permute-start | bytes 1179656 | tf_op jit(solution)/shard_map/ppermute | solution.py:688
  152.8 7.7 %collective-permute-start.20 = (bf16[256,768]{1,0:T(8,128)(2,1)}, bf16[256,768]{1,0:T(8,128)(2,1)}, u32[]{:S(2)}, u32[]{:S(2)}) collective-permute-start(bf16[256,768]{1,0:T(8,128)(2,1)} %get-tuple-element.103), channel_id=1, source_target_pairs={{0,2},{1,3},{2,0},{3,1},{4,6},{5,7},{6,4},{7,5},{8,10},{9,11},{10,... | collective-permute-start | bytes 1179656 | tf_op jit(solution)/shard_map/ppermute | solution.py:688
  162.0 4.1 %all-to-all-start.1 = ((bf16[8,96,704]{2,1,0:T(8,128)(2,1)}), bf16[8,96,704]{2,1,0:T(8,128)(2,1)S(1)}, u32[]{:S(2)}, u32[]{:S(2)}) async-start(bf16[8,96,704]{2,1,0:T(8,128)(2,1)} %bitcast.67), calls=%async_computation.1 | async-start | bytes 2359296 | tf_op jit(solution)/shard_map/all_to_all | solution.py:718
  168.8 26.5 %collective-permute-done.20 = bf16[256,768]{1,0:T(8,128)(2,1)} collective-permute-done((bf16[256,768]{1,0:T(8,128)(2,1)}, bf16[256,768]{1,0:T(8,128)(2,1)}, u32[]{:S(2)}, u32[]{:S(2)}) %collective-permute-start.20) | collective-permute-done | bytes 393248 | tf_op jit(solution)/shard_map/ppermute | solution.py:688
  199.9 6.5 %collective-permute-start.24 = (bf16[24,1472]{1,0:T(8,128)(2,1)S(1)}, bf16[24,1472]{1,0:T(8,128)(2,1)S(1)}, u32[]{:S(2)}, u32[]{:S(2)}) collective-permute-start(bf16[24,1472]{1,0:T(8,128)(2,1)S(1)} %get-tuple-element.110), channel_id=1, source_target_pairs={{0,3},{1,0},{2,1},{3,2},{4,7},{5,4},{6,5},{7,6},{8,11},{9,8},{10,9... | collective-permute-start | bytes 211976 | tf_op jit(solution)/shard_map/ppermute | solution.py:688
  207.0 3.0 %fusion.9 = (bf16[256,768]{1,0:T(8,128)(2,1)}, bf16[256,768]{1,0:T(8,128)(2,1)}) fusion(f32[256]{0:T(256)S(1)} %get-tuple-element.139, f32[256]{0:T(256)S(1)} %get-tuple-element.134, f32[256]{0:T(256)S(1)} %get-tuple-element.140, f32[256]{0:T(256)S(1)} %rsqrt_bitcast_fusion, bf16[1,2,128,768]{3,2,1,0:T(8,128)(2,1)S(1)} %copy-done.3, ...), kind=kLoop, calls=%fused_computation.17 | loop fusion | flops 5308416 | bytes 4725760 | tf_op jit(solution)/shard_map/convert_element_type | solution.py:928
  213.2 2.2 %shard_map.270 = (f32[24,2304]{1,0:T(8,128)}, f32[24,3072]{1,0:T(8,128)}, f32[24,768]{1,0:T(8,128)}, f32[96,768]{1,0:T(8,128)}, f32[24]{0:T(128)}, /*index=5*/f3...) custom-call(s32[2]{0:T(128)} %pad_add_fusion.rank_ref.spot_ref, ...), custom_call_target="tpu_custom_call" | custom-call | flops 1000000000 | tf_op jit(solution)/shard_map/pallas_call | solution.py:668
  (120 shorter events, 38.5 us)
Async XLA Ops:
  3.5 12.3 %collective-permute-start = (bf16[24,1472]{1,0:T(8,128)(2,1)}, bf16[24,1472]{1,0:T(8,128)(2,1)S(1)}, u32[]{:S(2)}, u32[]{:S(2)}) collective-permute-start(bf16[24,1472]{1,0:T(8,128)(2,1)} %get-tuple-element.69), channel_id=1, source_target_pairs={{0,1},{1,2},{2,3},{3,0},{4,5},{5,6},{6,7},{7,4},{8,9},{9,10},{10,1... | collective-permute-start | bytes 211976 | tf_op jit(solution)/shard_map/ppermute | solution.py:688
  6.5 9.3 %collective-permute-start.1 = (bf16[24,1472]{1,0:T(8,128)(2,1)}, bf16[24,1472]{1,0:T(8,128)(2,1)S(1)}, u32[]{:S(2)}, u32[]{:S(2)}) collective-permute-start(bf16[24,1472]{1,0:T(8,128)(2,1)} %get-tuple-element.70), channel_id=1, source_target_pairs={{0,2},{1,3},{2,0},{3,1},{4,6},{5,7},{6,4},{7,5},{8,10},{9,11},{10,... | collective-permute-start | bytes 211976 | tf_op jit(solution)/shard_map/ppermute | solution.py:688
  18.5 14.9 %collective-permute-start.6 = (bf16[96,2432]{1,0:T(8,128)(2,1)}, bf16[96,2432]{1,0:T(8,128)(2,1)S(1)}, u32[]{:S(2)}, u32[]{:S(2)}) collective-permute-start(bf16[96,2432]{1,0:T(8,128)(2,1)} %shard_map.264), channel_id=1, source_target_pairs={{0,8},{4,12},{8,0},{12,4},{16,24},{20,28},{24,16},{28,20},{1,9},{5... | collective-permute-start | bytes 1400840 | tf_op jit(solution)/shard_map/ppermute | solution.py:698
  23.7 11.1 %collective-permute-start.7 = (bf16[96,2432]{1,0:T(8,128)(2,1)}, bf16[96,2432]{1,0:T(8,128)(2,1)S(1)}, u32[]{:S(2)}, u32[]{:S(2)}) collective-permute-start(bf16[96,2432]{1,0:T(8,128)(2,1)} %shard_map.264), channel_id=1, source_target_pairs={{0,16},{4,20},{8,24},{12,28},{16,0},{20,4},{24,8},{28,12},{1,17},{... | collective-permute-start | bytes 1400840 | tf_op jit(solution)/shard_map/ppermute | solution.py:698
  25.2 20.5 %collective-permute-start.3 = (bf16[256,768]{1,0:T(8,128)(2,1)S(1)}, bf16[256,768]{1,0:T(8,128)(2,1)S(1)}, u32[]{:S(2)}, u32[]{:S(2)}) collective-permute-start(bf16[256,768]{1,0:T(8,128)(2,1)S(1)} %bitcast.48), channel_id=1, source_target_pairs={{0,1},{1,2},{2,3},{3,0},{4,5},{5,6},{6,7},{7,4},{8,9},{9,10},{10,1... | collective-permute-start | bytes 1179656 | tf_op jit(solution)/shard_map/ppermute | solution.py:688
  25.2 28.1 %collective-permute-start.4 = (bf16[256,768]{1,0:T(8,128)(2,1)S(1)}, bf16[256,768]{1,0:T(8,128)(2,1)S(1)}, u32[]{:S(2)}, u32[]{:S(2)}) collective-permute-start(bf16[256,768]{1,0:T(8,128)(2,1)S(1)} %bitcast.49), channel_id=1, source_target_pairs={{0,2},{1,3},{2,0},{3,1},{4,6},{5,7},{6,4},{7,5},{8,10},{9,11},{10,... | collective-permute-start | bytes 1179656 | tf_op jit(solution)/shard_map/ppermute | solution.py:688
  35.0 26.9 %collective-permute-start.9 = (bf16[3,96,2432]{2,1,0:T(8,128)(2,1)S(1)}, bf16[3,96,2432]{2,1,0:T(8,128)(2,1)S(1)}, u32[]{:S(2)}, u32[]{:S(2)}) collective-permute-start(bf16[3,96,2432]{2,1,0:T(8,128)(2,1)S(1)} %pad_maximum_fusion.2), channel_id=1, source_target_pairs={{0,4},{4,0},{8,12},{12,8},{16,20},{20,16},{24,28},{28,24},{1,5},{5... | collective-permute-start | bytes 4202504 | tf_op jit(solution)/shard_map/ppermute | solution.py:698
  35.1 8.2 %collective-permute-start.10 = (bf16[48,2432]{1,0:T(8,128)(2,1)S(1)}, bf16[48,2432]{1,0:T(8,128)(2,1)S(1)}, u32[]{:S(2)}, u32[]{:S(2)}) collective-permute-start(bf16[48,2432]{1,0:T(8,128)(2,1)S(1)} %slice.46), channel_id=1, source_target_pairs={{0,16},{4,20},{8,24},{12,28},{16,0},{20,4},{24,8},{28,12},{1,17},{... | collective-permute-start | bytes 700424 | tf_op jit(solution)/shard_map/ppermute | solution.py:698
  36.9 8.7 %collective-permute-start.11 = (bf16[48,2432]{1,0:T(8,128)(2,1)S(1)}, bf16[48,2432]{1,0:T(8,128)(2,1)S(1)}, u32[]{:S(2)}, u32[]{:S(2)}) collective-permute-start(bf16[48,2432]{1,0:T(8,128)(2,1)S(1)} %slice.47), channel_id=1, source_target_pairs={{0,8},{4,12},{8,0},{12,4},{16,24},{20,28},{24,16},{28,20},{1,9},{5... | collective-permute-start | bytes 700424 | tf_op jit(solution)/shard_map/ppermute | solution.py:698
  43.3 17.4 %collective-permute-start.8 = (bf16[256,768]{1,0:T(8,128)(2,1)S(1)}, bf16[256,768]{1,0:T(8,128)(2,1)S(1)}, u32[]{:S(2)}, u32[]{:S(2)}) collective-permute-start(bf16[256,768]{1,0:T(8,128)(2,1)S(1)} %bitcast.50), channel_id=1, source_target_pairs={{0,3},{1,0},{2,1},{3,2},{4,7},{5,4},{6,5},{7,6},{8,11},{9,8},{10,9... | collective-permute-start | bytes 1179656 | tf_op jit(solution)/shard_map/ppermute | solution.py:688
  45.6 16.5 %collective-permute-start.12 = (bf16[96,2432]{1,0:T(8,128)(2,1)S(1)}, bf16[96,2432]{1,0:T(8,128)(2,1)S(1)}, u32[]{:S(2)}, u32[]{:S(2)}) collective-permute-start(bf16[96,2432]{1,0:T(8,128)(2,1)S(1)} %constant_dynamic-update-slice_fusion), channel_id=1, source_target_pairs={{0,4},{4,0},{8,12},{12,8},{16,20},{20,16},{24,28},{28,24},{1,5},{5... | collective-permute-start | bytes 1400840 | tf_op jit(solution)/shard_map/ppermute | solution.py:698
  62.2 33.8 %collective-permute-start.15 = (bf16[256,768]{1,0:T(8,128)(2,1)S(1)}, bf16[256,768]{1,0:T(8,128)(2,1)S(1)}, u32[]{:S(2)}, u32[]{:S(2)}) collective-permute-start(bf16[256,768]{1,0:T(8,128)(2,1)S(1)} %bitcast.63), channel_id=1, source_target_pairs={{0,1},{1,2},{2,3},{3,0},{4,5},{5,6},{6,7},{7,4},{8,9},{9,10},{10,1... | collective-permute-start | bytes 1179656 | tf_op jit(solution)/shard_map/ppermute | solution.py:688
  62.9 33.1 %collective-permute-start.16 = (bf16[256,768]{1,0:T(8,128)(2,1)S(1)}, bf16[256,768]{1,0:T(8,128)(2,1)S(1)}, u32[]{:S(2)}, u32[]{:S(2)}) collective-permute-start(bf16[256,768]{1,0:T(8,128)(2,1)S(1)} %bitcast.64), channel_id=1, source_target_pairs={{0,2},{1,3},{2,0},{3,1},{4,6},{5,7},{6,4},{7,5},{8,10},{9,11},{10,... | collective-permute-start | bytes 1179656 | tf_op jit(solution)/shard_map/ppermute | solution.py:688
  63.5 32.6 %collective-permute-start.17 = (bf16[256,768]{1,0:T(8,128)(2,1)S(1)}, bf16[256,768]{1,0:T(8,128)(2,1)S(1)}, u32[]{:S(2)}, u32[]{:S(2)}) collective-permute-start(bf16[256,768]{1,0:T(8,128)(2,1)S(1)} %bitcast.65), channel_id=1, source_target_pairs={{0,3},{1,0},{2,1},{3,2},{4,7},{5,4},{6,5},{7,6},{8,11},{9,8},{10,9... | collective-permute-start | bytes 1179656 | tf_op jit(solution)/shard_map/ppermute | solution.py:688
  93.9 19.4 %collective-permute-start.13 = (bf16[256,768]{1,0:T(8,128)(2,1)}, bf16[256,768]{1,0:T(8,128)(2,1)}, u32[]{:S(2)}, u32[]{:S(2)}) collective-permute-start(bf16[256,768]{1,0:T(8,128)(2,1)} %get-tuple-element.81), channel_id=1, source_target_pairs={{0,3},{1,0},{2,1},{3,2},{4,7},{5,4},{6,5},{7,6},{8,11},{9,8},{10,9... | collective-permute-start | bytes 1179656 | tf_op jit(solution)/shard_map/ppermute | solution.py:688
  95.1 19.3 %collective-permute-start.14 = (bf16[256,768]{1,0:T(8,128)(2,1)}, bf16[256,768]{1,0:T(8,128)(2,1)}, u32[]{:S(2)}, u32[]{:S(2)}) collective-permute-start(bf16[256,768]{1,0:T(8,128)(2,1)} %get-tuple-element.82), channel_id=1, source_target_pairs={{0,1},{1,2},{2,3},{3,0},{4,5},{5,6},{6,7},{7,4},{8,9},{9,10},{10,1... | collective-permute-start | bytes 1179656 | tf_op jit(solution)/shard_map/ppermute | solution.py:688
  109.1 24.8 %collective-permute-start.18 = (bf16[256,768]{1,0:T(8,128)(2,1)}, bf16[256,768]{1,0:T(8,128)(2,1)}, u32[]{:S(2)}, u32[]{:S(2)}) collective-permute-start(bf16[256,768]{1,0:T(8,128)(2,1)} %get-tuple-element.91), channel_id=1, source_target_pairs={{0,2},{1,3},{2,0},{3,1},{4,6},{5,7},{6,4},{7,5},{8,10},{9,11},{10,... | collective-permute-start | bytes 1179656 | tf_op jit(solution)/shard_map/ppermute | solution.py:688
  114.5 46.3 %all-to-all-start = ((bf16[8,96,1728]{2,1,0:T(8,128)(2,1)}), bf16[8,96,1728]{2,1,0:T(8,128)(2,1)S(1)}, u32[]{:S(2)}, u32[]{:S(2)}) async-start(bf16[8,96,1728]{2,1,0:T(8,128)(2,1)} %bitcast.61), calls=%async_computation | async-start | bytes 5505024 | tf_op jit(solution)/shard_map/all_to_all | solution.py:718
  146.9 21.9 %collective-permute-start.19 = (bf16[256,768]{1,0:T(8,128)(2,1)}, bf16[256,768]{1,0:T(8,128)(2,1)}, u32[]{:S(2)}, u32[]{:S(2)}) collective-permute-start(bf16[256,768]{1,0:T(8,128)(2,1)} %get-tuple-element.102), channel_id=1, source_target_pairs={{0,3},{1,0},{2,1},{3,2},{4,7},{5,4},{6,5},{7,6},{8,11},{9,8},{10,9... | collective-permute-start | bytes 1179656 | tf_op jit(solution)/shard_map/ppermute | solution.py:688
  152.8 42.5 %collective-permute-start.20 = (bf16[256,768]{1,0:T(8,128)(2,1)}, bf16[256,768]{1,0:T(8,128)(2,1)}, u32[]{:S(2)}, u32[]{:S(2)}) collective-permute-start(bf16[256,768]{1,0:T(8,128)(2,1)} %get-tuple-element.103), channel_id=1, source_target_pairs={{0,2},{1,3},{2,0},{3,1},{4,6},{5,7},{6,4},{7,5},{8,10},{9,11},{10,... | collective-permute-start | bytes 1179656 | tf_op jit(solution)/shard_map/ppermute | solution.py:688
  160.5 34.8 %collective-permute-start.21 = (bf16[256,768]{1,0:T(8,128)(2,1)}, bf16[256,768]{1,0:T(8,128)(2,1)}, u32[]{:S(2)}, u32[]{:S(2)}) collective-permute-start(bf16[256,768]{1,0:T(8,128)(2,1)} %get-tuple-element.104), channel_id=1, source_target_pairs={{0,1},{1,2},{2,3},{3,0},{4,5},{5,6},{6,7},{7,4},{8,9},{9,10},{10,1... | collective-permute-start | bytes 1179656 | tf_op jit(solution)/shard_map/ppermute | solution.py:688
  162.0 37.0 %all-to-all-start.1 = ((bf16[8,96,704]{2,1,0:T(8,128)(2,1)}), bf16[8,96,704]{2,1,0:T(8,128)(2,1)S(1)}, u32[]{:S(2)}, u32[]{:S(2)}) async-start(bf16[8,96,704]{2,1,0:T(8,128)(2,1)} %bitcast.67), calls=%async_computation.1 | async-start | bytes 2359296 | tf_op jit(solution)/shard_map/all_to_all | solution.py:718
  197.1 13.0 %collective-permute-start.25 = (bf16[96,192]{1,0:T(8,128)(2,1)S(1)}, bf16[96,192]{1,0:T(8,128)(2,1)}, u32[]{:S(2)}, u32[]{:S(2)}) collective-permute-start(bf16[96,192]{1,0:T(8,128)(2,1)S(1)} %slice.50), channel_id=1, source_target_pairs={{0,0},{4,1},{8,2},{12,3},{16,4},{20,5},{24,6},{28,7},{1,8},{5,9},{... | collective-permute-start | bytes 110600 | tf_op jit(solution)/shard_map/ppermute | solution.py:916
  199.9 10.1 %collective-permute-start.24 = (bf16[24,1472]{1,0:T(8,128)(2,1)S(1)}, bf16[24,1472]{1,0:T(8,128)(2,1)S(1)}, u32[]{:S(2)}, u32[]{:S(2)}) collective-permute-start(bf16[24,1472]{1,0:T(8,128)(2,1)S(1)} %get-tuple-element.110), channel_id=1, source_target_pairs={{0,3},{1,0},{2,1},{3,2},{4,7},{5,4},{6,5},{7,6},{8,11},{9,8},{10,9... | collective-permute-start | bytes 211976 | tf_op jit(solution)/shard_map/ppermute | solution.py:688
  (20 other events, 212.0 us)

commit v3 on v2

--- a/solution.py
+++ b/solution.py
@@ -399,19 +399,27 @@
     )
 
 
-def store_at(refs, step, block):
-    for at, ref in enumerate(refs):
-
-        @pl.when(step == at)
-        def _():
-            ref[...] = block
-
-
-def front_kernel(
-    rank_ref, x_ref, small_ref, cos_ref, sin_ref, up_ref, down_ref, attn_ref,
-    n1_ref, n2_ref, act_ref, slope_ref, fed_ref, upright_ref, rows_ref, vec_ref, own_out_ref, bias_ref,
-    *, ranks, ratio,
-):
+def join(refs):
+    return jnp.concatenate([ref[...] for ref in refs], axis=0)
+
+
+def store_blocks(refs, spot_ref, step, tile, parts):
+    half = tile.shape[0] // parts
+    for k in range(parts):
+        block = tile[k * half : (k + 1) * half]
+        where = spot_ref[2 + step * parts + k]
+        for r, ref in enumerate(refs):
+            for slot in range(parts):
+
+                @pl.when(where == r * parts + slot)
+                def _():
+                    ref[slot * half : (slot + 1) * half, :] = block
+
+
+def front_kernel(rank_ref, *refs, ranks, ratio, parts):
+    x_refs, (small_ref, cos_ref, sin_ref, up_ref, down_ref, attn_ref) = refs[:parts], refs[parts:-10]
+    n1_ref, n2_ref, act_ref, slope_ref, fed_ref, upright_ref, rows_ref = refs[-10:-3]
+    vec_ref, own_out_ref, bias_ref = refs[-3:]
     width, part3 = n1_ref.shape[1], upright_ref.shape[0]
     cols, hidden = part3 // 3, act_ref.shape[1]
     owners = ranks * 8
@@ -441,7 +449,7 @@
             )
         own_out_ref[...] = jnp.concatenate(rebuilt, axis=0).astype(bf16)
 
-    hat = normalise(x_ref[...].astype(f32))
+    hat = normalise(join(x_refs).astype(f32))
     vec = vec_ref[...]
     n1 = (hat * vec[0:1] + vec[1:2]).astype(bf16)
     n2 = (hat * vec[2:3] + vec[3:4]).astype(bf16)
@@ -471,39 +479,35 @@
     fed_ref[...] = product(active, down_ref[...])
 
 
-def attend_kernel(
-    span_ref, place_ref, key_ref, query_ref, value_ref, fed_ref, out_ref,
-    soft_ref, inv_ref, heads_ref, *refs,
-):
-    *sum_refs, bias_ref = refs
-    head = pl.program_id(1)
-
-    @pl.when(head == 0)
-    def _():
-        place = place_ref[...]
-        ok = (place <= span_ref[0:1]) & (place >= span_ref[1:2])
-        bias_ref[...] = jnp.where(ok, 0.0, masked)
-
-    scores = product(key_ref[head], query_ref[...]) + bias_ref[...]
-    weights = jnp.exp(scores - jnp.max(scores, axis=0, keepdims=True))
-    inverse = 1.0 / jnp.sum(weights, axis=0, keepdims=True)
-    soft = weights.astype(bf16)
-    soft_ref[0] = soft
-    inv_ref[0] = jnp.broadcast_to(inverse, inv_ref.shape[1:])
-    spot = pl.ds(pl.multiple_of(head * HD, HD), HD)
-    heads_ref[spot, :] = (product(value_ref[...], soft) * inverse).astype(bf16)
-
-    @pl.when(head == pl.num_programs(1) - 1)
-    def _():
-        part = (fed_ref[...] + product(heads_ref[...], out_ref[...], 0, 0)).astype(bf16)
-        store_at(sum_refs, pl.program_id(0), part)
-
-
-def feed_back_kernel(
-    dy_ref, x_ref, act_ref, slope_ref, n2_ref, vec_ref, up_ref, down_ref, heads_ref,
-    scaled_ref, grads_ref, sums_ref, acc_up, acc_down, acc_out,
-    *, ranks,
-):
+def attend_kernel(spot_ref, *refs, ranks, parts):
+    start_ref, key_ref, query_ref, value_ref, fed_ref, out_ref, soft_ref, inv_ref, heads_ref = refs[:9]
+    step, own = pl.program_id(0), query_ref.shape[1]
+
+    def tile(at):
+        held = own * (at + 1)
+        place = lax.broadcasted_iota(jnp.int32, (held, own), 0)
+        asks = lax.broadcasted_iota(jnp.int32, (held, own), 1) + at * own
+        bias = jnp.where((place <= asks) & (place >= start_ref[0:1]), 0.0, masked)
+        for head in range(key_ref.shape[0]):
+            spot = slice(head * HD, (head + 1) * HD)
+            scores = product(key_ref[head, :held], query_ref[spot, :]) + bias
+            weights = jnp.exp(scores - jnp.max(scores, axis=0, keepdims=True))
+            inverse = 1.0 / jnp.sum(weights, axis=0, keepdims=True)
+            soft = weights.astype(bf16)
+            soft_ref[head, :held] = soft
+            inv_ref[head : head + 1] = inverse
+            heads_ref[spot, :] = (product(value_ref[spot, :held], soft) * inverse).astype(bf16)
+
+    for at in range(ranks):
+        pl.when(step == at)(functools.partial(tile, at))
+    part = (fed_ref[...] + product(heads_ref[...], out_ref[...], 0, 0)).astype(bf16)
+    store_blocks(refs[9:], spot_ref, step, part, parts)
+
+
+def feed_back_kernel(spot_ref, *refs, ranks, parts):
+    dy_refs, x_refs, refs = refs[:parts], refs[parts : 2 * parts], refs[2 * parts :]
+    own_ref, act_ref, slope_ref, n2_ref, vec_ref, up_ref, down_ref, heads_ref = refs[:8]
+    scaled_ref, grads_ref, sums_ref, acc_up, acc_down, acc_out = refs[8:]
     step = pl.program_id(0)
 
     @pl.when(step == 0)
@@ -512,13 +516,13 @@
         acc_down[...] = jnp.zeros_like(acc_down)
         acc_out[...] = jnp.zeros_like(acc_out)
         sums_ref[...] = jnp.zeros_like(sums_ref)
-        sums_ref[3:4] = jnp.sum(dy_ref[...].astype(f32), axis=0, keepdims=True)
-
-    dy = dy_ref[...]
+        sums_ref[3:4] = jnp.sum(own_ref[...].astype(f32), axis=0, keepdims=True)
+
+    dy = join(dy_refs)
     grad_inner = product(dy, down_ref[...], 1, 1) * slope_ref[...].astype(f32)
     low = grad_inner.astype(bf16)
     grad = product(low, up_ref[...], 1, 1)
-    hat = normalise(x_ref[...].astype(f32))
+    hat = normalise(join(x_refs).astype(f32))
     scaled_ref[...] = grad * vec_ref[2:3]
     sums_ref[0:1] += jnp.sum(grad * hat, axis=0, keepdims=True)
     sums_ref[1:2] += jnp.sum(grad, axis=0, keepdims=True)
@@ -542,45 +546,46 @@
         grads_ref[:, edge + acc_down.shape[1] :] = flat.astype(bf16)
 
 
-def attend_back_kernel(
-    dy_ref, out_ref, heads_ref, inv_ref, soft_ref, value_ref, key_ref, query_ref, cos_ref, sin_ref,
-    gquery_ref, gkey_ref, gvalue_ref, held_ref,
-):
-    step, head = pl.program_id(0), pl.program_id(1)
-
-    @pl.when((step == 0) & (head == 0))
+def attend_back_kernel(spot_ref, *refs, ranks, parts):
+    dy_refs, refs = refs[:parts], refs[parts:]
+    out_ref, heads_ref, inv_ref, soft_ref, value_ref, key_ref, query_ref, cos_ref, sin_ref = refs[:9]
+    gquery_ref, gkey_ref, gvalue_ref = refs[9:]
+    step, own = pl.program_id(0), cos_ref.shape[1]
+
+    @pl.when(step == 0)
     def _():
         gkey_ref[...] = jnp.zeros_like(gkey_ref)
         gvalue_ref[...] = jnp.zeros_like(gvalue_ref)
 
-    @pl.when(head == 0)
-    def _():
-        held_ref[...] = product(out_ref[...], dy_ref[...], 1, 1).astype(bf16).astype(f32)
-
-    spot = pl.ds(pl.multiple_of(head * HD, HD), HD)
-    lifted = held_ref[spot, :] * inv_ref[0, 0:1]
-    delta = jnp.sum(lifted * heads_ref[spot, :].astype(f32), axis=0, keepdims=True)
-    lifted_rows = lifted.T.astype(bf16)
-    soft = soft_ref[0]
-    grad_soft = product(value_ref[head], lifted.astype(bf16))
-    grad_scores = (soft.astype(f32) * (grad_soft - delta)).astype(bf16)
-    gvalue_ref[head] += product(soft, lifted_rows)
-    gkey_ref[head] += product(grad_scores, query_ref[0])
-    back = product(key_ref[...], grad_scores) * HD**-0.5
-    gquery_ref[spot, :] = jnp.concatenate(turn(back, cos_ref[...], -sin_ref[...]), axis=0)
-
-
-def rear_kernel(
-    spot_ref, gquery_ref, gkey_ref, gvalue_ref, cos_ref, sin_ref, n1_ref, x_ref, scaled_ref, vec_ref,
-    attn_ref, feed_ref, *refs, ranks, ratio,
-):
-    total_refs, grads_ref = refs[:ranks], refs[ranks]
-    acc_ref, sums_ref, gbias_ref, small_ref = refs[-4:]
+    lifted_all = product(out_ref[...], join(dy_refs), 1, 1).astype(bf16).astype(f32)
+
+    def tile(at):
+        held = own * (at + 1)
+        for head in range(gkey_ref.shape[0]):
+            spot = slice(head * HD, (head + 1) * HD)
+            lifted = lifted_all[spot] * inv_ref[head : head + 1]
+            delta = jnp.sum(lifted * heads_ref[spot, :].astype(f32), axis=0, keepdims=True)
+            lifted_rows = lifted.T.astype(bf16)
+            soft = soft_ref[head, :held]
+            grad_soft = product(value_ref[head, :held], lifted.astype(bf16))
+            grad_scores = (soft.astype(f32) * (grad_soft - delta)).astype(bf16)
+            gvalue_ref[head, :held] += product(soft, lifted_rows)
+            gkey_ref[head, :held] += product(grad_scores, query_ref[head])
+            back = product(key_ref[spot, :held], grad_scores) * HD**-0.5
+            gquery_ref[spot, :] = jnp.concatenate(turn(back, cos_ref[...], -sin_ref[...]), axis=0)
+
+    for at in range(ranks):
+        pl.when(step == at)(functools.partial(tile, at))
+
+
+def rear_kernel(spot_ref, *refs, ranks, parts):
+    x_refs, refs = refs[:parts], refs[parts:]
+    gquery_ref, gkey_ref, gvalue_ref, cos_ref, sin_ref, scaled_ref, vec_ref, attn_ref = refs[:8]
+    mixed_ref, sums_ref, gbias_ref = refs[8:11]
     step = pl.program_id(0)
 
     @pl.when(step == 0)
     def _():
-        acc_ref[...] = jnp.zeros_like(acc_ref)
         sums_ref[...] = jnp.zeros_like(sums_ref)
         gbias_ref[...] = jnp.zeros_like(gbias_ref)
 
@@ -592,32 +597,36 @@
     mixed = jnp.concatenate(pieces, axis=0).T
     gbias_ref[0:1] += jnp.sum(mixed, axis=0, keepdims=True)
     low = mixed.astype(bf16)
+    mixed_ref[...] = low
     grad = product(low, attn_ref[:, : low.shape[1]], 1, 1)
-    hat = normalise(x_ref[...].astype(f32))
-    store_at(total_refs, step, (grad * vec_ref[0:1] + scaled_ref[...]).astype(bf16))
+    hat = normalise(join(x_refs).astype(f32))
+    total = (grad * vec_ref[0:1] + scaled_ref[...]).astype(bf16)
+    store_blocks(refs[11:], spot_ref, step, total, parts)
     sums_ref[0:1] += jnp.sum(grad * hat, axis=0, keepdims=True)
     sums_ref[1:2] += jnp.sum(grad, axis=0, keepdims=True)
-    acc_ref[...] += product(n1_ref[...], low, 0, 0)
-
-    @pl.when(step == pl.num_programs(0) - 1)
-    def _():
-        width, part3 = acc_ref.shape
-        cols, owners = part3 // 3, small_ref.shape[0]
-        share = width // owners
-        feed = feed_ref[...]
-        vectors = [sums_ref[0:1], sums_ref[1:2], feed[0:1], feed[1:2], feed[3:4], None]
-        vectors += [gbias_ref[0:1], feed[2:3]]
-        maps = vector_maps(spot_ref[0], share, ranks, cols, feed.shape[1], ratio)
-        table = jnp.zeros((owners, LANES), f32)
-        for vector, (per, base, index) in zip(vectors, maps):
-            if vector is not None:
-                rows, lanes = places(owners, per, base, index)
-                table += product(jnp.where(rows, vector, 0.0).astype(bf16), lanes, 1, 1)
-        small_ref[...] = jnp.zeros_like(small_ref)
-        for j in range(LANES // 128):
-            small_ref[:, j, :] = table[:, j * 128 : (j + 1) * 128]
-        small = small_ref[...].reshape(width, 128)
-        grads_ref[...] = jnp.concatenate([acc_ref[...], small], axis=1).astype(bf16)
+
+
+def weigh_kernel(
+    spot_ref, n1_ref, mixed_ref, sums_ref, gbias_ref, feed_ref, grads_ref, small_ref, *, ranks, ratio
+):
+    acc = product(n1_ref[...], mixed_ref[...], 0, 0)
+    width, part3 = acc.shape
+    cols, owners = part3 // 3, small_ref.shape[0]
+    share = width // owners
+    feed = feed_ref[...]
+    vectors = [sums_ref[0:1], sums_ref[1:2], feed[0:1], feed[1:2], feed[3:4], None]
+    vectors += [gbias_ref[0:1], feed[2:3]]
+    maps = vector_maps(spot_ref[0], share, ranks, cols, feed.shape[1], ratio)
+    table = jnp.zeros((owners, LANES), f32)
+    for vector, (per, base, index) in zip(vectors, maps):
+        if vector is not None:
+            rows, lanes = places(owners, per, base, index)
+            table += product(jnp.where(rows, vector, 0.0).astype(bf16), lanes, 1, 1)
+    small_ref[...] = jnp.zeros_like(small_ref)
+    for j in range(LANES // 128):
+        small_ref[:, j, :] = table[:, j * 128 : (j + 1) * 128]
+    small = small_ref[...].reshape(width, 128)
+    grads_ref[...] = jnp.concatenate([acc, small], axis=1).astype(bf16)
 
 
 def finish_kernel(
@@ -690,25 +699,22 @@
 
 def around(blocks, sign, ranks):
     order = sorted(range(1, ranks), key=lambda r: abs(ranks - 2 * r))
-    got = {r: shift(blocks[r - 1], sign * r, ranks) for r in order}
-    return [got[r] for r in range(1, ranks)]
+    got = {r: shift(blocks[r - 1], sign * r, ranks) for r in order if blocks[r - 1] is not None}
+    return [got.get(r) for r in range(1, ranks)]
 
 
 def swap(block, mask):
     return lax.ppermute(block, "dp", [(k, k ^ mask) for k in range(8)])
 
 
-def gather_dp(piece, by_x, by_y):
-    half = piece.shape[0] // 2
+def gather_dp(piece):
     place = lax.axis_index("dp")
-    three = jnp.stack([piece, by_x, by_y])
-    other = swap(three, 1)
-    corner = jnp.concatenate([swap(by_x[:half], 4), swap(by_y[half:], 2)])
-    far = swap(corner, 1)
+    by_x, by_y, by_both = swap(piece, 2), swap(piece, 4), swap(piece, 6)
+    near, beside, across = swap(piece, 1), swap(jnp.stack([by_x, by_y]), 1), swap(by_both, 1)
     whole = jnp.zeros((8,) + piece.shape, piece.dtype)
     for mask, part in (
-        (0, piece), (2, by_x), (4, by_y), (1, other[0]), (3, other[1]), (5, other[2]),
-        (6, corner), (7, far),
+        (0, piece), (1, near), (2, by_x), (4, by_y), (6, by_both),
+        (3, beside[0]), (5, beside[1]), (7, across),
     ):
         whole = lax.dynamic_update_slice(whole, part[None], (place ^ mask, 0, 0))
     return whole.reshape(8 * piece.shape[0], piece.shape[1])
@@ -751,9 +757,16 @@
     mixed_cols = 3 * cols
     edge = hidden + width + mixed_cols
 
+    x_own = hidden_in.reshape(own, width)
+    dy_own = grad_out.reshape(own, width)
+
     small = [attn_gain, attn_shift, feed_gain, feed_shift, out_bias, down_bias, qkv_bias, up_bias]
     shape = jax.ShapeDtypeStruct
-    spot = jnp.stack([rank, lax.axis_index("dp")])
+    blocks = stretch_order.shape[0]
+    slots = jnp.arange(blocks, dtype=jnp.int32)
+    lies = jnp.sum(jnp.where(stretch_order[None] == slots[:, None], slots[None], 0), axis=1)
+    lies = (rank - lies // blocks_own) % ranks * blocks_own + lies % blocks_own
+    spot = jnp.concatenate([jnp.stack([rank, lax.axis_index("dp")]), lies])
     sent = (share, hidden + mixed_cols + 128)
     *packed, out_piece = call(
         functools.partial(pack_kernel, vectors=len(small), held=ratio * share),
@@ -769,6 +782,8 @@
         [(k, (k % groups) * ranks + k // groups) for k in range(spread)],
     )
     landed = packed[:1] + around(packed[1:], 1, ranks)
+    x_next = shift(x_own, 1, ranks)
+    landed[0] = after(landed[0], x_next)
     total_cols = edge + cols + 128
     (weight_piece,) = call(
         functools.partial(land_kernel, hidden=hidden),
@@ -776,73 +791,71 @@
         [(spot, SMEM)] + [(a, whole_block(a.shape)) for a in (*landed, down_weight, out_piece)],
         [(shape((piece, total_cols), bf16), whole_block((piece, total_cols)))],
     )
-    by_x, by_y = swap(weight_piece, 2), swap(weight_piece, 4)
-    weights = gather_dp(weight_piece, by_x, by_y)
-
-    x_own = hidden_in.reshape(own, width)
-    dy_own = grad_out.reshape(own, width)
+    weights = gather_dp(weight_piece)
+
     x_go = after(x_own, *landed)
-    x_near = after(x_own, by_x, by_y)
-    x_sent = [x_go] * (ranks - 2) + [x_near]
-    x_all = jnp.concatenate([x_own] + around(x_sent, 1, ranks))
-    dy_go = after(dy_own, x_all, weights)
-    dy_all = jnp.concatenate([dy_own] + around([dy_go] * (ranks - 1), 1, ranks))
-
-    owners = (rank - jnp.arange(ranks, dtype=jnp.int32)) % ranks
-    blocks = stretch_order.reshape(ranks, blocks_own)[owners].reshape(-1)
-    place = (blocks[:, None] * half + jnp.arange(half, dtype=jnp.int32)[None]).reshape(count)
+    x_rest = around([None] + [x_go] * (ranks - 2), 1, ranks)[1:]
+    x_all = jnp.concatenate([x_own, x_next] + x_rest)
+    dy_go = after(dy_own, x_all)
+    dy_got = around([dy_go] * (ranks - 1), 1, ranks)
+
     ends = jnp.cumsum(doc_lengths[0])[:-1]
-    first = jnp.max(jnp.where(place[:, None] >= ends[None], ends[None], 0), axis=1)
-    span = jnp.concatenate([place[None], first[None], jnp.zeros((6, count), jnp.int32)])
+    place = jnp.arange(count, dtype=jnp.int32)
+    first_of = jnp.max(jnp.where(place[:, None] >= ends[None], ends[None], 0), axis=1)
+    start = jnp.broadcast_to(first_of[None], (8, count))
     angle = frequencies()[:, None] * place.astype(f32)[None]
     cosine, sine = jnp.cos(angle), jnp.sin(angle)
 
     tile = lambda w: pl.BlockSpec((own, w), lambda t, *_: (t, 0))
     upright_tile = lambda n: pl.BlockSpec((n, own), lambda t, *_: (0, t))
+    upright_all = lambda j: pl.BlockSpec((cols, count), lambda *_: (j, 0))
     column = lambda j: pl.BlockSpec((width, width), lambda *_: (0, j))
     angles = [(cosine, upright_tile(ROT // 2)), (sine, upright_tile(ROT // 2))]
+    by_place = [
+        pl.BlockSpec((half, width), lambda t, spot, k=k: (spot[2 + t * blocks_own + k], 0))
+        for k in range(blocks_own)
+    ]
+    in_order = lambda array: [(array, spec) for spec in by_place]
+    each = [(shape((own, width), bf16), whole_block((own, width)))] * ranks
 
     n1, n2, active, slope, fed, upright, rows, vec, out_own = call(
-        functools.partial(front_kernel, ranks=ranks, ratio=ratio),
+        functools.partial(front_kernel, ranks=ranks, ratio=ratio, parts=blocks_own),
         (ranks,),
-        [(spot, SMEM), (x_all, tile(width)),
-         (weights, pl.BlockSpec((width, 128), lambda t: (0, (edge + cols) // 128)))] + angles
+        in_order(x_all)
+        + [(weights, pl.BlockSpec((width, 128), lambda *_: (0, (edge + cols) // 128)))] + angles
         + [(weights, column(0)), (weights, column(1)), (weights, column(2))],
         [(shape((count, width), bf16), tile(width)), (shape((count, width), bf16), tile(width)),
          (shape((count, hidden), bf16), tile(hidden)), (shape((count, hidden), bf16), tile(hidden)),
          (shape((count, width), f32), tile(width)),
          (shape((mixed_cols, count), bf16), upright_tile(mixed_cols)),
          (shape((3 * heads, count, HD), bf16),
-          pl.BlockSpec((3 * heads, own, HD), lambda t: (0, t, 0))),
+          pl.BlockSpec((3 * heads, own, HD), lambda t, *_: (0, t, 0))),
          (shape((8, width), f32), whole_block((8, width))),
          (shape((cols, width), bf16), whole_block((cols, width)))],
         [pltpu.VMEM((1, mixed_cols), f32)],
         cost=10,
+        first=(spot,),
     )
 
     all_heads = lambda j: pl.BlockSpec((heads, count, HD), lambda *_: (j, 0, 0))
-    soft_spec = pl.BlockSpec((1, count, own), lambda t, h, *_: (h, 0, t))
-    inv_spec = pl.BlockSpec((1, 8, own), lambda t, h, *_: (h, 0, t))
+    soft_spec = pl.BlockSpec((heads, count, own), lambda t, *_: (0, 0, t))
     soft, inverse, heads_low, *part_out = call(
-        attend_kernel,
-        (ranks, heads),
-        [(span, upright_tile(8)), (place[:, None], whole_block((count, 1))),
-         (rows, all_heads(1)), (upright, pl.BlockSpec((HD, own), lambda t, h, *_: (h, t))),
-         (upright, pl.BlockSpec((HD, count), lambda t, h, *_: (2 * heads + h, 0))),
-         (fed, tile(width)), (out_own, whole_block((cols, width)))],
-        [(shape((heads, count, count), bf16), soft_spec),
-         (shape((heads, 8, count), f32), inv_spec),
-         (shape((cols, count), bf16), upright_tile(cols))]
-        + [(shape((own, width), bf16), whole_block((own, width)))] * ranks,
-        [pltpu.VMEM((count, own), f32)],
-        cost=16,
-    )
-
-    dy_all = after(dy_all, heads_low)
+        functools.partial(attend_kernel, ranks=ranks, parts=blocks_own),
+        (ranks,),
+        [(start, upright_tile(8)), (rows, all_heads(1)), (upright, upright_tile(cols)),
+         (upright, upright_all(2)), (fed, tile(width)), (out_own, whole_block((cols, width)))],
+        [(shape((heads, count, count), bf16), soft_spec), (shape((8, count), f32), upright_tile(8)),
+         (shape((cols, count), bf16), upright_tile(cols))] + each,
+        cost=10,
+        first=(spot,),
+    )
+
+    dy_all = jnp.concatenate([dy_own] + [after(block, heads_low) for block in dy_got])
     scaled, grads_feed, feed_sums = call(
-        functools.partial(feed_back_kernel, ranks=ranks),
+        functools.partial(feed_back_kernel, ranks=ranks, parts=blocks_own),
         (ranks,),
-        [(dy_all, tile(width)), (x_all, tile(width)), (active, tile(hidden)),
+        in_order(dy_all) + in_order(x_all)
+        + [(dy_own, whole_block((own, width))), (active, tile(hidden)),
          (slope, tile(hidden)), (n2, tile(width)), (vec, whole_block((8, width))),
          (weights, column(0)), (weights, column(1)), (heads_low, upright_tile(cols))],
         [(shape((count, width), f32), tile(width)),
@@ -852,54 +865,64 @@
         [pltpu.VMEM((width, hidden), f32), pltpu.VMEM((hidden, width), f32),
          pltpu.VMEM((cols, width), f32)],
         cost=12,
+        first=(spot,),
     )
     feed_part = scatter_dp(grads_feed)
 
     far = [r for r in range(1, ranks) if 2 * r == ranks]
     near = [r for r in range(1, ranks) if r not in far]
-    out_parts = part_out[:1] + [shift(part_out[r], -r, ranks) for r in near]
+    out_parts = part_out[:1] + [shift(after(part_out[r], dy_all), -r, ranks) for r in near]
     heads_low = after(heads_low, scaled, *out_parts)
     far_parts = [shift(after(part_out[r], scaled), -r, ranks) for r in far]
+    head_tile = pl.BlockSpec((heads, own, HD), lambda t, *_: (0, t, 0))
     gquery, gkey, gvalue = call(
-        attend_back_kernel,
-        (ranks, heads),
-        [(dy_all, tile(width)), (out_own, whole_block((cols, width))),
-         (heads_low, upright_tile(cols)), (inverse, inv_spec), (soft, soft_spec),
-         (rows, all_heads(2)), (upright, pl.BlockSpec((HD, count), lambda t, h: (heads + h, 0))),
-         (rows, pl.BlockSpec((1, own, HD), lambda t, h: (h, t, 0)))] + angles,
+        functools.partial(attend_back_kernel, ranks=ranks, parts=blocks_own),
+        (ranks,),
+        in_order(dy_all)
+        + [(out_own, whole_block((cols, width))), (heads_low, upright_tile(cols)),
+           (inverse, upright_tile(8)), (soft, soft_spec), (rows, all_heads(2)),
+           (upright, upright_all(1)), (rows, head_tile)] + angles,
         [(shape((cols, count), f32), upright_tile(cols)),
          (shape((heads, count, HD), f32), whole_block((heads, count, HD))),
          (shape((heads, count, HD), f32), whole_block((heads, count, HD)))],
-        [pltpu.VMEM((cols, own), f32)],
-        cost=16,
+        cost=10,
+        first=(spot,),
     )
     gquery = after(gquery, *far_parts)
     out_sum = sum(part.astype(f32) for part in out_parts + far_parts)
     hidden_out = (x_own.astype(f32) + vec[5:6] + out_sum).astype(bf16)
 
-    head_tile = pl.BlockSpec((heads, own, HD), lambda t: (0, t, 0))
-    *total, grads_attn = call(
-        functools.partial(rear_kernel, ranks=ranks, ratio=ratio),
+    mixed, attn_sums, attn_bias, *total = call(
+        functools.partial(rear_kernel, ranks=ranks, parts=blocks_own),
         (ranks,),
-        [(spot, SMEM), (gquery, upright_tile(cols)), (gkey, head_tile), (gvalue, head_tile)]
+        in_order(x_all) + [(gquery, upright_tile(cols)), (gkey, head_tile), (gvalue, head_tile)]
         + angles
-        + [(n1, tile(width)), (x_all, tile(width)), (scaled, tile(width)),
-           (vec, whole_block((8, width))), (weights, column(2)),
-           (feed_sums, whole_block((8, width)))],
-        [(shape((own, width), bf16), whole_block((own, width)))] * ranks
-        + [(shape((width, mixed_cols + 128), bf16), whole_block((width, mixed_cols + 128)))],
-        [pltpu.VMEM((width, mixed_cols), f32), pltpu.VMEM((8, width), f32),
-         pltpu.VMEM((8, mixed_cols), f32), pltpu.VMEM((spread, share, 128), f32)],
-        cost=11,
-    )
-
-    dy = dy_own.astype(f32)
+        + [(scaled, tile(width)), (vec, whole_block((8, width))), (weights, column(2))],
+        [(shape((count, mixed_cols), bf16), tile(mixed_cols)),
+         (shape((8, width), f32), whole_block((8, width))),
+         (shape((8, mixed_cols), f32), whole_block((8, mixed_cols)))] + each,
+        cost=8,
+        first=(spot,),
+    )
+    (grads_attn,) = call(
+        functools.partial(weigh_kernel, ranks=ranks, ratio=ratio),
+        (1,),
+        [(a, whole_block(a.shape)) for a in (n1, mixed, attn_sums, attn_bias, feed_sums)],
+        [(shape((width, mixed_cols + 128), bf16), whole_block((width, mixed_cols + 128)))],
+        [pltpu.VMEM((spread, share, 128), f32)],
+        cost=5,
+        first=(spot,),
+    )
+
     grad_parts = total[:1] + around(total[1:], -1, ranks)
     attn_part = scatter_dp(after(grads_attn, feed_part))
+    home = [((k % groups) * ranks + k // groups, k) for k in range(spread)]
+    proj_part = lax.ppermute(feed_part[:, hidden + width :], ("dp", "seq"), home)
     parts = jnp.concatenate([feed_part[:, :hidden], attn_part], axis=1)
     parts = parts.reshape(ranks, share, parts.shape[1])
     parts = [lax.dynamic_index_in_dim(parts, (rank + r) % ranks, 0, False) for r in range(ranks)]
-    parts = parts[:1] + around([after(p, *grad_parts) for p in parts[1:]], 1, ranks)
+    parts = parts[:1] + around([after(p, proj_part, *grad_parts) for p in parts[1:]], 1, ranks)
+    dy = dy_own.astype(f32)
     grad = sum(part.astype(f32) for part in grad_parts)
     rows_own = x_own.astype(f32)
     centred = rows_own - jnp.mean(rows_own, axis=-1, keepdims=True)
@@ -912,8 +935,6 @@
     )
 
     factor = 1.0 / math.sqrt(count * groups)
-    home = [((k % groups) * ranks + k // groups, k) for k in range(spread)]
-    proj_part = lax.ppermute(feed_part[:, hidden + width :], ("dp", "seq"), home)
     down_part = feed_part[:, hidden : hidden + width]
     results = [(share, 3 * width), (share, ranks * hidden), (share, width), (piece, width)]
     results += [(share,)] * 5 + [(3 * share,), (ratio * share,)]

time: 218 us -> 212 us (0.972)
  waiting for transfers between devices: 60.4 us -> 54.8 us
  Pallas kernels: 74.8 us -> 70.6 us
    ppermute x6, waiting for transfers between devices: 13.4 us -> 2.76 us  [swap(): return lax.ppermute(block, 'dp', [(k, k ^ mask) for k in range(8)])]
    ppermute x18, waiting for transfers between devices: 47 us -> 52 us  [shift(): lax.ppermute(block, 'seq', [(k, (k + amount) % ranks) for k in range(rank...]
    pallas_call x8 -> x9, Pallas kernels: 74.8 us -> 70.6 us  [call(): pl.pallas_call(kernel, grid_spec=pltpu.PrefetchScalarGridSpec(num_scalar_...]
    unnamed x34 -> x37, local copies, waits for them, and re-layouts: 2.5 us -> 4.99 us
    ppermute x18, starting transfers between devices: 41.7 us -> 44.1 us  [shift(): lax.ppermute(block, 'seq', [(k, (k + amount) % ranks) for k in range(rank...]
where the time goes in v3:
time: 212 us; the launch traced here: 211 us
  Pallas kernels  70.6 us (33%)
  starting transfers between devices  62.9 us (30%)
  waiting for transfers between devices  54.8 us (26%)
  other arithmetic  12.4 us (6%)
  local copies, waits for them, and re-layouts  9 us (4%)
    pallas_call x9, Pallas kernels, call(): pl.pallas_call(kernel, grid_spec=pltpu.PrefetchScalarGridSpec(num_scalar_...  70.6 us
    ppermute x18, waiting for transfers between devices, shift(): lax.ppermute(block, 'seq', [(k, (k + amount) % ranks) for k in range(rank...  52 us
    ppermute x18, starting transfers between devices, shift(): lax.ppermute(block, 'seq', [(k, (k + amount) % ranks) for k in range(rank...  44.1 us
    all_to_all x2, starting transfers between devices, scatter_dp(): lax.all_to_all(parts.reshape(8, -1, parts.shape[1]), 'dp', 0, 0, tiled=True)  7.65 us
    ppermute x6, starting transfers between devices, swap(): return lax.ppermute(block, 'dp', [(k, k ^ mask) for k in range(8)])  7.56 us
    unnamed x37, local copies, waits for them, and re-layouts  4.99 us
  transfers between devices with their start and end apart: 28, of which 10 were waited for; matrix products, arithmetic and copies ran while one was open for 7% of the time, Pallas kernels for 32%

profile of v3, /device:TPU:0, one launch (start us, length us, event | category | flops | bytes accessed | tf_op | source)
XLA Modules:
  0.0 210.7 jit_solution(10455159184509674971)
XLA Ops:
  0.7 3.1 %collective-permute-start = (bf16[256,768]{1,0:T(8,128)(2,1)}, bf16[256,768]{1,0:T(8,128)(2,1)S(1)}, u32[]{:S(2)}, u32[]{:S(2)}) collective-permute-start(bf16[256,768]{1,0:T(8,128)(2,1)} %bitcast.41), channel_id=1, source_target_pairs={{0,1},{1,2},{2,3},{3,0},{4,5},{5,6},{6,7},{7,4},{8,9},{9,10},{10,1... | collective-permute-start | bytes 1179656 | tf_op jit(solution)/shard_map/ppermute | solution.py:697
  5.2 2.2 %shard_map.263 = (bf16[24,1472]{1,0:T(8,128)(2,1)}, bf16[24,1472]{1,0:T(8,128)(2,1)}, bf16[24,1472]{1,0:T(8,128)(2,1)}, bf16[24,1472]{1,0:T(8,128)(2,1)}, bf16[96,192]{1,0:T(8,128)(2,1)}) custom-call(s32[10]{0:T(128)} %pad_add_fusion.rank_ref.spot_ref, bf16[24,3072]{1,0:T(8,128)(2,1)} %up_ref.1, bf16[24,2304]{1,0:T(8,128)(2,1)} %qkv_ref.1, ...), custom_call_target="tpu_custom_call" | custom-call | flops 1000000000 | tf_op jit(solution)/shard_map/pallas_call | solution.py:677
  10.0 2.9 %collective-permute-start.3 = (bf16[24,1472]{1,0:T(8,128)(2,1)}, bf16[24,1472]{1,0:T(8,128)(2,1)S(1)}, u32[]{:S(2)}, u32[]{:S(2)}) collective-permute-start(bf16[24,1472]{1,0:T(8,128)(2,1)} %get-tuple-element.78), channel_id=1, source_target_pairs={{0,3},{1,0},{2,1},{3,2},{4,7},{5,4},{6,5},{7,6},{8,11},{9,8},{10,9... | collective-permute-start | bytes 211976 | tf_op jit(solution)/shard_map/ppermute | solution.py:697
  17.6 2.4 %collective-permute-done.2.refs_2_ = bf16[24,1472]{1,0:T(8,128)(2,1)S(1)} collective-permute-done((bf16[24,1472]{1,0:T(8,128)(2,1)}, bf16[24,1472]{1,0:T(8,128)(2,1)S(1)}, u32[]{:S(2)}, u32[]{:S(2)}) %collective-permute-start.2) | collective-permute-done | bytes 70688 | tf_op jit(solution)/shard_map/ppermute | solution.py:697
  25.1 3.3 %collective-permute-start.8 = (bf16[96,2432]{1,0:T(8,128)(2,1)}, bf16[96,2432]{1,0:T(8,128)(2,1)S(1)}, u32[]{:S(2)}, u32[]{:S(2)}) collective-permute-start(bf16[96,2432]{1,0:T(8,128)(2,1)} %shard_map.264), channel_id=1, source_target_pairs={{0,8},{4,12},{8,0},{12,4},{16,24},{20,28},{24,16},{28,20},{1,9},{5... | collective-permute-start | bytes 1400840 | tf_op jit(solution)/shard_map/ppermute | solution.py:707
  29.8 3.0 %collective-permute-start.5 = (bf16[256,768]{1,0:T(8,128)(2,1)S(1)}, bf16[256,768]{1,0:T(8,128)(2,1)S(1)}, u32[]{:S(2)}, u32[]{:S(2)}) collective-permute-start(bf16[256,768]{1,0:T(8,128)(2,1)S(1)} %bitcast.43), channel_id=1, source_target_pairs={{0,3},{1,0},{2,1},{3,2},{4,7},{5,4},{6,5},{7,6},{8,11},{9,8},{10,9... | collective-permute-start | bytes 1179656 | tf_op jit(solution)/shard_map/ppermute | solution.py:697
  33.1 17.1 %collective-permute-done.4 = bf16[256,768]{1,0:T(8,128)(2,1)S(1)} collective-permute-done((bf16[256,768]{1,0:T(8,128)(2,1)S(1)}, bf16[256,768]{1,0:T(8,128)(2,1)S(1)}, u32[]{:S(2)}, u32[]{:S(2)}) %collective-permute-start.4) | collective-permute-done | bytes 393248 | tf_op jit(solution)/shard_map/ppermute | solution.py:697
  52.3 8.0 %collective-permute-start.13 = (bf16[256,768]{1,0:T(8,128)(2,1)S(1)}, bf16[256,768]{1,0:T(8,128)(2,1)S(1)}, u32[]{:S(2)}, u32[]{:S(2)}) collective-permute-start(bf16[256,768]{1,0:T(8,128)(2,1)S(1)} %bitcast.56), channel_id=1, source_target_pairs={{0,1},{1,2},{2,3},{3,0},{4,5},{5,6},{6,7},{7,4},{8,9},{9,10},{10,1... | collective-permute-start | bytes 1179656 | tf_op jit(solution)/shard_map/ppermute | solution.py:697
  60.3 2.6 %collective-permute-start.14 = (bf16[256,768]{1,0:T(8,128)(2,1)S(1)}, bf16[256,768]{1,0:T(8,128)(2,1)S(1)}, u32[]{:S(2)}, u32[]{:S(2)}) collective-permute-start(bf16[256,768]{1,0:T(8,128)(2,1)S(1)} %bitcast.57), channel_id=1, source_target_pairs={{0,2},{1,3},{2,0},{3,1},{4,6},{5,7},{6,4},{7,5},{8,10},{9,11},{10,... | collective-permute-start | bytes 1179656 | tf_op jit(solution)/shard_map/ppermute | solution.py:697
  68.1 12.3 %shard_map.265 = (bf16[1024,768]{1,0:T(8,128)(2,1)}, bf16[1024,768]{1,0:T(8,128)(2,1)}, bf16[1024,768]{1,0:T(8,128)(2,1)}, bf16[1024,768]{1,0:T(8,128)(2,1)}, f3...) custom-call(s32[10]{0:T(128)} %pad_add_fusion.rank_ref.spot_ref, ...), custom_call_target="tpu_custom_call" | custom-call | flops 10000000000 | tf_op jit(solution)/shard_map/pallas_call | solution.py:677
  81.1 12.1 %shard_map.266 = (bf16[3,1024,1024]{2,1,0:T(8,128)(2,1)}, f32[8,1024]{1,0:T(8,128)}, bf16[192,1024]{1,0:T(8,128)(2,1)}, bf16[256,768]{1,0:T(8,128)(2,1)}, bf16[2...) custom-call(s32[10]{0:T(128)} %pad_add_fusion.rank_ref.spot_ref, ...), custom_call_target="tpu_custom_call" | custom-call | flops 10000000000 | tf_op jit(solution)/shard_map/pallas_call | solution.py:677
  94.6 5.9 %collective-permute-start.17 = (bf16[256,768]{1,0:T(8,128)(2,1)}, bf16[256,768]{1,0:T(8,128)(2,1)S(1)}, u32[]{:S(2)}, u32[]{:S(2)}) collective-permute-start(bf16[256,768]{1,0:T(8,128)(2,1)} %get-tuple-element.95), channel_id=1, source_target_pairs={{0,1},{1,2},{2,3},{3,0},{4,5},{5,6},{6,7},{7,4},{8,9},{9,10},{10,1... | collective-permute-start | bytes 1179656 | tf_op jit(solution)/shard_map/ppermute | solution.py:697
  100.5 2.8 %collective-permute-start.16 = (bf16[256,768]{1,0:T(8,128)(2,1)}, bf16[256,768]{1,0:T(8,128)(2,1)}, u32[]{:S(2)}, u32[]{:S(2)}) collective-permute-start(bf16[256,768]{1,0:T(8,128)(2,1)} %get-tuple-element.93), channel_id=1, source_target_pairs={{0,3},{1,0},{2,1},{3,2},{4,7},{5,4},{6,5},{7,6},{8,11},{9,8},{10,9... | collective-permute-start | bytes 1179656 | tf_op jit(solution)/shard_map/ppermute | solution.py:697
  103.3 13.0 %shard_map.267 = (f32[1024,768]{1,0:T(8,128)}, bf16[768,1728]{1,0:T(8,128)(2,1)}, f32[8,768]{1,0:T(8,128)}) custom-call(s32[10]{0:T(128)} %pad_add_fusion.rank_ref.spot_ref, bf16[1024,768]{1,0:T(8,128)(2,1)} %pad_maximum_fusion.1.refs_0_.refs_1_, bf16[1024,768]{1,0:T(8,128)(2,1)} %pad_maximum_fusion.1.refs_0_.refs_1_, ...), custom_call_target="tpu_custom_call" | custom-call | flops 12000000000 | tf_op jit(solution)/shard_map/pallas_call | solution.py:677
  116.3 3.6 %all-to-all-start = ((bf16[8,96,1728]{2,1,0:T(8,128)(2,1)}), bf16[8,96,1728]{2,1,0:T(8,128)(2,1)S(1)}, u32[]{:S(2)}, u32[]{:S(2)}) async-start(bf16[8,96,1728]{2,1,0:T(8,128)(2,1)} %bitcast.52), calls=%async_computation | async-start | bytes 5505024 | tf_op jit(solution)/shard_map/all_to_all | solution.py:724
  120.9 11.3 %shard_map.268 = (f32[192,1024]{1,0:T(8,128)}, f32[3,1024,64]{2,1,0:T(8,128)}, f32[3,1024,64]{2,1,0:T(8,128)}) custom-call(s32[10]{0:T(128)} %pad_add_fusion.rank_ref.spot_ref, bf16[1024,768]{1,0:T(8,128)(2,1)} %pad_maximum_fusion.1.refs_0_.refs_1_, bf16[1024,768]{1,0:T(8,128)(2,1)} %pad_maximum_fusion.1.refs_0_.refs_1_, ...), custom_call_target="tpu_custom_call" | custom-call | flops 10000000000 | tf_op jit(solution)/shard_map/pallas_call | solution.py:677
  132.2 8.4 %collective-permute-done.18 = bf16[256,768]{1,0:T(8,128)(2,1)S(1)} collective-permute-done((bf16[256,768]{1,0:T(8,128)(2,1)}, bf16[256,768]{1,0:T(8,128)(2,1)S(1)}, u32[]{:S(2)}, u32[]{:S(2)}) %collective-permute-start.18) | collective-permute-done | bytes 393248 | tf_op jit(solution)/shard_map/ppermute | solution.py:697
  140.6 9.4 %shard_map.269 = (bf16[1024,576]{1,0:T(8,128)(2,1)}, f32[8,768]{1,0:T(8,128)}, f32[8,576]{1,0:T(8,128)}, bf16[256,768]{1,0:T(8,128)(2,1)}, bf16[256,768]{1,0:T(8...) custom-call(s32[10]{0:T(128)} %pad_add_fusion.rank_ref.spot_ref, ...), custom_call_target="tpu_custom_call" | custom-call | flops 8000000000 | tf_op jit(solution)/shard_map/pallas_call | solution.py:677
  152.8 6.1 %shard_map.270 = bf16[768,704]{1,0:T(8,128)(2,1)} custom-call(s32[10]{0:T(128)} %pad_add_fusion.rank_ref.spot_ref, bf16[1024,768]{1,0:T(8,128)(2,1)} %get-tuple-element.114.n1_ref, bf16[1024,576]{1,0:T(8,128)(2,1)} %get-tuple-element.115.mixed_ref, f32[8,768]{1,0:T(8,128)} %get-tuple-element.116.sums_ref, f32[8,576]{1,0:T(8,128)} %get-tuple-element.117.gbias_ref, ...), custom_call_target="tpu_custom_call" | custom-call | flops 5000000000 | tf_op jit(solution)/shard_map/pallas_call | solution.py:677
  160.1 4.0 %all-to-all-start.1 = ((bf16[8,96,704]{2,1,0:T(8,128)(2,1)}), bf16[8,96,704]{2,1,0:T(8,128)(2,1)S(1)}, u32[]{:S(2)}, u32[]{:S(2)}) async-start(bf16[8,96,704]{2,1,0:T(8,128)(2,1)} %bitcast.60), calls=%async_computation.1 | async-start | bytes 2359296 | tf_op jit(solution)/shard_map/all_to_all | solution.py:724
  165.0 20.6 %collective-permute-done.20 = bf16[256,768]{1,0:T(8,128)(2,1)} collective-permute-done((bf16[256,768]{1,0:T(8,128)(2,1)}, bf16[256,768]{1,0:T(8,128)(2,1)}, u32[]{:S(2)}, u32[]{:S(2)}) %collective-permute-start.20) | collective-permute-done | bytes 393248 | tf_op jit(solution)/shard_map/ppermute | solution.py:697
  192.1 6.2 %collective-permute-start.25 = (bf16[24,1472]{1,0:T(8,128)(2,1)S(1)}, bf16[24,1472]{1,0:T(8,128)(2,1)S(1)}, u32[]{:S(2)}, u32[]{:S(2)}) collective-permute-start(bf16[24,1472]{1,0:T(8,128)(2,1)S(1)} %get-tuple-element.122), channel_id=1, source_target_pairs={{0,3},{1,0},{2,1},{3,2},{4,7},{5,4},{6,5},{7,6},{8,11},{9,8},{10,9... | collective-permute-start | bytes 211976 | tf_op jit(solution)/shard_map/ppermute | solution.py:697
  202.0 3.1 %fusion.9 = (bf16[256,768]{1,0:T(8,128)(2,1)}, bf16[256,768]{1,0:T(8,128)(2,1)}) fusion(f32[256]{0:T(256)S(1)} %get-tuple-element.148, f32[256]{0:T(256)S(1)} %get-tuple-element.146, f32[256]{0:T(256)} %get-tuple-element.149, f32[256]{0:T(256)S(1)} %rsqrt_bitcast_fusion, bf16[1,2,128,768]{3,2,1,0:T(8,128)(2,1)S(1)} %copy-done.3, ...), kind=kLoop, calls=%fused_computation.16 | loop fusion | flops 5308416 | bytes 4725760 | tf_op jit(solution)/shard_map/convert_element_type | solution.py:949
  207.3 2.2 %shard_map.271 = (f32[24,2304]{1,0:T(8,128)}, f32[24,3072]{1,0:T(8,128)}, f32[24,768]{1,0:T(8,128)}, f32[96,768]{1,0:T(8,128)}, f32[24]{0:T(128)}, /*index=5*/f3...) custom-call(s32[10]{0:T(128)} %pad_add_fusion.rank_ref.spot_ref, ...), custom_call_target="tpu_custom_call" | custom-call | flops 1000000000 | tf_op jit(solution)/shard_map/pallas_call | solution.py:677
  (114 shorter events, 44.2 us)
Async XLA Ops:
  0.7 15.4 %collective-permute-start = (bf16[256,768]{1,0:T(8,128)(2,1)}, bf16[256,768]{1,0:T(8,128)(2,1)S(1)}, u32[]{:S(2)}, u32[]{:S(2)}) collective-permute-start(bf16[256,768]{1,0:T(8,128)(2,1)} %bitcast.41), channel_id=1, source_target_pairs={{0,1},{1,2},{2,3},{3,0},{4,5},{5,6},{6,7},{7,4},{8,9},{9,10},{10,1... | collective-permute-start | bytes 1179656 | tf_op jit(solution)/shard_map/ppermute | solution.py:697
  7.4 10.2 %collective-permute-start.1 = (bf16[24,1472]{1,0:T(8,128)(2,1)}, bf16[24,1472]{1,0:T(8,128)(2,1)S(1)}, u32[]{:S(2)}, u32[]{:S(2)}) collective-permute-start(bf16[24,1472]{1,0:T(8,128)(2,1)} %get-tuple-element.76), channel_id=1, source_target_pairs={{0,1},{1,2},{2,3},{3,0},{4,5},{5,6},{6,7},{7,4},{8,9},{9,10},{10,1... | collective-permute-start | bytes 211976 | tf_op jit(solution)/shard_map/ppermute | solution.py:697
  9.0 11.0 %collective-permute-start.2 = (bf16[24,1472]{1,0:T(8,128)(2,1)}, bf16[24,1472]{1,0:T(8,128)(2,1)S(1)}, u32[]{:S(2)}, u32[]{:S(2)}) collective-permute-start(bf16[24,1472]{1,0:T(8,128)(2,1)} %get-tuple-element.77), channel_id=1, source_target_pairs={{0,2},{1,3},{2,0},{3,1},{4,6},{5,7},{6,4},{7,5},{8,10},{9,11},{10,... | collective-permute-start | bytes 211976 | tf_op jit(solution)/shard_map/ppermute | solution.py:697
  10.0 9.9 %collective-permute-start.3 = (bf16[24,1472]{1,0:T(8,128)(2,1)}, bf16[24,1472]{1,0:T(8,128)(2,1)S(1)}, u32[]{:S(2)}, u32[]{:S(2)}) collective-permute-start(bf16[24,1472]{1,0:T(8,128)(2,1)} %get-tuple-element.78), channel_id=1, source_target_pairs={{0,3},{1,0},{2,1},{3,2},{4,7},{5,4},{6,5},{7,6},{8,11},{9,8},{10,9... | collective-permute-start | bytes 211976 | tf_op jit(solution)/shard_map/ppermute | solution.py:697
  23.2 39.7 %collective-permute-start.7 = (bf16[96,2432]{1,0:T(8,128)(2,1)}, bf16[96,2432]{1,0:T(8,128)(2,1)S(1)}, u32[]{:S(2)}, u32[]{:S(2)}) collective-permute-start(bf16[96,2432]{1,0:T(8,128)(2,1)} %shard_map.264), channel_id=1, source_target_pairs={{0,4},{4,0},{8,12},{12,8},{16,20},{20,16},{24,28},{28,24},{1,5},{5... | collective-permute-start | bytes 1400840 | tf_op jit(solution)/shard_map/ppermute | solution.py:707
  25.1 35.2 %collective-permute-start.8 = (bf16[96,2432]{1,0:T(8,128)(2,1)}, bf16[96,2432]{1,0:T(8,128)(2,1)S(1)}, u32[]{:S(2)}, u32[]{:S(2)}) collective-permute-start(bf16[96,2432]{1,0:T(8,128)(2,1)} %shard_map.264), channel_id=1, source_target_pairs={{0,8},{4,12},{8,0},{12,4},{16,24},{20,28},{24,16},{28,20},{1,9},{5... | collective-permute-start | bytes 1400840 | tf_op jit(solution)/shard_map/ppermute | solution.py:707
  28.4 34.5 %collective-permute-start.9 = (bf16[96,2432]{1,0:T(8,128)(2,1)}, bf16[96,2432]{1,0:T(8,128)(2,1)S(1)}, u32[]{:S(2)}, u32[]{:S(2)}) collective-permute-start(bf16[96,2432]{1,0:T(8,128)(2,1)} %shard_map.264), channel_id=1, source_target_pairs={{0,16},{4,20},{8,24},{12,28},{16,0},{20,4},{24,8},{28,12},{1,17},{... | collective-permute-start | bytes 1400840 | tf_op jit(solution)/shard_map/ppermute | solution.py:707
  29.8 20.3 %collective-permute-start.4 = (bf16[256,768]{1,0:T(8,128)(2,1)S(1)}, bf16[256,768]{1,0:T(8,128)(2,1)S(1)}, u32[]{:S(2)}, u32[]{:S(2)}) collective-permute-start(bf16[256,768]{1,0:T(8,128)(2,1)S(1)} %bitcast.42), channel_id=1, source_target_pairs={{0,2},{1,3},{2,0},{3,1},{4,6},{5,7},{6,4},{7,5},{8,10},{9,11},{10,... | collective-permute-start | bytes 1179656 | tf_op jit(solution)/shard_map/ppermute | solution.py:697
  29.8 21.2 %collective-permute-start.5 = (bf16[256,768]{1,0:T(8,128)(2,1)S(1)}, bf16[256,768]{1,0:T(8,128)(2,1)S(1)}, u32[]{:S(2)}, u32[]{:S(2)}) collective-permute-start(bf16[256,768]{1,0:T(8,128)(2,1)S(1)} %bitcast.43), channel_id=1, source_target_pairs={{0,3},{1,0},{2,1},{3,2},{4,7},{5,4},{6,5},{7,6},{8,11},{9,8},{10,9... | collective-permute-start | bytes 1179656 | tf_op jit(solution)/shard_map/ppermute | solution.py:697
  50.1 13.4 %collective-permute-start.10 = (bf16[96,2432]{1,0:T(8,128)(2,1)S(1)}, bf16[96,2432]{1,0:T(8,128)(2,1)S(1)}, u32[]{:S(2)}, u32[]{:S(2)}) collective-permute-start(bf16[96,2432]{1,0:T(8,128)(2,1)S(1)} %copy-done.6), channel_id=1, source_target_pairs={{0,24},{4,28},{8,16},{12,20},{16,8},{20,12},{24,0},{28,4},{1,25},{... | collective-permute-start | bytes 1400840 | tf_op jit(solution)/shard_map/ppermute | solution.py:707
  52.3 40.9 %collective-permute-start.13 = (bf16[256,768]{1,0:T(8,128)(2,1)S(1)}, bf16[256,768]{1,0:T(8,128)(2,1)S(1)}, u32[]{:S(2)}, u32[]{:S(2)}) collective-permute-start(bf16[256,768]{1,0:T(8,128)(2,1)S(1)} %bitcast.56), channel_id=1, source_target_pairs={{0,1},{1,2},{2,3},{3,0},{4,5},{5,6},{6,7},{7,4},{8,9},{9,10},{10,1... | collective-permute-start | bytes 1179656 | tf_op jit(solution)/shard_map/ppermute | solution.py:697
  60.3 32.9 %collective-permute-start.14 = (bf16[256,768]{1,0:T(8,128)(2,1)S(1)}, bf16[256,768]{1,0:T(8,128)(2,1)S(1)}, u32[]{:S(2)}, u32[]{:S(2)}) collective-permute-start(bf16[256,768]{1,0:T(8,128)(2,1)S(1)} %bitcast.57), channel_id=1, source_target_pairs={{0,2},{1,3},{2,0},{3,1},{4,6},{5,7},{6,4},{7,5},{8,10},{9,11},{10,... | collective-permute-start | bytes 1179656 | tf_op jit(solution)/shard_map/ppermute | solution.py:697
  62.9 30.4 %collective-permute-start.15 = (bf16[256,768]{1,0:T(8,128)(2,1)S(1)}, bf16[256,768]{1,0:T(8,128)(2,1)S(1)}, u32[]{:S(2)}, u32[]{:S(2)}) collective-permute-start(bf16[256,768]{1,0:T(8,128)(2,1)S(1)} %bitcast.58), channel_id=1, source_target_pairs={{0,3},{1,0},{2,1},{3,2},{4,7},{5,4},{6,5},{7,6},{8,11},{9,8},{10,9... | collective-permute-start | bytes 1179656 | tf_op jit(solution)/shard_map/ppermute | solution.py:697
  94.6 26.3 %collective-permute-start.17 = (bf16[256,768]{1,0:T(8,128)(2,1)}, bf16[256,768]{1,0:T(8,128)(2,1)S(1)}, u32[]{:S(2)}, u32[]{:S(2)}) collective-permute-start(bf16[256,768]{1,0:T(8,128)(2,1)} %get-tuple-element.95), channel_id=1, source_target_pairs={{0,1},{1,2},{2,3},{3,0},{4,5},{5,6},{6,7},{7,4},{8,9},{9,10},{10,1... | collective-permute-start | bytes 1179656 | tf_op jit(solution)/shard_map/ppermute | solution.py:697
  100.5 20.4 %collective-permute-start.16 = (bf16[256,768]{1,0:T(8,128)(2,1)}, bf16[256,768]{1,0:T(8,128)(2,1)}, u32[]{:S(2)}, u32[]{:S(2)}) collective-permute-start(bf16[256,768]{1,0:T(8,128)(2,1)} %get-tuple-element.93), channel_id=1, source_target_pairs={{0,3},{1,0},{2,1},{3,2},{4,7},{5,4},{6,5},{7,6},{8,11},{9,8},{10,9... | collective-permute-start | bytes 1179656 | tf_op jit(solution)/shard_map/ppermute | solution.py:697
  116.3 42.6 %all-to-all-start = ((bf16[8,96,1728]{2,1,0:T(8,128)(2,1)}), bf16[8,96,1728]{2,1,0:T(8,128)(2,1)S(1)}, u32[]{:S(2)}, u32[]{:S(2)}) async-start(bf16[8,96,1728]{2,1,0:T(8,128)(2,1)} %bitcast.52), calls=%async_computation | async-start | bytes 5505024 | tf_op jit(solution)/shard_map/all_to_all | solution.py:724
  120.3 20.3 %collective-permute-start.18 = (bf16[256,768]{1,0:T(8,128)(2,1)}, bf16[256,768]{1,0:T(8,128)(2,1)S(1)}, u32[]{:S(2)}, u32[]{:S(2)}) collective-permute-start(bf16[256,768]{1,0:T(8,128)(2,1)} %get-tuple-element.101), channel_id=1, source_target_pairs={{0,2},{1,3},{2,0},{3,1},{4,6},{5,7},{6,4},{7,5},{8,10},{9,11},{10,... | collective-permute-start | bytes 1179656 | tf_op jit(solution)/shard_map/ppermute | solution.py:697
  150.0 14.9 %collective-permute-start.19 = (bf16[256,768]{1,0:T(8,128)(2,1)}, bf16[256,768]{1,0:T(8,128)(2,1)}, u32[]{:S(2)}, u32[]{:S(2)}) collective-permute-start(bf16[256,768]{1,0:T(8,128)(2,1)} %get-tuple-element.110), channel_id=1, source_target_pairs={{0,3},{1,0},{2,1},{3,2},{4,7},{5,4},{6,5},{7,6},{8,11},{9,8},{10,9... | collective-permute-start | bytes 1179656 | tf_op jit(solution)/shard_map/ppermute | solution.py:697
  152.2 33.4 %collective-permute-start.20 = (bf16[256,768]{1,0:T(8,128)(2,1)}, bf16[256,768]{1,0:T(8,128)(2,1)}, u32[]{:S(2)}, u32[]{:S(2)}) collective-permute-start(bf16[256,768]{1,0:T(8,128)(2,1)} %get-tuple-element.111), channel_id=1, source_target_pairs={{0,2},{1,3},{2,0},{3,1},{4,6},{5,7},{6,4},{7,5},{8,10},{9,11},{10,... | collective-permute-start | bytes 1179656 | tf_op jit(solution)/shard_map/ppermute | solution.py:697
  152.2 33.4 %collective-permute-start.21 = (bf16[256,768]{1,0:T(8,128)(2,1)}, bf16[256,768]{1,0:T(8,128)(2,1)}, u32[]{:S(2)}, u32[]{:S(2)}) collective-permute-start(bf16[256,768]{1,0:T(8,128)(2,1)} %get-tuple-element.112), channel_id=1, source_target_pairs={{0,1},{1,2},{2,3},{3,0},{4,5},{5,6},{6,7},{7,4},{8,9},{9,10},{10,1... | collective-permute-start | bytes 1179656 | tf_op jit(solution)/shard_map/ppermute | solution.py:697
  160.1 31.1 %all-to-all-start.1 = ((bf16[8,96,704]{2,1,0:T(8,128)(2,1)}), bf16[8,96,704]{2,1,0:T(8,128)(2,1)S(1)}, u32[]{:S(2)}, u32[]{:S(2)}) async-start(bf16[8,96,704]{2,1,0:T(8,128)(2,1)} %bitcast.60), calls=%async_computation.1 | async-start | bytes 2359296 | tf_op jit(solution)/shard_map/all_to_all | solution.py:724
  192.1 13.0 %collective-permute-start.25 = (bf16[24,1472]{1,0:T(8,128)(2,1)S(1)}, bf16[24,1472]{1,0:T(8,128)(2,1)S(1)}, u32[]{:S(2)}, u32[]{:S(2)}) collective-permute-start(bf16[24,1472]{1,0:T(8,128)(2,1)S(1)} %get-tuple-element.122), channel_id=1, source_target_pairs={{0,3},{1,0},{2,1},{3,2},{4,7},{5,4},{6,5},{7,6},{8,11},{9,8},{10,9... | collective-permute-start | bytes 211976 | tf_op jit(solution)/shard_map/ppermute | solution.py:697
  198.2 8.4 %collective-permute-start.24 = (bf16[24,1472]{1,0:T(8,128)(2,1)S(1)}, bf16[24,1472]{1,0:T(8,128)(2,1)S(1)}, u32[]{:S(2)}, u32[]{:S(2)}) collective-permute-start(bf16[24,1472]{1,0:T(8,128)(2,1)S(1)} %get-tuple-element.121), channel_id=1, source_target_pairs={{0,2},{1,3},{2,0},{3,1},{4,6},{5,7},{6,4},{7,5},{8,10},{9,11},{10,... | collective-permute-start | bytes 211976 | tf_op jit(solution)/shard_map/ppermute | solution.py:697
  199.9 6.7 %collective-permute-start.23 = (bf16[24,1472]{1,0:T(8,128)(2,1)S(1)}, bf16[24,1472]{1,0:T(8,128)(2,1)S(1)}, u32[]{:S(2)}, u32[]{:S(2)}) collective-permute-start(bf16[24,1472]{1,0:T(8,128)(2,1)S(1)} %get-tuple-element.120), channel_id=1, source_target_pairs={{0,1},{1,2},{2,3},{3,0},{4,5},{5,6},{6,7},{7,4},{8,9},{9,10},{10,1... | collective-permute-start | bytes 211976 | tf_op jit(solution)/shard_map/ppermute | solution.py:697
  (22 other events, 241.6 us)

commit v4 on v3

--- a/solution.py
+++ b/solution.py
@@ -523,7 +523,7 @@
     low = grad_inner.astype(bf16)
     grad = product(low, up_ref[...], 1, 1)
     hat = normalise(join(x_refs).astype(f32))
-    scaled_ref[...] = grad * vec_ref[2:3]
+    scaled_ref[...] = (grad * vec_ref[2:3]).astype(bf16)
     sums_ref[0:1] += jnp.sum(grad * hat, axis=0, keepdims=True)
     sums_ref[1:2] += jnp.sum(grad, axis=0, keepdims=True)
     sums_ref[2:3] += jnp.sum(grad_inner, axis=0, keepdims=True)
@@ -600,7 +600,7 @@
     mixed_ref[...] = low
     grad = product(low, attn_ref[:, : low.shape[1]], 1, 1)
     hat = normalise(join(x_refs).astype(f32))
-    total = (grad * vec_ref[0:1] + scaled_ref[...]).astype(bf16)
+    total = (grad * vec_ref[0:1] + scaled_ref[...].astype(f32)).astype(bf16)
     store_blocks(refs[11:], spot_ref, step, total, parts)
     sums_ref[0:1] += jnp.sum(grad * hat, axis=0, keepdims=True)
     sums_ref[1:2] += jnp.sum(grad, axis=0, keepdims=True)
@@ -632,8 +632,8 @@
 def finish_kernel(
     rank_ref, *refs, factor, hidden,
 ):
-    qkv_ref, up_ref, proj_ref, down_ref, *small_refs = refs[-11:]
-    down_in, proj_in, refs = refs[-13], refs[-12], refs[:-13]
+    qkv_ref, up_ref, proj_ref, down_ref, *small_refs = refs[-12:]
+    down_in, proj_in, refs = refs[-14], refs[-13], refs[:-14]
     ranks, rank = len(refs), rank_ref[0]
     blocks = [ref[...].astype(f32) * factor for ref in refs]
     share, width = proj_ref.shape
@@ -658,8 +658,8 @@
     line = jnp.concatenate([small[j : j + 1] for j in range(LANES // 128)], axis=1)
     at = 0
     for j, ref in enumerate(small_refs):
-        if j == 5:
-            at += share
+        at -= share if j == 5 else 0
+        at += share if j == 6 else 0
         ref[...] = line[0, at : at + ref.shape[0]]
         at += ref.shape[0]
 
@@ -795,7 +795,7 @@
 
     x_go = after(x_own, *landed)
     x_rest = around([None] + [x_go] * (ranks - 2), 1, ranks)[1:]
-    x_all = jnp.concatenate([x_own, x_next] + x_rest)
+    x_all = jnp.concatenate([x_own] + [after(block, weights) for block in (x_next, *x_rest)])
     dy_go = after(dy_own, x_all)
     dy_got = around([dy_go] * (ranks - 1), 1, ranks)
 
@@ -858,7 +858,7 @@
         + [(dy_own, whole_block((own, width))), (active, tile(hidden)),
          (slope, tile(hidden)), (n2, tile(width)), (vec, whole_block((8, width))),
          (weights, column(0)), (weights, column(1)), (heads_low, upright_tile(cols))],
-        [(shape((count, width), f32), tile(width)),
+        [(shape((count, width), bf16), tile(width)),
          (shape((width, edge - mixed_cols + cols), bf16),
           whole_block((width, edge - mixed_cols + cols))),
          (shape((8, width), f32), whole_block((8, width)))],
@@ -871,7 +871,7 @@
 
     far = [r for r in range(1, ranks) if 2 * r == ranks]
     near = [r for r in range(1, ranks) if r not in far]
-    out_parts = part_out[:1] + [shift(after(part_out[r], dy_all), -r, ranks) for r in near]
+    out_parts = part_out[:1] + [shift(part_out[r], -r, ranks) for r in near]
     heads_low = after(heads_low, scaled, *out_parts)
     far_parts = [shift(after(part_out[r], scaled), -r, ranks) for r in far]
     head_tile = pl.BlockSpec((heads, own, HD), lambda t, *_: (0, t, 0))
@@ -937,7 +937,7 @@
     factor = 1.0 / math.sqrt(count * groups)
     down_part = feed_part[:, hidden : hidden + width]
     results = [(share, 3 * width), (share, ranks * hidden), (share, width), (piece, width)]
-    results += [(share,)] * 5 + [(3 * share,), (ratio * share,)]
+    results += [(share,)] * 6 + [(3 * share,), (ratio * share,)]
     qkv_own, up_own, proj_own, down_own, *small_own = call(
         functools.partial(finish_kernel, factor=factor, hidden=hidden),
         (1,),
@@ -949,13 +949,13 @@
         grad_in.astype(bf16).reshape(hidden_in.shape),
         *small_own[:4],
         qkv_own,
-        small_own[5],
+        small_own[6],
         proj_own,
         small_own[4],
         up_own,
-        small_own[6],
+        small_own[7],
         down_own,
-        small_own[4],
+        small_own[5],
     )
 
 

time: 212 us -> 206 us (0.972)
  waiting for transfers between devices: 54.8 us -> 50.2 us
  local copies, waits for them, and re-layouts: 9 us -> 5.98 us
  starting transfers between devices: 62.9 us -> 65.2 us
    ppermute x18, waiting for transfers between devices: 52 us -> 32.4 us  [shift(): lax.ppermute(block, 'seq', [(k, (k + amount) % ranks) for k in range(rank...]
    ppermute x6, waiting for transfers between devices: 2.76 us -> 17.8 us  [swap(): return lax.ppermute(block, 'dp', [(k, k ^ mask) for k in range(8)])]
    unnamed x37 -> x36, local copies, waits for them, and re-layouts: 4.99 us -> 1.96 us
    ppermute x18, starting transfers between devices: 44.1 us -> 46.6 us  [shift(): lax.ppermute(block, 'seq', [(k, (k + amount) % ranks) for k in range(rank...]
where the time goes in v4:
time: 206 us; the launch traced here: 205 us
  Pallas kernels  70.3 us (34%)
  starting transfers between devices  65.2 us (32%)
  waiting for transfers between devices  50.2 us (24%)
  other arithmetic  12.3 us (6%)
  local copies, waits for them, and re-layouts  5.98 us (3%)
    pallas_call x9, Pallas kernels, call(): pl.pallas_call(kernel, grid_spec=pltpu.PrefetchScalarGridSpec(num_scalar_...  70.3 us
    ppermute x18, starting transfers between devices, shift(): lax.ppermute(block, 'seq', [(k, (k + amount) % ranks) for k in range(rank...  46.6 us
    ppermute x18, waiting for transfers between devices, shift(): lax.ppermute(block, 'seq', [(k, (k + amount) % ranks) for k in range(rank...  32.4 us
    ppermute x6, waiting for transfers between devices, swap(): return lax.ppermute(block, 'dp', [(k, k ^ mask) for k in range(8)])  17.8 us
    all_to_all x2, starting transfers between devices, scatter_dp(): lax.all_to_all(parts.reshape(8, -1, parts.shape[1]), 'dp', 0, 0, tiled=True)  7.81 us
    ppermute x6, starting transfers between devices, swap(): return lax.ppermute(block, 'dp', [(k, k ^ mask) for k in range(8)])  7.26 us
  transfers between devices with their start and end apart: 28, of which 10 were waited for; matrix products, arithmetic and copies ran while one was open for 7% of the time, Pallas kernels for 32%

profile of v4, /device:TPU:0, one launch (start us, length us, event | category | flops | bytes accessed | tf_op | source)
XLA Modules:
  0.0 205.2 jit_solution(17342390439001602649)
XLA Ops:
  0.7 3.1 %collective-permute-start = (bf16[256,768]{1,0:T(8,128)(2,1)}, bf16[256,768]{1,0:T(8,128)(2,1)S(1)}, u32[]{:S(2)}, u32[]{:S(2)}) collective-permute-start(bf16[256,768]{1,0:T(8,128)(2,1)} %bitcast.41), channel_id=1, source_target_pairs={{0,1},{1,2},{2,3},{3,0},{4,5},{5,6},{6,7},{7,4},{8,9},{9,10},{10,1... | collective-permute-start | bytes 1179656 | tf_op jit(solution)/shard_map/ppermute | solution.py:697
  5.2 2.2 %shard_map.263 = (bf16[24,1472]{1,0:T(8,128)(2,1)}, bf16[24,1472]{1,0:T(8,128)(2,1)}, bf16[24,1472]{1,0:T(8,128)(2,1)}, bf16[24,1472]{1,0:T(8,128)(2,1)}, bf16[96,192]{1,0:T(8,128)(2,1)}) custom-call(s32[10]{0:T(128)} %pad_add_fusion.rank_ref.spot_ref, bf16[24,3072]{1,0:T(8,128)(2,1)} %up_ref.1, bf16[24,2304]{1,0:T(8,128)(2,1)} %qkv_ref.1, ...), custom_call_target="tpu_custom_call" | custom-call | flops 1000000000 | tf_op jit(solution)/shard_map/pallas_call | solution.py:677
  10.0 2.9 %collective-permute-start.3 = (bf16[24,1472]{1,0:T(8,128)(2,1)}, bf16[24,1472]{1,0:T(8,128)(2,1)S(1)}, u32[]{:S(2)}, u32[]{:S(2)}) collective-permute-start(bf16[24,1472]{1,0:T(8,128)(2,1)} %get-tuple-element.80), channel_id=1, source_target_pairs={{0,3},{1,0},{2,1},{3,2},{4,7},{5,4},{6,5},{7,6},{8,11},{9,8},{10,9... | collective-permute-start | bytes 211976 | tf_op jit(solution)/shard_map/ppermute | solution.py:697
  17.6 2.4 %collective-permute-done.2.refs_2_ = bf16[24,1472]{1,0:T(8,128)(2,1)S(1)} collective-permute-done((bf16[24,1472]{1,0:T(8,128)(2,1)}, bf16[24,1472]{1,0:T(8,128)(2,1)S(1)}, u32[]{:S(2)}, u32[]{:S(2)}) %collective-permute-start.2) | collective-permute-done | bytes 70688 | tf_op jit(solution)/shard_map/ppermute | solution.py:697
  25.1 3.3 %collective-permute-start.6 = (bf16[96,2432]{1,0:T(8,128)(2,1)}, bf16[96,2432]{1,0:T(8,128)(2,1)S(1)}, u32[]{:S(2)}, u32[]{:S(2)}) collective-permute-start(bf16[96,2432]{1,0:T(8,128)(2,1)} %shard_map.264), channel_id=1, source_target_pairs={{0,8},{4,12},{8,0},{12,4},{16,24},{20,28},{24,16},{28,20},{1,9},{5... | collective-permute-start | bytes 1400840 | tf_op jit(solution)/shard_map/ppermute | solution.py:707
  32.1 8.0 %collective-permute-done.6 = bf16[96,2432]{1,0:T(8,128)(2,1)S(1)} collective-permute-done((bf16[96,2432]{1,0:T(8,128)(2,1)}, bf16[96,2432]{1,0:T(8,128)(2,1)S(1)}, u32[]{:S(2)}, u32[]{:S(2)}) %collective-permute-start.6) | collective-permute-done | bytes 466976 | tf_op jit(solution)/shard_map/ppermute | solution.py:707
  40.2 3.8 %collective-permute-start.12 = (bf16[256,768]{1,0:T(8,128)(2,1)S(1)}, bf16[256,768]{1,0:T(8,128)(2,1)S(1)}, u32[]{:S(2)}, u32[]{:S(2)}) collective-permute-start(bf16[256,768]{1,0:T(8,128)(2,1)S(1)} %bitcast.43), channel_id=1, source_target_pairs={{0,3},{1,0},{2,1},{3,2},{4,7},{5,4},{6,5},{7,6},{8,11},{9,8},{10,9... | collective-permute-start | bytes 1179656 | tf_op jit(solution)/shard_map/ppermute | solution.py:697
  43.9 7.5 %collective-permute-done.7 = bf16[96,2432]{1,0:T(8,128)(2,1)S(1)} collective-permute-done((bf16[96,2432]{1,0:T(8,128)(2,1)}, bf16[96,2432]{1,0:T(8,128)(2,1)S(1)}, u32[]{:S(2)}, u32[]{:S(2)}) %collective-permute-start.7) | collective-permute-done | bytes 466976 | tf_op jit(solution)/shard_map/ppermute | solution.py:707
  54.8 3.7 %collective-permute-done.12 = bf16[256,768]{1,0:T(8,128)(2,1)S(1)} collective-permute-done((bf16[256,768]{1,0:T(8,128)(2,1)S(1)}, bf16[256,768]{1,0:T(8,128)(2,1)S(1)}, u32[]{:S(2)}, u32[]{:S(2)}) %collective-permute-start.12) | collective-permute-done | bytes 393248 | tf_op jit(solution)/shard_map/ppermute | solution.py:697
  60.4 2.2 %collective-permute-start.16 = (bf16[256,768]{1,0:T(8,128)(2,1)S(1)}, bf16[256,768]{1,0:T(8,128)(2,1)S(1)}, u32[]{:S(2)}, u32[]{:S(2)}) collective-permute-start(bf16[256,768]{1,0:T(8,128)(2,1)S(1)} %bitcast.57), channel_id=1, source_target_pairs={{0,2},{1,3},{2,0},{3,1},{4,6},{5,7},{6,4},{7,5},{8,10},{9,11},{10,... | collective-permute-start | bytes 1179656 | tf_op jit(solution)/shard_map/ppermute | solution.py:697
  63.6 12.2 %shard_map.265 = (bf16[1024,768]{1,0:T(8,128)(2,1)}, bf16[1024,768]{1,0:T(8,128)(2,1)}, bf16[1024,768]{1,0:T(8,128)(2,1)}, bf16[1024,768]{1,0:T(8,128)(2,1)}, f3...) custom-call(s32[10]{0:T(128)} %pad_add_fusion.rank_ref.spot_ref, ...), custom_call_target="tpu_custom_call" | custom-call | flops 10000000000 | tf_op jit(solution)/shard_map/pallas_call | solution.py:677
  76.5 12.2 %shard_map.266 = (bf16[3,1024,1024]{2,1,0:T(8,128)(2,1)}, f32[8,1024]{1,0:T(8,128)}, bf16[192,1024]{1,0:T(8,128)(2,1)}, bf16[256,768]{1,0:T(8,128)(2,1)}, bf16[2...) custom-call(s32[10]{0:T(128)} %pad_add_fusion.rank_ref.spot_ref, ...), custom_call_target="tpu_custom_call" | custom-call | flops 10000000000 | tf_op jit(solution)/shard_map/pallas_call | solution.py:677
  92.0 12.9 %shard_map.267 = (bf16[1024,768]{1,0:T(8,128)(2,1)}, bf16[768,1728]{1,0:T(8,128)(2,1)}, f32[8,768]{1,0:T(8,128)}) custom-call(s32[10]{0:T(128)} %pad_add_fusion.rank_ref.spot_ref, bf16[1024,768]{1,0:T(8,128)(2,1)} %pad_maximum_fusion.1.refs_0_.refs_1_, bf16[1024,768]{1,0:T(8,128)(2,1)} %pad_maximum_fusion.1.refs_0_.refs_1_, ...), custom_call_target="tpu_custom_call" | custom-call | flops 12000000000 | tf_op jit(solution)/shard_map/pallas_call | solution.py:677
  104.9 3.8 %all-to-all-start = ((bf16[8,96,1728]{2,1,0:T(8,128)(2,1)}), bf16[8,96,1728]{2,1,0:T(8,128)(2,1)S(1)}, u32[]{:S(2)}, u32[]{:S(2)}) async-start(bf16[8,96,1728]{2,1,0:T(8,128)(2,1)} %bitcast.52), calls=%async_computation | async-start | bytes 5505024 | tf_op jit(solution)/shard_map/all_to_all | solution.py:724
  109.1 7.0 %collective-permute-start.18 = (bf16[256,768]{1,0:T(8,128)(2,1)}, bf16[256,768]{1,0:T(8,128)(2,1)S(1)}, u32[]{:S(2)}, u32[]{:S(2)}) collective-permute-start(bf16[256,768]{1,0:T(8,128)(2,1)} %get-tuple-element.104), channel_id=1, source_target_pairs={{0,2},{1,3},{2,0},{3,1},{4,6},{5,7},{6,4},{7,5},{8,10},{9,11},{10,... | collective-permute-start | bytes 1179656 | tf_op jit(solution)/shard_map/ppermute | solution.py:697
  116.1 11.3 %shard_map.268 = (f32[192,1024]{1,0:T(8,128)}, f32[3,1024,64]{2,1,0:T(8,128)}, f32[3,1024,64]{2,1,0:T(8,128)}) custom-call(s32[10]{0:T(128)} %pad_add_fusion.rank_ref.spot_ref, bf16[1024,768]{1,0:T(8,128)(2,1)} %pad_maximum_fusion.1.refs_0_.refs_1_, bf16[1024,768]{1,0:T(8,128)(2,1)} %pad_maximum_fusion.1.refs_0_.refs_1_, ...), custom_call_target="tpu_custom_call" | custom-call | flops 10000000000 | tf_op jit(solution)/shard_map/pallas_call | solution.py:677
  127.5 9.2 %shard_map.269 = (bf16[1024,576]{1,0:T(8,128)(2,1)}, f32[8,768]{1,0:T(8,128)}, f32[8,576]{1,0:T(8,128)}, bf16[256,768]{1,0:T(8,128)(2,1)}, bf16[256,768]{1,0:T(8...) custom-call(s32[10]{0:T(128)} %pad_add_fusion.rank_ref.spot_ref, ...), custom_call_target="tpu_custom_call" | custom-call | flops 8000000000 | tf_op jit(solution)/shard_map/pallas_call | solution.py:677
  136.7 10.6 %collective-permute-start.19 = (bf16[256,768]{1,0:T(8,128)(2,1)}, bf16[256,768]{1,0:T(8,128)(2,1)}, u32[]{:S(2)}, u32[]{:S(2)}) collective-permute-start(bf16[256,768]{1,0:T(8,128)(2,1)} %get-tuple-element.113), channel_id=1, source_target_pairs={{0,3},{1,0},{2,1},{3,2},{4,7},{5,4},{6,5},{7,6},{8,11},{9,8},{10,9... | collective-permute-start | bytes 1179656 | tf_op jit(solution)/shard_map/ppermute | solution.py:697
  147.9 6.1 %shard_map.270 = bf16[768,704]{1,0:T(8,128)(2,1)} custom-call(s32[10]{0:T(128)} %pad_add_fusion.rank_ref.spot_ref, bf16[1024,768]{1,0:T(8,128)(2,1)} %get-tuple-element.117.n1_ref, bf16[1024,576]{1,0:T(8,128)(2,1)} %get-tuple-element.118.mixed_ref, f32[8,768]{1,0:T(8,128)} %get-tuple-element.119.sums_ref, f32[8,576]{1,0:T(8,128)} %get-tuple-element.120.gbias_ref, ...), custom_call_target="tpu_custom_call" | custom-call | flops 5000000000 | tf_op jit(solution)/shard_map/pallas_call | solution.py:677
  155.2 4.0 %all-to-all-start.1 = ((bf16[8,96,704]{2,1,0:T(8,128)(2,1)}), bf16[8,96,704]{2,1,0:T(8,128)(2,1)S(1)}, u32[]{:S(2)}, u32[]{:S(2)}) async-start(bf16[8,96,704]{2,1,0:T(8,128)(2,1)} %bitcast.60), calls=%async_computation.1 | async-start | bytes 2359296 | tf_op jit(solution)/shard_map/all_to_all | solution.py:724
  160.1 22.3 %collective-permute-done.20 = bf16[256,768]{1,0:T(8,128)(2,1)} collective-permute-done((bf16[256,768]{1,0:T(8,128)(2,1)}, bf16[256,768]{1,0:T(8,128)(2,1)}, u32[]{:S(2)}, u32[]{:S(2)}) %collective-permute-start.20) | collective-permute-done | bytes 393248 | tf_op jit(solution)/shard_map/ppermute | solution.py:697
  188.9 6.1 %collective-permute-start.25 = (bf16[24,1472]{1,0:T(8,128)(2,1)S(1)}, bf16[24,1472]{1,0:T(8,128)(2,1)S(1)}, u32[]{:S(2)}, u32[]{:S(2)}) collective-permute-start(bf16[24,1472]{1,0:T(8,128)(2,1)S(1)} %get-tuple-element.125), channel_id=1, source_target_pairs={{0,3},{1,0},{2,1},{3,2},{4,7},{5,4},{6,5},{7,6},{8,11},{9,8},{10,9... | collective-permute-start | bytes 211976 | tf_op jit(solution)/shard_map/ppermute | solution.py:697
  197.1 3.1 %fusion.9 = (bf16[256,768]{1,0:T(8,128)(2,1)}, bf16[256,768]{1,0:T(8,128)(2,1)}) fusion(f32[256]{0:T(256)S(1)} %get-tuple-element.152, f32[256]{0:T(256)S(1)} %get-tuple-element.150, f32[256]{0:T(256)} %get-tuple-element.153, f32[256]{0:T(256)S(1)} %rsqrt_bitcast_fusion, bf16[1,2,128,768]{3,2,1,0:T(8,128)(2,1)S(1)} %copy-done.3, ...), kind=kLoop, calls=%fused_computation.16 | loop fusion | flops 5308416 | bytes 4725760 | tf_op jit(solution)/shard_map/convert_element_type | solution.py:949
  202.8 2.2 %shard_map.271 = (f32[24,2304]{1,0:T(8,128)}, f32[24,3072]{1,0:T(8,128)}, f32[24,768]{1,0:T(8,128)}, f32[96,768]{1,0:T(8,128)}, f32[24]{0:T(128)}, /*index=5*/f3...) custom-call(s32[10]{0:T(128)} %pad_add_fusion.rank_ref.spot_ref, ...), custom_call_target="tpu_custom_call" | custom-call | flops 1000000000 | tf_op jit(solution)/shard_map/pallas_call | solution.py:677
  (113 shorter events, 41.9 us)
Async XLA Ops:
  0.7 15.4 %collective-permute-start = (bf16[256,768]{1,0:T(8,128)(2,1)}, bf16[256,768]{1,0:T(8,128)(2,1)S(1)}, u32[]{:S(2)}, u32[]{:S(2)}) collective-permute-start(bf16[256,768]{1,0:T(8,128)(2,1)} %bitcast.41), channel_id=1, source_target_pairs={{0,1},{1,2},{2,3},{3,0},{4,5},{5,6},{6,7},{7,4},{8,9},{9,10},{10,1... | collective-permute-start | bytes 1179656 | tf_op jit(solution)/shard_map/ppermute | solution.py:697
  7.4 10.2 %collective-permute-start.1 = (bf16[24,1472]{1,0:T(8,128)(2,1)}, bf16[24,1472]{1,0:T(8,128)(2,1)S(1)}, u32[]{:S(2)}, u32[]{:S(2)}) collective-permute-start(bf16[24,1472]{1,0:T(8,128)(2,1)} %get-tuple-element.78), channel_id=1, source_target_pairs={{0,1},{1,2},{2,3},{3,0},{4,5},{5,6},{6,7},{7,4},{8,9},{9,10},{10,1... | collective-permute-start | bytes 211976 | tf_op jit(solution)/shard_map/ppermute | solution.py:697
  9.0 11.0 %collective-permute-start.2 = (bf16[24,1472]{1,0:T(8,128)(2,1)}, bf16[24,1472]{1,0:T(8,128)(2,1)S(1)}, u32[]{:S(2)}, u32[]{:S(2)}) collective-permute-start(bf16[24,1472]{1,0:T(8,128)(2,1)} %get-tuple-element.79), channel_id=1, source_target_pairs={{0,2},{1,3},{2,0},{3,1},{4,6},{5,7},{6,4},{7,5},{8,10},{9,11},{10,... | collective-permute-start | bytes 211976 | tf_op jit(solution)/shard_map/ppermute | solution.py:697
  10.0 9.9 %collective-permute-start.3 = (bf16[24,1472]{1,0:T(8,128)(2,1)}, bf16[24,1472]{1,0:T(8,128)(2,1)S(1)}, u32[]{:S(2)}, u32[]{:S(2)}) collective-permute-start(bf16[24,1472]{1,0:T(8,128)(2,1)} %get-tuple-element.80), channel_id=1, source_target_pairs={{0,3},{1,0},{2,1},{3,2},{4,7},{5,4},{6,5},{7,6},{8,11},{9,8},{10,9... | collective-permute-start | bytes 211976 | tf_op jit(solution)/shard_map/ppermute | solution.py:697
  23.2 28.8 %collective-permute-start.5 = (bf16[96,2432]{1,0:T(8,128)(2,1)}, bf16[96,2432]{1,0:T(8,128)(2,1)S(1)}, u32[]{:S(2)}, u32[]{:S(2)}) collective-permute-start(bf16[96,2432]{1,0:T(8,128)(2,1)} %shard_map.264), channel_id=1, source_target_pairs={{0,4},{4,0},{8,12},{12,8},{16,20},{20,16},{24,28},{28,24},{1,5},{5... | collective-permute-start | bytes 1400840 | tf_op jit(solution)/shard_map/ppermute | solution.py:707
  25.1 15.1 %collective-permute-start.6 = (bf16[96,2432]{1,0:T(8,128)(2,1)}, bf16[96,2432]{1,0:T(8,128)(2,1)S(1)}, u32[]{:S(2)}, u32[]{:S(2)}) collective-permute-start(bf16[96,2432]{1,0:T(8,128)(2,1)} %shard_map.264), channel_id=1, source_target_pairs={{0,8},{4,12},{8,0},{12,4},{16,24},{20,28},{24,16},{28,20},{1,9},{5... | collective-permute-start | bytes 1400840 | tf_op jit(solution)/shard_map/ppermute | solution.py:707
  28.4 23.0 %collective-permute-start.7 = (bf16[96,2432]{1,0:T(8,128)(2,1)}, bf16[96,2432]{1,0:T(8,128)(2,1)S(1)}, u32[]{:S(2)}, u32[]{:S(2)}) collective-permute-start(bf16[96,2432]{1,0:T(8,128)(2,1)} %shard_map.264), channel_id=1, source_target_pairs={{0,16},{4,20},{8,24},{12,28},{16,0},{20,4},{24,8},{28,12},{1,17},{... | collective-permute-start | bytes 1400840 | tf_op jit(solution)/shard_map/ppermute | solution.py:707
  29.8 21.8 %collective-permute-start.8 = (bf16[96,2432]{1,0:T(8,128)(2,1)}, bf16[96,2432]{1,0:T(8,128)(2,1)S(1)}, u32[]{:S(2)}, u32[]{:S(2)}) collective-permute-start(bf16[96,2432]{1,0:T(8,128)(2,1)} %shard_map.264), channel_id=1, source_target_pairs={{0,24},{4,28},{8,16},{12,20},{16,8},{20,12},{24,0},{28,4},{1,25},{... | collective-permute-start | bytes 1400840 | tf_op jit(solution)/shard_map/ppermute | solution.py:707
  30.0 24.8 %collective-permute-start.11 = (bf16[256,768]{1,0:T(8,128)(2,1)S(1)}, bf16[256,768]{1,0:T(8,128)(2,1)S(1)}, u32[]{:S(2)}, u32[]{:S(2)}) collective-permute-start(bf16[256,768]{1,0:T(8,128)(2,1)S(1)} %bitcast.42), channel_id=1, source_target_pairs={{0,2},{1,3},{2,0},{3,1},{4,6},{5,7},{6,4},{7,5},{8,10},{9,11},{10,... | collective-permute-start | bytes 1179656 | tf_op jit(solution)/shard_map/ppermute | solution.py:697
  40.2 18.4 %collective-permute-start.12 = (bf16[256,768]{1,0:T(8,128)(2,1)S(1)}, bf16[256,768]{1,0:T(8,128)(2,1)S(1)}, u32[]{:S(2)}, u32[]{:S(2)}) collective-permute-start(bf16[256,768]{1,0:T(8,128)(2,1)S(1)} %bitcast.43), channel_id=1, source_target_pairs={{0,3},{1,0},{2,1},{3,2},{4,7},{5,4},{6,5},{7,6},{8,11},{9,8},{10,9... | collective-permute-start | bytes 1179656 | tf_op jit(solution)/shard_map/ppermute | solution.py:697
  59.8 30.9 %collective-permute-start.15 = (bf16[256,768]{1,0:T(8,128)(2,1)S(1)}, bf16[256,768]{1,0:T(8,128)(2,1)S(1)}, u32[]{:S(2)}, u32[]{:S(2)}) collective-permute-start(bf16[256,768]{1,0:T(8,128)(2,1)S(1)} %bitcast.56), channel_id=1, source_target_pairs={{0,1},{1,2},{2,3},{3,0},{4,5},{5,6},{6,7},{7,4},{8,9},{9,10},{10,1... | collective-permute-start | bytes 1179656 | tf_op jit(solution)/shard_map/ppermute | solution.py:697
  60.4 30.3 %collective-permute-start.16 = (bf16[256,768]{1,0:T(8,128)(2,1)S(1)}, bf16[256,768]{1,0:T(8,128)(2,1)S(1)}, u32[]{:S(2)}, u32[]{:S(2)}) collective-permute-start(bf16[256,768]{1,0:T(8,128)(2,1)S(1)} %bitcast.57), channel_id=1, source_target_pairs={{0,2},{1,3},{2,0},{3,1},{4,6},{5,7},{6,4},{7,5},{8,10},{9,11},{10,... | collective-permute-start | bytes 1179656 | tf_op jit(solution)/shard_map/ppermute | solution.py:697
  62.6 28.2 %collective-permute-start.17 = (bf16[256,768]{1,0:T(8,128)(2,1)S(1)}, bf16[256,768]{1,0:T(8,128)(2,1)S(1)}, u32[]{:S(2)}, u32[]{:S(2)}) collective-permute-start(bf16[256,768]{1,0:T(8,128)(2,1)S(1)} %bitcast.58), channel_id=1, source_target_pairs={{0,3},{1,0},{2,1},{3,2},{4,7},{5,4},{6,5},{7,6},{8,11},{9,8},{10,9... | collective-permute-start | bytes 1179656 | tf_op jit(solution)/shard_map/ppermute | solution.py:697
  88.6 27.5 %collective-permute-start.13 = (bf16[256,768]{1,0:T(8,128)(2,1)}, bf16[256,768]{1,0:T(8,128)(2,1)S(1)}, u32[]{:S(2)}, u32[]{:S(2)}) collective-permute-start(bf16[256,768]{1,0:T(8,128)(2,1)} %get-tuple-element.92), channel_id=1, source_target_pairs={{0,3},{1,0},{2,1},{3,2},{4,7},{5,4},{6,5},{7,6},{8,11},{9,8},{10,9... | collective-permute-start | bytes 1179656 | tf_op jit(solution)/shard_map/ppermute | solution.py:697
  89.9 26.2 %collective-permute-start.14 = (bf16[256,768]{1,0:T(8,128)(2,1)}, bf16[256,768]{1,0:T(8,128)(2,1)}, u32[]{:S(2)}, u32[]{:S(2)}) collective-permute-start(bf16[256,768]{1,0:T(8,128)(2,1)} %get-tuple-element.93), channel_id=1, source_target_pairs={{0,1},{1,2},{2,3},{3,0},{4,5},{5,6},{6,7},{7,4},{8,9},{9,10},{10,1... | collective-permute-start | bytes 1179656 | tf_op jit(solution)/shard_map/ppermute | solution.py:697
  104.9 49.1 %all-to-all-start = ((bf16[8,96,1728]{2,1,0:T(8,128)(2,1)}), bf16[8,96,1728]{2,1,0:T(8,128)(2,1)S(1)}, u32[]{:S(2)}, u32[]{:S(2)}) async-start(bf16[8,96,1728]{2,1,0:T(8,128)(2,1)} %bitcast.52), calls=%async_computation | async-start | bytes 5505024 | tf_op jit(solution)/shard_map/all_to_all | solution.py:724
  109.1 18.4 %collective-permute-start.18 = (bf16[256,768]{1,0:T(8,128)(2,1)}, bf16[256,768]{1,0:T(8,128)(2,1)S(1)}, u32[]{:S(2)}, u32[]{:S(2)}) collective-permute-start(bf16[256,768]{1,0:T(8,128)(2,1)} %get-tuple-element.104), channel_id=1, source_target_pairs={{0,2},{1,3},{2,0},{3,1},{4,6},{5,7},{6,4},{7,5},{8,10},{9,11},{10,... | collective-permute-start | bytes 1179656 | tf_op jit(solution)/shard_map/ppermute | solution.py:697
  136.7 23.4 %collective-permute-start.19 = (bf16[256,768]{1,0:T(8,128)(2,1)}, bf16[256,768]{1,0:T(8,128)(2,1)}, u32[]{:S(2)}, u32[]{:S(2)}) collective-permute-start(bf16[256,768]{1,0:T(8,128)(2,1)} %get-tuple-element.113), channel_id=1, source_target_pairs={{0,3},{1,0},{2,1},{3,2},{4,7},{5,4},{6,5},{7,6},{8,11},{9,8},{10,9... | collective-permute-start | bytes 1179656 | tf_op jit(solution)/shard_map/ppermute | solution.py:697
  147.3 35.1 %collective-permute-start.20 = (bf16[256,768]{1,0:T(8,128)(2,1)}, bf16[256,768]{1,0:T(8,128)(2,1)}, u32[]{:S(2)}, u32[]{:S(2)}) collective-permute-start(bf16[256,768]{1,0:T(8,128)(2,1)} %get-tuple-element.114), channel_id=1, source_target_pairs={{0,2},{1,3},{2,0},{3,1},{4,6},{5,7},{6,4},{7,5},{8,10},{9,11},{10,... | collective-permute-start | bytes 1179656 | tf_op jit(solution)/shard_map/ppermute | solution.py:697
  147.6 34.8 %collective-permute-start.21 = (bf16[256,768]{1,0:T(8,128)(2,1)}, bf16[256,768]{1,0:T(8,128)(2,1)}, u32[]{:S(2)}, u32[]{:S(2)}) collective-permute-start(bf16[256,768]{1,0:T(8,128)(2,1)} %get-tuple-element.115), channel_id=1, source_target_pairs={{0,1},{1,2},{2,3},{3,0},{4,5},{5,6},{6,7},{7,4},{8,9},{9,10},{10,1... | collective-permute-start | bytes 1179656 | tf_op jit(solution)/shard_map/ppermute | solution.py:697
  155.2 32.8 %all-to-all-start.1 = ((bf16[8,96,704]{2,1,0:T(8,128)(2,1)}), bf16[8,96,704]{2,1,0:T(8,128)(2,1)S(1)}, u32[]{:S(2)}, u32[]{:S(2)}) async-start(bf16[8,96,704]{2,1,0:T(8,128)(2,1)} %bitcast.60), calls=%async_computation.1 | async-start | bytes 2359296 | tf_op jit(solution)/shard_map/all_to_all | solution.py:724
  188.9 11.3 %collective-permute-start.25 = (bf16[24,1472]{1,0:T(8,128)(2,1)S(1)}, bf16[24,1472]{1,0:T(8,128)(2,1)S(1)}, u32[]{:S(2)}, u32[]{:S(2)}) collective-permute-start(bf16[24,1472]{1,0:T(8,128)(2,1)S(1)} %get-tuple-element.125), channel_id=1, source_target_pairs={{0,3},{1,0},{2,1},{3,2},{4,7},{5,4},{6,5},{7,6},{8,11},{9,8},{10,9... | collective-permute-start | bytes 211976 | tf_op jit(solution)/shard_map/ppermute | solution.py:697
  195.0 7.1 %collective-permute-start.24 = (bf16[24,1472]{1,0:T(8,128)(2,1)S(1)}, bf16[24,1472]{1,0:T(8,128)(2,1)S(1)}, u32[]{:S(2)}, u32[]{:S(2)}) collective-permute-start(bf16[24,1472]{1,0:T(8,128)(2,1)S(1)} %get-tuple-element.124), channel_id=1, source_target_pairs={{0,2},{1,3},{2,0},{3,1},{4,6},{5,7},{6,4},{7,5},{8,10},{9,11},{10,... | collective-permute-start | bytes 211976 | tf_op jit(solution)/shard_map/ppermute | solution.py:697
  195.0 7.1 %collective-permute-start.23 = (bf16[24,1472]{1,0:T(8,128)(2,1)S(1)}, bf16[24,1472]{1,0:T(8,128)(2,1)S(1)}, u32[]{:S(2)}, u32[]{:S(2)}) collective-permute-start(bf16[24,1472]{1,0:T(8,128)(2,1)S(1)} %get-tuple-element.123), channel_id=1, source_target_pairs={{0,1},{1,2},{2,3},{3,0},{4,5},{5,6},{6,7},{7,4},{8,9},{9,10},{10,1... | collective-permute-start | bytes 211976 | tf_op jit(solution)/shard_map/ppermute | solution.py:697
  (22 other events, 230.2 us)

commit v5 on v4

--- a/solution.py
+++ b/solution.py
@@ -417,8 +417,8 @@
 
 
 def front_kernel(rank_ref, *refs, ranks, ratio, parts):
-    x_refs, (small_ref, cos_ref, sin_ref, up_ref, down_ref, attn_ref) = refs[:parts], refs[parts:-10]
-    n1_ref, n2_ref, act_ref, slope_ref, fed_ref, upright_ref, rows_ref = refs[-10:-3]
+    x_refs, (small_ref, cos_ref, sin_ref, up_ref, down_ref, attn_ref) = refs[:parts], refs[parts:-11]
+    hat_ref, n1_ref, n2_ref, act_ref, slope_ref, fed_ref, upright_ref, rows_ref = refs[-11:-3]
     vec_ref, own_out_ref, bias_ref = refs[-3:]
     width, part3 = n1_ref.shape[1], upright_ref.shape[0]
     cols, hidden = part3 // 3, act_ref.shape[1]
@@ -450,6 +450,7 @@
         own_out_ref[...] = jnp.concatenate(rebuilt, axis=0).astype(bf16)
 
     hat = normalise(join(x_refs).astype(f32))
+    hat_ref[...] = hat.astype(bf16)
     vec = vec_ref[...]
     n1 = (hat * vec[0:1] + vec[1:2]).astype(bf16)
     n2 = (hat * vec[2:3] + vec[3:4]).astype(bf16)
@@ -505,7 +506,7 @@
 
 
 def feed_back_kernel(spot_ref, *refs, ranks, parts):
-    dy_refs, x_refs, refs = refs[:parts], refs[parts : 2 * parts], refs[2 * parts :]
+    dy_refs, hat_ref, refs = refs[:parts], refs[parts], refs[parts + 1 :]
     own_ref, act_ref, slope_ref, n2_ref, vec_ref, up_ref, down_ref, heads_ref = refs[:8]
     scaled_ref, grads_ref, sums_ref, acc_up, acc_down, acc_out = refs[8:]
     step = pl.program_id(0)
@@ -522,7 +523,7 @@
     grad_inner = product(dy, down_ref[...], 1, 1) * slope_ref[...].astype(f32)
     low = grad_inner.astype(bf16)
     grad = product(low, up_ref[...], 1, 1)
-    hat = normalise(join(x_refs).astype(f32))
+    hat = hat_ref[...].astype(f32)
     scaled_ref[...] = (grad * vec_ref[2:3]).astype(bf16)
     sums_ref[0:1] += jnp.sum(grad * hat, axis=0, keepdims=True)
     sums_ref[1:2] += jnp.sum(grad, axis=0, keepdims=True)
@@ -579,7 +580,7 @@
 
 
 def rear_kernel(spot_ref, *refs, ranks, parts):
-    x_refs, refs = refs[:parts], refs[parts:]
+    hat_ref, refs = refs[0], refs[1:]
     gquery_ref, gkey_ref, gvalue_ref, cos_ref, sin_ref, scaled_ref, vec_ref, attn_ref = refs[:8]
     mixed_ref, sums_ref, gbias_ref = refs[8:11]
     step = pl.program_id(0)
@@ -599,7 +600,7 @@
     low = mixed.astype(bf16)
     mixed_ref[...] = low
     grad = product(low, attn_ref[:, : low.shape[1]], 1, 1)
-    hat = normalise(join(x_refs).astype(f32))
+    hat = hat_ref[...].astype(f32)
     total = (grad * vec_ref[0:1] + scaled_ref[...].astype(f32)).astype(bf16)
     store_blocks(refs[11:], spot_ref, step, total, parts)
     sums_ref[0:1] += jnp.sum(grad * hat, axis=0, keepdims=True)
@@ -818,14 +819,14 @@
     in_order = lambda array: [(array, spec) for spec in by_place]
     each = [(shape((own, width), bf16), whole_block((own, width)))] * ranks
 
-    n1, n2, active, slope, fed, upright, rows, vec, out_own = call(
+    hat, n1, n2, active, slope, fed, upright, rows, vec, out_own = call(
         functools.partial(front_kernel, ranks=ranks, ratio=ratio, parts=blocks_own),
         (ranks,),
         in_order(x_all)
         + [(weights, pl.BlockSpec((width, 128), lambda *_: (0, (edge + cols) // 128)))] + angles
         + [(weights, column(0)), (weights, column(1)), (weights, column(2))],
-        [(shape((count, width), bf16), tile(width)), (shape((count, width), bf16), tile(width)),
-         (shape((count, hidden), bf16), tile(hidden)), (shape((count, hidden), bf16), tile(hidden)),
+        [(shape((count, width), bf16), tile(width))] * 3
+        + [(shape((count, hidden), bf16), tile(hidden)), (shape((count, hidden), bf16), tile(hidden)),
          (shape((count, width), f32), tile(width)),
          (shape((mixed_cols, count), bf16), upright_tile(mixed_cols)),
          (shape((3 * heads, count, HD), bf16),
@@ -854,8 +855,8 @@
     scaled, grads_feed, feed_sums = call(
         functools.partial(feed_back_kernel, ranks=ranks, parts=blocks_own),
         (ranks,),
-        in_order(dy_all) + in_order(x_all)
-        + [(dy_own, whole_block((own, width))), (active, tile(hidden)),
+        in_order(dy_all)
+        + [(hat, tile(width)), (dy_own, whole_block((own, width))), (active, tile(hidden)),
          (slope, tile(hidden)), (n2, tile(width)), (vec, whole_block((8, width))),
          (weights, column(0)), (weights, column(1)), (heads_low, upright_tile(cols))],
         [(shape((count, width), bf16), tile(width)),
@@ -895,7 +896,7 @@
     mixed, attn_sums, attn_bias, *total = call(
         functools.partial(rear_kernel, ranks=ranks, parts=blocks_own),
         (ranks,),
-        in_order(x_all) + [(gquery, upright_tile(cols)), (gkey, head_tile), (gvalue, head_tile)]
+        [(hat, tile(width)), (gquery, upright_tile(cols)), (gkey, head_tile), (gvalue, head_tile)]
         + angles
         + [(scaled, tile(width)), (vec, whole_block((8, width))), (weights, column(2))],
         [(shape((count, mixed_cols), bf16), tile(mixed_cols)),

time: 206 us -> 205 us (level)
  no operation moved by 1% of the time
where the time goes in v5:
time: 205 us
  Pallas kernels  69.7 us (34%)
  starting transfers between devices  65.1 us (32%)
  waiting for transfers between devices  50.1 us (24%)
  other arithmetic  12.3 us (6%)
  local copies, waits for them, and re-layouts  5.97 us (3%)
    pallas_call x9, Pallas kernels, call(): pl.pallas_call(kernel, grid_spec=pltpu.PrefetchScalarGridSpec(num_scalar_...  69.7 us
    ppermute x18, starting transfers between devices, shift(): lax.ppermute(block, 'seq', [(k, (k + amount) % ranks) for k in range(rank...  46.6 us
    ppermute x18, waiting for transfers between devices, shift(): lax.ppermute(block, 'seq', [(k, (k + amount) % ranks) for k in range(rank...  32.3 us
    ppermute x6, waiting for transfers between devices, swap(): return lax.ppermute(block, 'dp', [(k, k ^ mask) for k in range(8)])  17.8 us
    all_to_all x2, starting transfers between devices, scatter_dp(): lax.all_to_all(parts.reshape(8, -1, parts.shape[1]), 'dp', 0, 0, tiled=True)  7.8 us
    ppermute x6, starting transfers between devices, swap(): return lax.ppermute(block, 'dp', [(k, k ^ mask) for k in range(8)])  7.26 us
  transfers between devices with their start and end apart: 28, of which 10 were waited for; matrix products, arithmetic and copies ran while one was open for 7% of the time, Pallas kernels for 32%

profile of v5, /device:TPU:0, one launch (start us, length us, event | category | flops | bytes accessed | tf_op | source)
XLA Modules:
  0.0 204.5 jit_solution(12545593117969489449)
XLA Ops:
  0.7 3.1 %collective-permute-start = (bf16[256,768]{1,0:T(8,128)(2,1)}, bf16[256,768]{1,0:T(8,128)(2,1)S(1)}, u32[]{:S(2)}, u32[]{:S(2)}) collective-permute-start(bf16[256,768]{1,0:T(8,128)(2,1)} %bitcast.41), channel_id=1, source_target_pairs={{0,1},{1,2},{2,3},{3,0},{4,5},{5,6},{6,7},{7,4},{8,9},{9,10},{10,1... | collective-permute-start | bytes 1179656 | tf_op jit(solution)/shard_map/ppermute | solution.py:698
  5.2 2.2 %shard_map.263 = (bf16[24,1472]{1,0:T(8,128)(2,1)}, bf16[24,1472]{1,0:T(8,128)(2,1)}, bf16[24,1472]{1,0:T(8,128)(2,1)}, bf16[24,1472]{1,0:T(8,128)(2,1)}, bf16[96,192]{1,0:T(8,128)(2,1)}) custom-call(s32[10]{0:T(128)} %pad_add_fusion.rank_ref.spot_ref, bf16[24,3072]{1,0:T(8,128)(2,1)} %up_ref.1, bf16[24,2304]{1,0:T(8,128)(2,1)} %qkv_ref.1, ...), custom_call_target="tpu_custom_call" | custom-call | flops 1000000000 | tf_op jit(solution)/shard_map/pallas_call | solution.py:678
  10.0 2.9 %collective-permute-start.3 = (bf16[24,1472]{1,0:T(8,128)(2,1)}, bf16[24,1472]{1,0:T(8,128)(2,1)S(1)}, u32[]{:S(2)}, u32[]{:S(2)}) collective-permute-start(bf16[24,1472]{1,0:T(8,128)(2,1)} %get-tuple-element.81), channel_id=1, source_target_pairs={{0,3},{1,0},{2,1},{3,2},{4,7},{5,4},{6,5},{7,6},{8,11},{9,8},{10,9... | collective-permute-start | bytes 211976 | tf_op jit(solution)/shard_map/ppermute | solution.py:698
  17.6 2.4 %collective-permute-done.2.refs_2_ = bf16[24,1472]{1,0:T(8,128)(2,1)S(1)} collective-permute-done((bf16[24,1472]{1,0:T(8,128)(2,1)}, bf16[24,1472]{1,0:T(8,128)(2,1)S(1)}, u32[]{:S(2)}, u32[]{:S(2)}) %collective-permute-start.2) | collective-permute-done | bytes 70688 | tf_op jit(solution)/shard_map/ppermute | solution.py:698
  25.1 3.3 %collective-permute-start.6 = (bf16[96,2432]{1,0:T(8,128)(2,1)}, bf16[96,2432]{1,0:T(8,128)(2,1)S(1)}, u32[]{:S(2)}, u32[]{:S(2)}) collective-permute-start(bf16[96,2432]{1,0:T(8,128)(2,1)} %shard_map.264), channel_id=1, source_target_pairs={{0,8},{4,12},{8,0},{12,4},{16,24},{20,28},{24,16},{28,20},{1,9},{5... | collective-permute-start | bytes 1400840 | tf_op jit(solution)/shard_map/ppermute | solution.py:708
  32.1 8.0 %collective-permute-done.6 = bf16[96,2432]{1,0:T(8,128)(2,1)S(1)} collective-permute-done((bf16[96,2432]{1,0:T(8,128)(2,1)}, bf16[96,2432]{1,0:T(8,128)(2,1)S(1)}, u32[]{:S(2)}, u32[]{:S(2)}) %collective-permute-start.6) | collective-permute-done | bytes 466976 | tf_op jit(solution)/shard_map/ppermute | solution.py:708
  40.2 3.8 %collective-permute-start.12 = (bf16[256,768]{1,0:T(8,128)(2,1)S(1)}, bf16[256,768]{1,0:T(8,128)(2,1)S(1)}, u32[]{:S(2)}, u32[]{:S(2)}) collective-permute-start(bf16[256,768]{1,0:T(8,128)(2,1)S(1)} %bitcast.43), channel_id=1, source_target_pairs={{0,3},{1,0},{2,1},{3,2},{4,7},{5,4},{6,5},{7,6},{8,11},{9,8},{10,9... | collective-permute-start | bytes 1179656 | tf_op jit(solution)/shard_map/ppermute | solution.py:698
  43.9 7.5 %collective-permute-done.7 = bf16[96,2432]{1,0:T(8,128)(2,1)S(1)} collective-permute-done((bf16[96,2432]{1,0:T(8,128)(2,1)}, bf16[96,2432]{1,0:T(8,128)(2,1)S(1)}, u32[]{:S(2)}, u32[]{:S(2)}) %collective-permute-start.7) | collective-permute-done | bytes 466976 | tf_op jit(solution)/shard_map/ppermute | solution.py:708
  54.8 3.7 %collective-permute-done.12 = bf16[256,768]{1,0:T(8,128)(2,1)S(1)} collective-permute-done((bf16[256,768]{1,0:T(8,128)(2,1)S(1)}, bf16[256,768]{1,0:T(8,128)(2,1)S(1)}, u32[]{:S(2)}, u32[]{:S(2)}) %collective-permute-start.12) | collective-permute-done | bytes 393248 | tf_op jit(solution)/shard_map/ppermute | solution.py:698
  60.4 2.2 %collective-permute-start.16 = (bf16[256,768]{1,0:T(8,128)(2,1)S(1)}, bf16[256,768]{1,0:T(8,128)(2,1)S(1)}, u32[]{:S(2)}, u32[]{:S(2)}) collective-permute-start(bf16[256,768]{1,0:T(8,128)(2,1)S(1)} %bitcast.57), channel_id=1, source_target_pairs={{0,2},{1,3},{2,0},{3,1},{4,6},{5,7},{6,4},{7,5},{8,10},{9,11},{10,... | collective-permute-start | bytes 1179656 | tf_op jit(solution)/shard_map/ppermute | solution.py:698
  63.6 12.3 %shard_map.265 = (bf16[1024,768]{1,0:T(8,128)(2,1)}, bf16[1024,768]{1,0:T(8,128)(2,1)}, bf16[1024,768]{1,0:T(8,128)(2,1)}, bf16[1024,768]{1,0:T(8,128)(2,1)}, bf...) custom-call(s32[10]{0:T(128)} %pad_add_fusion.rank_ref.spot_ref, ...), custom_call_target="tpu_custom_call" | custom-call | flops 10000000000 | tf_op jit(solution)/shard_map/pallas_call | solution.py:678
  76.5 12.1 %shard_map.266 = (bf16[3,1024,1024]{2,1,0:T(8,128)(2,1)}, f32[8,1024]{1,0:T(8,128)}, bf16[192,1024]{1,0:T(8,128)(2,1)}, bf16[256,768]{1,0:T(8,128)(2,1)}, bf16[2...) custom-call(s32[10]{0:T(128)} %pad_add_fusion.rank_ref.spot_ref, ...), custom_call_target="tpu_custom_call" | custom-call | flops 10000000000 | tf_op jit(solution)/shard_map/pallas_call | solution.py:678
  92.1 12.6 %shard_map.267 = (bf16[1024,768]{1,0:T(8,128)(2,1)}, bf16[768,1728]{1,0:T(8,128)(2,1)}, f32[8,768]{1,0:T(8,128)}) custom-call(s32[10]{0:T(128)} %pad_add_fusion.rank_ref.spot_ref, bf16[1024,768]{1,0:T(8,128)(2,1)} %pad_maximum_fusion.1.refs_0_.refs_1_, bf16[1024,768]{1,0:T(8,128)(2,1)} %pad_maximum_fusion.1.refs_0_.refs_1_, ...), custom_call_target="tpu_custom_call" | custom-call | flops 12000000000 | tf_op jit(solution)/shard_map/pallas_call | solution.py:678
  104.7 3.8 %all-to-all-start = ((bf16[8,96,1728]{2,1,0:T(8,128)(2,1)}), bf16[8,96,1728]{2,1,0:T(8,128)(2,1)S(1)}, u32[]{:S(2)}, u32[]{:S(2)}) async-start(bf16[8,96,1728]{2,1,0:T(8,128)(2,1)} %bitcast.52), calls=%async_computation | async-start | bytes 5505024 | tf_op jit(solution)/shard_map/all_to_all | solution.py:725
  108.8 6.9 %collective-permute-start.18 = (bf16[256,768]{1,0:T(8,128)(2,1)}, bf16[256,768]{1,0:T(8,128)(2,1)S(1)}, u32[]{:S(2)}, u32[]{:S(2)}) collective-permute-start(bf16[256,768]{1,0:T(8,128)(2,1)} %get-tuple-element.106), channel_id=1, source_target_pairs={{0,2},{1,3},{2,0},{3,1},{4,6},{5,7},{6,4},{7,5},{8,10},{9,11},{10,... | collective-permute-start | bytes 1179656 | tf_op jit(solution)/shard_map/ppermute | solution.py:698
  115.8 11.3 %shard_map.268 = (f32[192,1024]{1,0:T(8,128)}, f32[3,1024,64]{2,1,0:T(8,128)}, f32[3,1024,64]{2,1,0:T(8,128)}) custom-call(s32[10]{0:T(128)} %pad_add_fusion.rank_ref.spot_ref, bf16[1024,768]{1,0:T(8,128)(2,1)} %pad_maximum_fusion.1.refs_0_.refs_1_, bf16[1024,768]{1,0:T(8,128)(2,1)} %pad_maximum_fusion.1.refs_0_.refs_1_, ...), custom_call_target="tpu_custom_call" | custom-call | flops 10000000000 | tf_op jit(solution)/shard_map/pallas_call | solution.py:678
  127.1 8.8 %shard_map.269 = (bf16[1024,576]{1,0:T(8,128)(2,1)}, f32[8,768]{1,0:T(8,128)}, f32[8,576]{1,0:T(8,128)}, bf16[256,768]{1,0:T(8,128)(2,1)}, bf16[256,768]{1,0:T(8...) custom-call(s32[10]{0:T(128)} %pad_add_fusion.rank_ref.spot_ref, ...), custom_call_target="tpu_custom_call" | custom-call | flops 8000000000 | tf_op jit(solution)/shard_map/pallas_call | solution.py:678
  135.9 10.6 %collective-permute-start.19 = (bf16[256,768]{1,0:T(8,128)(2,1)}, bf16[256,768]{1,0:T(8,128)(2,1)}, u32[]{:S(2)}, u32[]{:S(2)}) collective-permute-start(bf16[256,768]{1,0:T(8,128)(2,1)} %get-tuple-element.115), channel_id=1, source_target_pairs={{0,3},{1,0},{2,1},{3,2},{4,7},{5,4},{6,5},{7,6},{8,11},{9,8},{10,9... | collective-permute-start | bytes 1179656 | tf_op jit(solution)/shard_map/ppermute | solution.py:698
  147.2 6.1 %shard_map.270 = bf16[768,704]{1,0:T(8,128)(2,1)} custom-call(s32[10]{0:T(128)} %pad_add_fusion.rank_ref.spot_ref, bf16[1024,768]{1,0:T(8,128)(2,1)} %get-tuple-element.119.n1_ref, bf16[1024,576]{1,0:T(8,128)(2,1)} %get-tuple-element.120.mixed_ref, f32[8,768]{1,0:T(8,128)} %get-tuple-element.121.sums_ref, f32[8,576]{1,0:T(8,128)} %get-tuple-element.122.gbias_ref, ...), custom_call_target="tpu_custom_call" | custom-call | flops 5000000000 | tf_op jit(solution)/shard_map/pallas_call | solution.py:678
  154.5 4.0 %all-to-all-start.1 = ((bf16[8,96,704]{2,1,0:T(8,128)(2,1)}), bf16[8,96,704]{2,1,0:T(8,128)(2,1)S(1)}, u32[]{:S(2)}, u32[]{:S(2)}) async-start(bf16[8,96,704]{2,1,0:T(8,128)(2,1)} %bitcast.60), calls=%async_computation.1 | async-start | bytes 2359296 | tf_op jit(solution)/shard_map/all_to_all | solution.py:725
  159.3 22.2 %collective-permute-done.20 = bf16[256,768]{1,0:T(8,128)(2,1)} collective-permute-done((bf16[256,768]{1,0:T(8,128)(2,1)}, bf16[256,768]{1,0:T(8,128)(2,1)}, u32[]{:S(2)}, u32[]{:S(2)}) %collective-permute-start.20) | collective-permute-done | bytes 393248 | tf_op jit(solution)/shard_map/ppermute | solution.py:698
  188.1 6.2 %collective-permute-start.25 = (bf16[24,1472]{1,0:T(8,128)(2,1)S(1)}, bf16[24,1472]{1,0:T(8,128)(2,1)S(1)}, u32[]{:S(2)}, u32[]{:S(2)}) collective-permute-start(bf16[24,1472]{1,0:T(8,128)(2,1)S(1)} %get-tuple-element.127), channel_id=1, source_target_pairs={{0,3},{1,0},{2,1},{3,2},{4,7},{5,4},{6,5},{7,6},{8,11},{9,8},{10,9... | collective-permute-start | bytes 211976 | tf_op jit(solution)/shard_map/ppermute | solution.py:698
  196.3 3.1 %fusion.9 = (bf16[256,768]{1,0:T(8,128)(2,1)}, bf16[256,768]{1,0:T(8,128)(2,1)}) fusion(f32[256]{0:T(256)S(1)} %get-tuple-element.154, f32[256]{0:T(256)S(1)} %get-tuple-element.152, f32[256]{0:T(256)} %get-tuple-element.155, f32[256]{0:T(256)S(1)} %rsqrt_bitcast_fusion, bf16[1,2,128,768]{3,2,1,0:T(8,128)(2,1)S(1)} %copy-done.3, ...), kind=kLoop, calls=%fused_computation.16 | loop fusion | flops 5308416 | bytes 4725760 | tf_op jit(solution)/shard_map/convert_element_type | solution.py:950
  202.1 2.2 %shard_map.271 = (f32[24,2304]{1,0:T(8,128)}, f32[24,3072]{1,0:T(8,128)}, f32[24,768]{1,0:T(8,128)}, f32[96,768]{1,0:T(8,128)}, f32[24]{0:T(128)}, /*index=5*/f3...) custom-call(s32[10]{0:T(128)} %pad_add_fusion.rank_ref.spot_ref, ...), custom_call_target="tpu_custom_call" | custom-call | flops 1000000000 | tf_op jit(solution)/shard_map/pallas_call | solution.py:678
  (113 shorter events, 42.0 us)
Async XLA Ops:
  0.7 15.4 %collective-permute-start = (bf16[256,768]{1,0:T(8,128)(2,1)}, bf16[256,768]{1,0:T(8,128)(2,1)S(1)}, u32[]{:S(2)}, u32[]{:S(2)}) collective-permute-start(bf16[256,768]{1,0:T(8,128)(2,1)} %bitcast.41), channel_id=1, source_target_pairs={{0,1},{1,2},{2,3},{3,0},{4,5},{5,6},{6,7},{7,4},{8,9},{9,10},{10,1... | collective-permute-start | bytes 1179656 | tf_op jit(solution)/shard_map/ppermute | solution.py:698
  7.4 10.2 %collective-permute-start.1 = (bf16[24,1472]{1,0:T(8,128)(2,1)}, bf16[24,1472]{1,0:T(8,128)(2,1)S(1)}, u32[]{:S(2)}, u32[]{:S(2)}) collective-permute-start(bf16[24,1472]{1,0:T(8,128)(2,1)} %get-tuple-element.79), channel_id=1, source_target_pairs={{0,1},{1,2},{2,3},{3,0},{4,5},{5,6},{6,7},{7,4},{8,9},{9,10},{10,1... | collective-permute-start | bytes 211976 | tf_op jit(solution)/shard_map/ppermute | solution.py:698
  9.0 11.0 %collective-permute-start.2 = (bf16[24,1472]{1,0:T(8,128)(2,1)}, bf16[24,1472]{1,0:T(8,128)(2,1)S(1)}, u32[]{:S(2)}, u32[]{:S(2)}) collective-permute-start(bf16[24,1472]{1,0:T(8,128)(2,1)} %get-tuple-element.80), channel_id=1, source_target_pairs={{0,2},{1,3},{2,0},{3,1},{4,6},{5,7},{6,4},{7,5},{8,10},{9,11},{10,... | collective-permute-start | bytes 211976 | tf_op jit(solution)/shard_map/ppermute | solution.py:698
  10.0 9.9 %collective-permute-start.3 = (bf16[24,1472]{1,0:T(8,128)(2,1)}, bf16[24,1472]{1,0:T(8,128)(2,1)S(1)}, u32[]{:S(2)}, u32[]{:S(2)}) collective-permute-start(bf16[24,1472]{1,0:T(8,128)(2,1)} %get-tuple-element.81), channel_id=1, source_target_pairs={{0,3},{1,0},{2,1},{3,2},{4,7},{5,4},{6,5},{7,6},{8,11},{9,8},{10,9... | collective-permute-start | bytes 211976 | tf_op jit(solution)/shard_map/ppermute | solution.py:698
  23.2 28.8 %collective-permute-start.5 = (bf16[96,2432]{1,0:T(8,128)(2,1)}, bf16[96,2432]{1,0:T(8,128)(2,1)S(1)}, u32[]{:S(2)}, u32[]{:S(2)}) collective-permute-start(bf16[96,2432]{1,0:T(8,128)(2,1)} %shard_map.264), channel_id=1, source_target_pairs={{0,4},{4,0},{8,12},{12,8},{16,20},{20,16},{24,28},{28,24},{1,5},{5... | collective-permute-start | bytes 1400840 | tf_op jit(solution)/shard_map/ppermute | solution.py:708
  25.1 15.1 %collective-permute-start.6 = (bf16[96,2432]{1,0:T(8,128)(2,1)}, bf16[96,2432]{1,0:T(8,128)(2,1)S(1)}, u32[]{:S(2)}, u32[]{:S(2)}) collective-permute-start(bf16[96,2432]{1,0:T(8,128)(2,1)} %shard_map.264), channel_id=1, source_target_pairs={{0,8},{4,12},{8,0},{12,4},{16,24},{20,28},{24,16},{28,20},{1,9},{5... | collective-permute-start | bytes 1400840 | tf_op jit(solution)/shard_map/ppermute | solution.py:708
  28.4 23.0 %collective-permute-start.7 = (bf16[96,2432]{1,0:T(8,128)(2,1)}, bf16[96,2432]{1,0:T(8,128)(2,1)S(1)}, u32[]{:S(2)}, u32[]{:S(2)}) collective-permute-start(bf16[96,2432]{1,0:T(8,128)(2,1)} %shard_map.264), channel_id=1, source_target_pairs={{0,16},{4,20},{8,24},{12,28},{16,0},{20,4},{24,8},{28,12},{1,17},{... | collective-permute-start | bytes 1400840 | tf_op jit(solution)/shard_map/ppermute | solution.py:708
  29.8 21.8 %collective-permute-start.8 = (bf16[96,2432]{1,0:T(8,128)(2,1)}, bf16[96,2432]{1,0:T(8,128)(2,1)S(1)}, u32[]{:S(2)}, u32[]{:S(2)}) collective-permute-start(bf16[96,2432]{1,0:T(8,128)(2,1)} %shard_map.264), channel_id=1, source_target_pairs={{0,24},{4,28},{8,16},{12,20},{16,8},{20,12},{24,0},{28,4},{1,25},{... | collective-permute-start | bytes 1400840 | tf_op jit(solution)/shard_map/ppermute | solution.py:708
  30.0 24.8 %collective-permute-start.11 = (bf16[256,768]{1,0:T(8,128)(2,1)S(1)}, bf16[256,768]{1,0:T(8,128)(2,1)S(1)}, u32[]{:S(2)}, u32[]{:S(2)}) collective-permute-start(bf16[256,768]{1,0:T(8,128)(2,1)S(1)} %bitcast.42), channel_id=1, source_target_pairs={{0,2},{1,3},{2,0},{3,1},{4,6},{5,7},{6,4},{7,5},{8,10},{9,11},{10,... | collective-permute-start | bytes 1179656 | tf_op jit(solution)/shard_map/ppermute | solution.py:698
  40.2 18.4 %collective-permute-start.12 = (bf16[256,768]{1,0:T(8,128)(2,1)S(1)}, bf16[256,768]{1,0:T(8,128)(2,1)S(1)}, u32[]{:S(2)}, u32[]{:S(2)}) collective-permute-start(bf16[256,768]{1,0:T(8,128)(2,1)S(1)} %bitcast.43), channel_id=1, source_target_pairs={{0,3},{1,0},{2,1},{3,2},{4,7},{5,4},{6,5},{7,6},{8,11},{9,8},{10,9... | collective-permute-start | bytes 1179656 | tf_op jit(solution)/shard_map/ppermute | solution.py:698
  59.8 31.0 %collective-permute-start.15 = (bf16[256,768]{1,0:T(8,128)(2,1)S(1)}, bf16[256,768]{1,0:T(8,128)(2,1)S(1)}, u32[]{:S(2)}, u32[]{:S(2)}) collective-permute-start(bf16[256,768]{1,0:T(8,128)(2,1)S(1)} %bitcast.56), channel_id=1, source_target_pairs={{0,1},{1,2},{2,3},{3,0},{4,5},{5,6},{6,7},{7,4},{8,9},{9,10},{10,1... | collective-permute-start | bytes 1179656 | tf_op jit(solution)/shard_map/ppermute | solution.py:698
  60.4 30.4 %collective-permute-start.16 = (bf16[256,768]{1,0:T(8,128)(2,1)S(1)}, bf16[256,768]{1,0:T(8,128)(2,1)S(1)}, u32[]{:S(2)}, u32[]{:S(2)}) collective-permute-start(bf16[256,768]{1,0:T(8,128)(2,1)S(1)} %bitcast.57), channel_id=1, source_target_pairs={{0,2},{1,3},{2,0},{3,1},{4,6},{5,7},{6,4},{7,5},{8,10},{9,11},{10,... | collective-permute-start | bytes 1179656 | tf_op jit(solution)/shard_map/ppermute | solution.py:698
  62.5 28.2 %collective-permute-start.17 = (bf16[256,768]{1,0:T(8,128)(2,1)S(1)}, bf16[256,768]{1,0:T(8,128)(2,1)S(1)}, u32[]{:S(2)}, u32[]{:S(2)}) collective-permute-start(bf16[256,768]{1,0:T(8,128)(2,1)S(1)} %bitcast.58), channel_id=1, source_target_pairs={{0,3},{1,0},{2,1},{3,2},{4,7},{5,4},{6,5},{7,6},{8,11},{9,8},{10,9... | collective-permute-start | bytes 1179656 | tf_op jit(solution)/shard_map/ppermute | solution.py:698
  88.7 27.1 %collective-permute-start.13 = (bf16[256,768]{1,0:T(8,128)(2,1)}, bf16[256,768]{1,0:T(8,128)(2,1)S(1)}, u32[]{:S(2)}, u32[]{:S(2)}) collective-permute-start(bf16[256,768]{1,0:T(8,128)(2,1)} %get-tuple-element.93), channel_id=1, source_target_pairs={{0,3},{1,0},{2,1},{3,2},{4,7},{5,4},{6,5},{7,6},{8,11},{9,8},{10,9... | collective-permute-start | bytes 1179656 | tf_op jit(solution)/shard_map/ppermute | solution.py:698
  89.9 25.9 %collective-permute-start.14 = (bf16[256,768]{1,0:T(8,128)(2,1)}, bf16[256,768]{1,0:T(8,128)(2,1)}, u32[]{:S(2)}, u32[]{:S(2)}) collective-permute-start(bf16[256,768]{1,0:T(8,128)(2,1)} %get-tuple-element.94), channel_id=1, source_target_pairs={{0,1},{1,2},{2,3},{3,0},{4,5},{5,6},{6,7},{7,4},{8,9},{9,10},{10,1... | collective-permute-start | bytes 1179656 | tf_op jit(solution)/shard_map/ppermute | solution.py:698
  104.7 48.6 %all-to-all-start = ((bf16[8,96,1728]{2,1,0:T(8,128)(2,1)}), bf16[8,96,1728]{2,1,0:T(8,128)(2,1)S(1)}, u32[]{:S(2)}, u32[]{:S(2)}) async-start(bf16[8,96,1728]{2,1,0:T(8,128)(2,1)} %bitcast.52), calls=%async_computation | async-start | bytes 5505024 | tf_op jit(solution)/shard_map/all_to_all | solution.py:725
  108.8 18.3 %collective-permute-start.18 = (bf16[256,768]{1,0:T(8,128)(2,1)}, bf16[256,768]{1,0:T(8,128)(2,1)S(1)}, u32[]{:S(2)}, u32[]{:S(2)}) collective-permute-start(bf16[256,768]{1,0:T(8,128)(2,1)} %get-tuple-element.106), channel_id=1, source_target_pairs={{0,2},{1,3},{2,0},{3,1},{4,6},{5,7},{6,4},{7,5},{8,10},{9,11},{10,... | collective-permute-start | bytes 1179656 | tf_op jit(solution)/shard_map/ppermute | solution.py:698
  135.9 23.4 %collective-permute-start.19 = (bf16[256,768]{1,0:T(8,128)(2,1)}, bf16[256,768]{1,0:T(8,128)(2,1)}, u32[]{:S(2)}, u32[]{:S(2)}) collective-permute-start(bf16[256,768]{1,0:T(8,128)(2,1)} %get-tuple-element.115), channel_id=1, source_target_pairs={{0,3},{1,0},{2,1},{3,2},{4,7},{5,4},{6,5},{7,6},{8,11},{9,8},{10,9... | collective-permute-start | bytes 1179656 | tf_op jit(solution)/shard_map/ppermute | solution.py:698
  146.5 35.0 %collective-permute-start.20 = (bf16[256,768]{1,0:T(8,128)(2,1)}, bf16[256,768]{1,0:T(8,128)(2,1)}, u32[]{:S(2)}, u32[]{:S(2)}) collective-permute-start(bf16[256,768]{1,0:T(8,128)(2,1)} %get-tuple-element.116), channel_id=1, source_target_pairs={{0,2},{1,3},{2,0},{3,1},{4,6},{5,7},{6,4},{7,5},{8,10},{9,11},{10,... | collective-permute-start | bytes 1179656 | tf_op jit(solution)/shard_map/ppermute | solution.py:698
  146.8 34.8 %collective-permute-start.21 = (bf16[256,768]{1,0:T(8,128)(2,1)}, bf16[256,768]{1,0:T(8,128)(2,1)}, u32[]{:S(2)}, u32[]{:S(2)}) collective-permute-start(bf16[256,768]{1,0:T(8,128)(2,1)} %get-tuple-element.117), channel_id=1, source_target_pairs={{0,1},{1,2},{2,3},{3,0},{4,5},{5,6},{6,7},{7,4},{8,9},{9,10},{10,1... | collective-permute-start | bytes 1179656 | tf_op jit(solution)/shard_map/ppermute | solution.py:698
  154.5 32.7 %all-to-all-start.1 = ((bf16[8,96,704]{2,1,0:T(8,128)(2,1)}), bf16[8,96,704]{2,1,0:T(8,128)(2,1)S(1)}, u32[]{:S(2)}, u32[]{:S(2)}) async-start(bf16[8,96,704]{2,1,0:T(8,128)(2,1)} %bitcast.60), calls=%async_computation.1 | async-start | bytes 2359296 | tf_op jit(solution)/shard_map/all_to_all | solution.py:725
  188.1 11.4 %collective-permute-start.25 = (bf16[24,1472]{1,0:T(8,128)(2,1)S(1)}, bf16[24,1472]{1,0:T(8,128)(2,1)S(1)}, u32[]{:S(2)}, u32[]{:S(2)}) collective-permute-start(bf16[24,1472]{1,0:T(8,128)(2,1)S(1)} %get-tuple-element.127), channel_id=1, source_target_pairs={{0,3},{1,0},{2,1},{3,2},{4,7},{5,4},{6,5},{7,6},{8,11},{9,8},{10,9... | collective-permute-start | bytes 211976 | tf_op jit(solution)/shard_map/ppermute | solution.py:698
  194.2 7.2 %collective-permute-start.24 = (bf16[24,1472]{1,0:T(8,128)(2,1)S(1)}, bf16[24,1472]{1,0:T(8,128)(2,1)S(1)}, u32[]{:S(2)}, u32[]{:S(2)}) collective-permute-start(bf16[24,1472]{1,0:T(8,128)(2,1)S(1)} %get-tuple-element.126), channel_id=1, source_target_pairs={{0,2},{1,3},{2,0},{3,1},{4,6},{5,7},{6,4},{7,5},{8,10},{9,11},{10,... | collective-permute-start | bytes 211976 | tf_op jit(solution)/shard_map/ppermute | solution.py:698
  194.3 7.1 %collective-permute-start.23 = (bf16[24,1472]{1,0:T(8,128)(2,1)S(1)}, bf16[24,1472]{1,0:T(8,128)(2,1)S(1)}, u32[]{:S(2)}, u32[]{:S(2)}) collective-permute-start(bf16[24,1472]{1,0:T(8,128)(2,1)S(1)} %get-tuple-element.125), channel_id=1, source_target_pairs={{0,1},{1,2},{2,3},{3,0},{4,5},{5,6},{6,7},{7,4},{8,9},{9,10},{10,1... | collective-permute-start | bytes 211976 | tf_op jit(solution)/shard_map/ppermute | solution.py:698
  (22 other events, 229.6 us)

commit v6 on v5

--- a/solution.py
+++ b/solution.py
@@ -550,7 +550,7 @@
 def attend_back_kernel(spot_ref, *refs, ranks, parts):
     dy_refs, refs = refs[:parts], refs[parts:]
     out_ref, heads_ref, inv_ref, soft_ref, value_ref, key_ref, query_ref, cos_ref, sin_ref = refs[:9]
-    gquery_ref, gkey_ref, gvalue_ref = refs[9:]
+    gquery_ref, low_key_ref, low_value_ref, gkey_ref, gvalue_ref = refs[9:]
     step, own = pl.program_id(0), cos_ref.shape[1]
 
     @pl.when(step == 0)
@@ -578,6 +578,11 @@
     for at in range(ranks):
         pl.when(step == at)(functools.partial(tile, at))
 
+    @pl.when(step == ranks - 1)
+    def _():
+        low_key_ref[...] = gkey_ref[...].astype(bf16)
+        low_value_ref[...] = gvalue_ref[...].astype(bf16)
+
 
 def rear_kernel(spot_ref, *refs, ranks, parts):
     hat_ref, refs = refs[0], refs[1:]
@@ -593,8 +598,8 @@
     cosine, sine = cos_ref[...], sin_ref[...]
     pieces = [gquery_ref[...]]
     for j in range(gkey_ref.shape[0]):
-        pieces += turn(gkey_ref[j].T, cosine, -sine)
-    pieces += [gvalue_ref[j].T for j in range(gvalue_ref.shape[0])]
+        pieces += turn(gkey_ref[j].astype(f32).T, cosine, -sine)
+    pieces += [gvalue_ref[j].astype(f32).T for j in range(gvalue_ref.shape[0])]
     mixed = jnp.concatenate(pieces, axis=0).T
     gbias_ref[0:1] += jnp.sum(mixed, axis=0, keepdims=True)
     low = mixed.astype(bf16)
@@ -884,8 +889,9 @@
            (inverse, upright_tile(8)), (soft, soft_spec), (rows, all_heads(2)),
            (upright, upright_all(1)), (rows, head_tile)] + angles,
         [(shape((cols, count), f32), upright_tile(cols)),
-         (shape((heads, count, HD), f32), whole_block((heads, count, HD))),
-         (shape((heads, count, HD), f32), whole_block((heads, count, HD)))],
+         (shape((heads, count, HD), bf16), whole_block((heads, count, HD))),
+         (shape((heads, count, HD), bf16), whole_block((heads, count, HD)))],
+        [pltpu.VMEM((heads, count, HD), f32), pltpu.VMEM((heads, count, HD), f32)],
         cost=10,
         first=(spot,),
     )

time: 205 us -> 205 us (level)
  no operation moved by 1% of the time
where the time goes in v6:
time: 205 us; the launch traced here: 204 us
  Pallas kernels  68.9 us (34%)
  starting transfers between devices  65.2 us (32%)
  waiting for transfers between devices  50.1 us (24%)
  other arithmetic  12.3 us (6%)
  local copies, waits for them, and re-layouts  5.98 us (3%)
    pallas_call x9, Pallas kernels, call(): pl.pallas_call(kernel, grid_spec=pltpu.PrefetchScalarGridSpec(num_scalar_...  68.9 us
    ppermute x18, starting transfers between devices, shift(): lax.ppermute(block, 'seq', [(k, (k + amount) % ranks) for k in range(rank...  46.7 us
    ppermute x18, waiting for transfers between devices, shift(): lax.ppermute(block, 'seq', [(k, (k + amount) % ranks) for k in range(rank...  32.3 us
    ppermute x6, waiting for transfers between devices, swap(): return lax.ppermute(block, 'dp', [(k, k ^ mask) for k in range(8)])  17.8 us
    all_to_all x2, starting transfers between devices, scatter_dp(): lax.all_to_all(parts.reshape(8, -1, parts.shape[1]), 'dp', 0, 0, tiled=True)  7.8 us
    ppermute x6, starting transfers between devices, swap(): return lax.ppermute(block, 'dp', [(k, k ^ mask) for k in range(8)])  7.26 us
  transfers between devices with their start and end apart: 28, of which 10 were waited for; matrix products, arithmetic and copies ran while one was open for 7% of the time, Pallas kernels for 32%

profile of v6, /device:TPU:0, one launch (start us, length us, event | category | flops | bytes accessed | tf_op | source)
XLA Modules:
  0.0 203.7 jit_solution(227138667895528165)
XLA Ops:
  0.7 3.1 %collective-permute-start = (bf16[256,768]{1,0:T(8,128)(2,1)}, bf16[256,768]{1,0:T(8,128)(2,1)S(1)}, u32[]{:S(2)}, u32[]{:S(2)}) collective-permute-start(bf16[256,768]{1,0:T(8,128)(2,1)} %bitcast.41), channel_id=1, source_target_pairs={{0,1},{1,2},{2,3},{3,0},{4,5},{5,6},{6,7},{7,4},{8,9},{9,10},{10,1... | collective-permute-start | bytes 1179656 | tf_op jit(solution)/shard_map/ppermute | solution.py:703
  5.2 2.2 %shard_map.263 = (bf16[24,1472]{1,0:T(8,128)(2,1)}, bf16[24,1472]{1,0:T(8,128)(2,1)}, bf16[24,1472]{1,0:T(8,128)(2,1)}, bf16[24,1472]{1,0:T(8,128)(2,1)}, bf16[96,192]{1,0:T(8,128)(2,1)}) custom-call(s32[10]{0:T(128)} %pad_add_fusion.rank_ref.spot_ref, bf16[24,3072]{1,0:T(8,128)(2,1)} %up_ref.1, bf16[24,2304]{1,0:T(8,128)(2,1)} %qkv_ref.1, ...), custom_call_target="tpu_custom_call" | custom-call | flops 1000000000 | tf_op jit(solution)/shard_map/pallas_call | solution.py:683
  10.0 2.9 %collective-permute-start.3 = (bf16[24,1472]{1,0:T(8,128)(2,1)}, bf16[24,1472]{1,0:T(8,128)(2,1)S(1)}, u32[]{:S(2)}, u32[]{:S(2)}) collective-permute-start(bf16[24,1472]{1,0:T(8,128)(2,1)} %get-tuple-element.81), channel_id=1, source_target_pairs={{0,3},{1,0},{2,1},{3,2},{4,7},{5,4},{6,5},{7,6},{8,11},{9,8},{10,9... | collective-permute-start | bytes 211976 | tf_op jit(solution)/shard_map/ppermute | solution.py:703
  17.6 2.4 %collective-permute-done.2.refs_2_ = bf16[24,1472]{1,0:T(8,128)(2,1)S(1)} collective-permute-done((bf16[24,1472]{1,0:T(8,128)(2,1)}, bf16[24,1472]{1,0:T(8,128)(2,1)S(1)}, u32[]{:S(2)}, u32[]{:S(2)}) %collective-permute-start.2) | collective-permute-done | bytes 70688 | tf_op jit(solution)/shard_map/ppermute | solution.py:703
  25.1 3.3 %collective-permute-start.6 = (bf16[96,2432]{1,0:T(8,128)(2,1)}, bf16[96,2432]{1,0:T(8,128)(2,1)S(1)}, u32[]{:S(2)}, u32[]{:S(2)}) collective-permute-start(bf16[96,2432]{1,0:T(8,128)(2,1)} %shard_map.264), channel_id=1, source_target_pairs={{0,8},{4,12},{8,0},{12,4},{16,24},{20,28},{24,16},{28,20},{1,9},{5... | collective-permute-start | bytes 1400840 | tf_op jit(solution)/shard_map/ppermute | solution.py:713
  32.1 8.0 %collective-permute-done.6 = bf16[96,2432]{1,0:T(8,128)(2,1)S(1)} collective-permute-done((bf16[96,2432]{1,0:T(8,128)(2,1)}, bf16[96,2432]{1,0:T(8,128)(2,1)S(1)}, u32[]{:S(2)}, u32[]{:S(2)}) %collective-permute-start.6) | collective-permute-done | bytes 466976 | tf_op jit(solution)/shard_map/ppermute | solution.py:713
  40.2 3.8 %collective-permute-start.12 = (bf16[256,768]{1,0:T(8,128)(2,1)S(1)}, bf16[256,768]{1,0:T(8,128)(2,1)S(1)}, u32[]{:S(2)}, u32[]{:S(2)}) collective-permute-start(bf16[256,768]{1,0:T(8,128)(2,1)S(1)} %bitcast.43), channel_id=1, source_target_pairs={{0,3},{1,0},{2,1},{3,2},{4,7},{5,4},{6,5},{7,6},{8,11},{9,8},{10,9... | collective-permute-start | bytes 1179656 | tf_op jit(solution)/shard_map/ppermute | solution.py:703
  43.9 7.5 %collective-permute-done.7 = bf16[96,2432]{1,0:T(8,128)(2,1)S(1)} collective-permute-done((bf16[96,2432]{1,0:T(8,128)(2,1)}, bf16[96,2432]{1,0:T(8,128)(2,1)S(1)}, u32[]{:S(2)}, u32[]{:S(2)}) %collective-permute-start.7) | collective-permute-done | bytes 466976 | tf_op jit(solution)/shard_map/ppermute | solution.py:713
  54.8 3.7 %collective-permute-done.12 = bf16[256,768]{1,0:T(8,128)(2,1)S(1)} collective-permute-done((bf16[256,768]{1,0:T(8,128)(2,1)S(1)}, bf16[256,768]{1,0:T(8,128)(2,1)S(1)}, u32[]{:S(2)}, u32[]{:S(2)}) %collective-permute-start.12) | collective-permute-done | bytes 393248 | tf_op jit(solution)/shard_map/ppermute | solution.py:703
  60.4 2.2 %collective-permute-start.16 = (bf16[256,768]{1,0:T(8,128)(2,1)S(1)}, bf16[256,768]{1,0:T(8,128)(2,1)S(1)}, u32[]{:S(2)}, u32[]{:S(2)}) collective-permute-start(bf16[256,768]{1,0:T(8,128)(2,1)S(1)} %bitcast.57), channel_id=1, source_target_pairs={{0,2},{1,3},{2,0},{3,1},{4,6},{5,7},{6,4},{7,5},{8,10},{9,11},{10,... | collective-permute-start | bytes 1179656 | tf_op jit(solution)/shard_map/ppermute | solution.py:703
  63.6 12.3 %shard_map.265 = (bf16[1024,768]{1,0:T(8,128)(2,1)}, bf16[1024,768]{1,0:T(8,128)(2,1)}, bf16[1024,768]{1,0:T(8,128)(2,1)}, bf16[1024,768]{1,0:T(8,128)(2,1)}, bf...) custom-call(s32[10]{0:T(128)} %pad_add_fusion.rank_ref.spot_ref, ...), custom_call_target="tpu_custom_call" | custom-call | flops 10000000000 | tf_op jit(solution)/shard_map/pallas_call | solution.py:683
  76.5 12.1 %shard_map.266 = (bf16[3,1024,1024]{2,1,0:T(8,128)(2,1)}, f32[8,1024]{1,0:T(8,128)}, bf16[192,1024]{1,0:T(8,128)(2,1)}, bf16[256,768]{1,0:T(8,128)(2,1)}, bf16[2...) custom-call(s32[10]{0:T(128)} %pad_add_fusion.rank_ref.spot_ref, ...), custom_call_target="tpu_custom_call" | custom-call | flops 10000000000 | tf_op jit(solution)/shard_map/pallas_call | solution.py:683
  92.1 12.6 %shard_map.267 = (bf16[1024,768]{1,0:T(8,128)(2,1)}, bf16[768,1728]{1,0:T(8,128)(2,1)}, f32[8,768]{1,0:T(8,128)}) custom-call(s32[10]{0:T(128)} %pad_add_fusion.rank_ref.spot_ref, bf16[1024,768]{1,0:T(8,128)(2,1)} %pad_maximum_fusion.1.refs_0_.refs_1_, bf16[1024,768]{1,0:T(8,128)(2,1)} %pad_maximum_fusion.1.refs_0_.refs_1_, ...), custom_call_target="tpu_custom_call" | custom-call | flops 12000000000 | tf_op jit(solution)/shard_map/pallas_call | solution.py:683
  104.7 3.8 %all-to-all-start = ((bf16[8,96,1728]{2,1,0:T(8,128)(2,1)}), bf16[8,96,1728]{2,1,0:T(8,128)(2,1)S(1)}, u32[]{:S(2)}, u32[]{:S(2)}) async-start(bf16[8,96,1728]{2,1,0:T(8,128)(2,1)} %bitcast.52), calls=%async_computation | async-start | bytes 5505024 | tf_op jit(solution)/shard_map/all_to_all | solution.py:730
  108.8 6.9 %collective-permute-start.18 = (bf16[256,768]{1,0:T(8,128)(2,1)}, bf16[256,768]{1,0:T(8,128)(2,1)S(1)}, u32[]{:S(2)}, u32[]{:S(2)}) collective-permute-start(bf16[256,768]{1,0:T(8,128)(2,1)} %get-tuple-element.106), channel_id=1, source_target_pairs={{0,2},{1,3},{2,0},{3,1},{4,6},{5,7},{6,4},{7,5},{8,10},{9,11},{10,... | collective-permute-start | bytes 1179656 | tf_op jit(solution)/shard_map/ppermute | solution.py:703
  115.8 11.3 %shard_map.268 = (f32[192,1024]{1,0:T(8,128)}, bf16[3,1024,64]{2,1,0:T(8,128)(2,1)}, bf16[3,1024,64]{2,1,0:T(8,128)(2,1)}) custom-call(s32[10]{0:T(128)} %pad_add_fusion.rank_ref.spot_ref, bf16[1024,768]{1,0:T(8,128)(2,1)} %pad_maximum_fusion.1.refs_0_.refs_1_, bf16[1024,768]{1,0:T(8,128)(2,1)} %pad_maximum_fusion.1.refs_0_.refs_1_, ...), custom_call_target="tpu_custom_call" | custom-call | flops 10000000000 | tf_op jit(solution)/shard_map/pallas_call | solution.py:683
  127.1 8.0 %shard_map.269 = (bf16[1024,576]{1,0:T(8,128)(2,1)}, f32[8,768]{1,0:T(8,128)}, f32[8,576]{1,0:T(8,128)}, bf16[256,768]{1,0:T(8,128)(2,1)}, bf16[256,768]{1,0:T(8...) custom-call(s32[10]{0:T(128)} %pad_add_fusion.rank_ref.spot_ref, ...), custom_call_target="tpu_custom_call" | custom-call | flops 8000000000 | tf_op jit(solution)/shard_map/pallas_call | solution.py:683
  135.1 10.7 %collective-permute-start.19 = (bf16[256,768]{1,0:T(8,128)(2,1)}, bf16[256,768]{1,0:T(8,128)(2,1)}, u32[]{:S(2)}, u32[]{:S(2)}) collective-permute-start(bf16[256,768]{1,0:T(8,128)(2,1)} %get-tuple-element.115), channel_id=1, source_target_pairs={{0,3},{1,0},{2,1},{3,2},{4,7},{5,4},{6,5},{7,6},{8,11},{9,8},{10,9... | collective-permute-start | bytes 1179656 | tf_op jit(solution)/shard_map/ppermute | solution.py:703
  146.4 6.1 %shard_map.270 = bf16[768,704]{1,0:T(8,128)(2,1)} custom-call(s32[10]{0:T(128)} %pad_add_fusion.rank_ref.spot_ref, bf16[1024,768]{1,0:T(8,128)(2,1)} %get-tuple-element.119.n1_ref, bf16[1024,576]{1,0:T(8,128)(2,1)} %get-tuple-element.120.mixed_ref, f32[8,768]{1,0:T(8,128)} %get-tuple-element.121.sums_ref, f32[8,576]{1,0:T(8,128)} %get-tuple-element.122.gbias_ref, ...), custom_call_target="tpu_custom_call" | custom-call | flops 5000000000 | tf_op jit(solution)/shard_map/pallas_call | solution.py:683
  153.7 4.0 %all-to-all-start.1 = ((bf16[8,96,704]{2,1,0:T(8,128)(2,1)}), bf16[8,96,704]{2,1,0:T(8,128)(2,1)S(1)}, u32[]{:S(2)}, u32[]{:S(2)}) async-start(bf16[8,96,704]{2,1,0:T(8,128)(2,1)} %bitcast.60), calls=%async_computation.1 | async-start | bytes 2359296 | tf_op jit(solution)/shard_map/all_to_all | solution.py:730
  158.5 22.2 %collective-permute-done.20 = bf16[256,768]{1,0:T(8,128)(2,1)} collective-permute-done((bf16[256,768]{1,0:T(8,128)(2,1)}, bf16[256,768]{1,0:T(8,128)(2,1)}, u32[]{:S(2)}, u32[]{:S(2)}) %collective-permute-start.20) | collective-permute-done | bytes 393248 | tf_op jit(solution)/shard_map/ppermute | solution.py:703
  187.2 6.1 %collective-permute-start.25 = (bf16[24,1472]{1,0:T(8,128)(2,1)S(1)}, bf16[24,1472]{1,0:T(8,128)(2,1)S(1)}, u32[]{:S(2)}, u32[]{:S(2)}) collective-permute-start(bf16[24,1472]{1,0:T(8,128)(2,1)S(1)} %get-tuple-element.127), channel_id=1, source_target_pairs={{0,3},{1,0},{2,1},{3,2},{4,7},{5,4},{6,5},{7,6},{8,11},{9,8},{10,9... | collective-permute-start | bytes 211976 | tf_op jit(solution)/shard_map/ppermute | solution.py:703
  195.6 3.1 %fusion.9 = (bf16[256,768]{1,0:T(8,128)(2,1)}, bf16[256,768]{1,0:T(8,128)(2,1)}) fusion(f32[256]{0:T(256)S(1)} %get-tuple-element.154, f32[256]{0:T(256)S(1)} %get-tuple-element.152, f32[256]{0:T(256)} %get-tuple-element.155, f32[256]{0:T(256)S(1)} %rsqrt_bitcast_fusion, bf16[1,2,128,768]{3,2,1,0:T(8,128)(2,1)S(1)} %copy-done.3, ...), kind=kLoop, calls=%fused_computation.16 | loop fusion | flops 5308416 | bytes 4725760 | tf_op jit(solution)/shard_map/convert_element_type | solution.py:956
  201.3 2.2 %shard_map.271 = (f32[24,2304]{1,0:T(8,128)}, f32[24,3072]{1,0:T(8,128)}, f32[24,768]{1,0:T(8,128)}, f32[96,768]{1,0:T(8,128)}, f32[24]{0:T(128)}, /*index=5*/f3...) custom-call(s32[10]{0:T(128)} %pad_add_fusion.rank_ref.spot_ref, ...), custom_call_target="tpu_custom_call" | custom-call | flops 1000000000 | tf_op jit(solution)/shard_map/pallas_call | solution.py:683
  (113 shorter events, 42.0 us)
Async XLA Ops:
  0.7 15.4 %collective-permute-start = (bf16[256,768]{1,0:T(8,128)(2,1)}, bf16[256,768]{1,0:T(8,128)(2,1)S(1)}, u32[]{:S(2)}, u32[]{:S(2)}) collective-permute-start(bf16[256,768]{1,0:T(8,128)(2,1)} %bitcast.41), channel_id=1, source_target_pairs={{0,1},{1,2},{2,3},{3,0},{4,5},{5,6},{6,7},{7,4},{8,9},{9,10},{10,1... | collective-permute-start | bytes 1179656 | tf_op jit(solution)/shard_map/ppermute | solution.py:703
  7.4 10.2 %collective-permute-start.1 = (bf16[24,1472]{1,0:T(8,128)(2,1)}, bf16[24,1472]{1,0:T(8,128)(2,1)S(1)}, u32[]{:S(2)}, u32[]{:S(2)}) collective-permute-start(bf16[24,1472]{1,0:T(8,128)(2,1)} %get-tuple-element.79), channel_id=1, source_target_pairs={{0,1},{1,2},{2,3},{3,0},{4,5},{5,6},{6,7},{7,4},{8,9},{9,10},{10,1... | collective-permute-start | bytes 211976 | tf_op jit(solution)/shard_map/ppermute | solution.py:703
  9.0 11.0 %collective-permute-start.2 = (bf16[24,1472]{1,0:T(8,128)(2,1)}, bf16[24,1472]{1,0:T(8,128)(2,1)S(1)}, u32[]{:S(2)}, u32[]{:S(2)}) collective-permute-start(bf16[24,1472]{1,0:T(8,128)(2,1)} %get-tuple-element.80), channel_id=1, source_target_pairs={{0,2},{1,3},{2,0},{3,1},{4,6},{5,7},{6,4},{7,5},{8,10},{9,11},{10,... | collective-permute-start | bytes 211976 | tf_op jit(solution)/shard_map/ppermute | solution.py:703
  10.0 9.9 %collective-permute-start.3 = (bf16[24,1472]{1,0:T(8,128)(2,1)}, bf16[24,1472]{1,0:T(8,128)(2,1)S(1)}, u32[]{:S(2)}, u32[]{:S(2)}) collective-permute-start(bf16[24,1472]{1,0:T(8,128)(2,1)} %get-tuple-element.81), channel_id=1, source_target_pairs={{0,3},{1,0},{2,1},{3,2},{4,7},{5,4},{6,5},{7,6},{8,11},{9,8},{10,9... | collective-permute-start | bytes 211976 | tf_op jit(solution)/shard_map/ppermute | solution.py:703
  23.2 28.8 %collective-permute-start.5 = (bf16[96,2432]{1,0:T(8,128)(2,1)}, bf16[96,2432]{1,0:T(8,128)(2,1)S(1)}, u32[]{:S(2)}, u32[]{:S(2)}) collective-permute-start(bf16[96,2432]{1,0:T(8,128)(2,1)} %shard_map.264), channel_id=1, source_target_pairs={{0,4},{4,0},{8,12},{12,8},{16,20},{20,16},{24,28},{28,24},{1,5},{5... | collective-permute-start | bytes 1400840 | tf_op jit(solution)/shard_map/ppermute | solution.py:713
  25.1 15.1 %collective-permute-start.6 = (bf16[96,2432]{1,0:T(8,128)(2,1)}, bf16[96,2432]{1,0:T(8,128)(2,1)S(1)}, u32[]{:S(2)}, u32[]{:S(2)}) collective-permute-start(bf16[96,2432]{1,0:T(8,128)(2,1)} %shard_map.264), channel_id=1, source_target_pairs={{0,8},{4,12},{8,0},{12,4},{16,24},{20,28},{24,16},{28,20},{1,9},{5... | collective-permute-start | bytes 1400840 | tf_op jit(solution)/shard_map/ppermute | solution.py:713
  28.4 23.0 %collective-permute-start.7 = (bf16[96,2432]{1,0:T(8,128)(2,1)}, bf16[96,2432]{1,0:T(8,128)(2,1)S(1)}, u32[]{:S(2)}, u32[]{:S(2)}) collective-permute-start(bf16[96,2432]{1,0:T(8,128)(2,1)} %shard_map.264), channel_id=1, source_target_pairs={{0,16},{4,20},{8,24},{12,28},{16,0},{20,4},{24,8},{28,12},{1,17},{... | collective-permute-start | bytes 1400840 | tf_op jit(solution)/shard_map/ppermute | solution.py:713
  29.8 21.8 %collective-permute-start.8 = (bf16[96,2432]{1,0:T(8,128)(2,1)}, bf16[96,2432]{1,0:T(8,128)(2,1)S(1)}, u32[]{:S(2)}, u32[]{:S(2)}) collective-permute-start(bf16[96,2432]{1,0:T(8,128)(2,1)} %shard_map.264), channel_id=1, source_target_pairs={{0,24},{4,28},{8,16},{12,20},{16,8},{20,12},{24,0},{28,4},{1,25},{... | collective-permute-start | bytes 1400840 | tf_op jit(solution)/shard_map/ppermute | solution.py:713
  30.0 24.8 %collective-permute-start.11 = (bf16[256,768]{1,0:T(8,128)(2,1)S(1)}, bf16[256,768]{1,0:T(8,128)(2,1)S(1)}, u32[]{:S(2)}, u32[]{:S(2)}) collective-permute-start(bf16[256,768]{1,0:T(8,128)(2,1)S(1)} %bitcast.42), channel_id=1, source_target_pairs={{0,2},{1,3},{2,0},{3,1},{4,6},{5,7},{6,4},{7,5},{8,10},{9,11},{10,... | collective-permute-start | bytes 1179656 | tf_op jit(solution)/shard_map/ppermute | solution.py:703
  40.2 18.4 %collective-permute-start.12 = (bf16[256,768]{1,0:T(8,128)(2,1)S(1)}, bf16[256,768]{1,0:T(8,128)(2,1)S(1)}, u32[]{:S(2)}, u32[]{:S(2)}) collective-permute-start(bf16[256,768]{1,0:T(8,128)(2,1)S(1)} %bitcast.43), channel_id=1, source_target_pairs={{0,3},{1,0},{2,1},{3,2},{4,7},{5,4},{6,5},{7,6},{8,11},{9,8},{10,9... | collective-permute-start | bytes 1179656 | tf_op jit(solution)/shard_map/ppermute | solution.py:703
  59.8 31.0 %collective-permute-start.15 = (bf16[256,768]{1,0:T(8,128)(2,1)S(1)}, bf16[256,768]{1,0:T(8,128)(2,1)S(1)}, u32[]{:S(2)}, u32[]{:S(2)}) collective-permute-start(bf16[256,768]{1,0:T(8,128)(2,1)S(1)} %bitcast.56), channel_id=1, source_target_pairs={{0,1},{1,2},{2,3},{3,0},{4,5},{5,6},{6,7},{7,4},{8,9},{9,10},{10,1... | collective-permute-start | bytes 1179656 | tf_op jit(solution)/shard_map/ppermute | solution.py:703
  60.4 30.4 %collective-permute-start.16 = (bf16[256,768]{1,0:T(8,128)(2,1)S(1)}, bf16[256,768]{1,0:T(8,128)(2,1)S(1)}, u32[]{:S(2)}, u32[]{:S(2)}) collective-permute-start(bf16[256,768]{1,0:T(8,128)(2,1)S(1)} %bitcast.57), channel_id=1, source_target_pairs={{0,2},{1,3},{2,0},{3,1},{4,6},{5,7},{6,4},{7,5},{8,10},{9,11},{10,... | collective-permute-start | bytes 1179656 | tf_op jit(solution)/shard_map/ppermute | solution.py:703
  62.5 28.2 %collective-permute-start.17 = (bf16[256,768]{1,0:T(8,128)(2,1)S(1)}, bf16[256,768]{1,0:T(8,128)(2,1)S(1)}, u32[]{:S(2)}, u32[]{:S(2)}) collective-permute-start(bf16[256,768]{1,0:T(8,128)(2,1)S(1)} %bitcast.58), channel_id=1, source_target_pairs={{0,3},{1,0},{2,1},{3,2},{4,7},{5,4},{6,5},{7,6},{8,11},{9,8},{10,9... | collective-permute-start | bytes 1179656 | tf_op jit(solution)/shard_map/ppermute | solution.py:703
  88.7 27.1 %collective-permute-start.13 = (bf16[256,768]{1,0:T(8,128)(2,1)}, bf16[256,768]{1,0:T(8,128)(2,1)S(1)}, u32[]{:S(2)}, u32[]{:S(2)}) collective-permute-start(bf16[256,768]{1,0:T(8,128)(2,1)} %get-tuple-element.93), channel_id=1, source_target_pairs={{0,3},{1,0},{2,1},{3,2},{4,7},{5,4},{6,5},{7,6},{8,11},{9,8},{10,9... | collective-permute-start | bytes 1179656 | tf_op jit(solution)/shard_map/ppermute | solution.py:703
  89.9 25.9 %collective-permute-start.14 = (bf16[256,768]{1,0:T(8,128)(2,1)}, bf16[256,768]{1,0:T(8,128)(2,1)}, u32[]{:S(2)}, u32[]{:S(2)}) collective-permute-start(bf16[256,768]{1,0:T(8,128)(2,1)} %get-tuple-element.94), channel_id=1, source_target_pairs={{0,1},{1,2},{2,3},{3,0},{4,5},{5,6},{6,7},{7,4},{8,9},{9,10},{10,1... | collective-permute-start | bytes 1179656 | tf_op jit(solution)/shard_map/ppermute | solution.py:703
  104.7 47.8 %all-to-all-start = ((bf16[8,96,1728]{2,1,0:T(8,128)(2,1)}), bf16[8,96,1728]{2,1,0:T(8,128)(2,1)S(1)}, u32[]{:S(2)}, u32[]{:S(2)}) async-start(bf16[8,96,1728]{2,1,0:T(8,128)(2,1)} %bitcast.52), calls=%async_computation | async-start | bytes 5505024 | tf_op jit(solution)/shard_map/all_to_all | solution.py:730
  108.8 18.2 %collective-permute-start.18 = (bf16[256,768]{1,0:T(8,128)(2,1)}, bf16[256,768]{1,0:T(8,128)(2,1)S(1)}, u32[]{:S(2)}, u32[]{:S(2)}) collective-permute-start(bf16[256,768]{1,0:T(8,128)(2,1)} %get-tuple-element.106), channel_id=1, source_target_pairs={{0,2},{1,3},{2,0},{3,1},{4,6},{5,7},{6,4},{7,5},{8,10},{9,11},{10,... | collective-permute-start | bytes 1179656 | tf_op jit(solution)/shard_map/ppermute | solution.py:703
  135.1 23.4 %collective-permute-start.19 = (bf16[256,768]{1,0:T(8,128)(2,1)}, bf16[256,768]{1,0:T(8,128)(2,1)}, u32[]{:S(2)}, u32[]{:S(2)}) collective-permute-start(bf16[256,768]{1,0:T(8,128)(2,1)} %get-tuple-element.115), channel_id=1, source_target_pairs={{0,3},{1,0},{2,1},{3,2},{4,7},{5,4},{6,5},{7,6},{8,11},{9,8},{10,9... | collective-permute-start | bytes 1179656 | tf_op jit(solution)/shard_map/ppermute | solution.py:703
  145.8 35.0 %collective-permute-start.20 = (bf16[256,768]{1,0:T(8,128)(2,1)}, bf16[256,768]{1,0:T(8,128)(2,1)}, u32[]{:S(2)}, u32[]{:S(2)}) collective-permute-start(bf16[256,768]{1,0:T(8,128)(2,1)} %get-tuple-element.116), channel_id=1, source_target_pairs={{0,2},{1,3},{2,0},{3,1},{4,6},{5,7},{6,4},{7,5},{8,10},{9,11},{10,... | collective-permute-start | bytes 1179656 | tf_op jit(solution)/shard_map/ppermute | solution.py:703
  146.0 34.8 %collective-permute-start.21 = (bf16[256,768]{1,0:T(8,128)(2,1)}, bf16[256,768]{1,0:T(8,128)(2,1)}, u32[]{:S(2)}, u32[]{:S(2)}) collective-permute-start(bf16[256,768]{1,0:T(8,128)(2,1)} %get-tuple-element.117), channel_id=1, source_target_pairs={{0,1},{1,2},{2,3},{3,0},{4,5},{5,6},{6,7},{7,4},{8,9},{9,10},{10,1... | collective-permute-start | bytes 1179656 | tf_op jit(solution)/shard_map/ppermute | solution.py:703
  153.7 32.6 %all-to-all-start.1 = ((bf16[8,96,704]{2,1,0:T(8,128)(2,1)}), bf16[8,96,704]{2,1,0:T(8,128)(2,1)S(1)}, u32[]{:S(2)}, u32[]{:S(2)}) async-start(bf16[8,96,704]{2,1,0:T(8,128)(2,1)} %bitcast.60), calls=%async_computation.1 | async-start | bytes 2359296 | tf_op jit(solution)/shard_map/all_to_all | solution.py:730
  187.2 11.4 %collective-permute-start.25 = (bf16[24,1472]{1,0:T(8,128)(2,1)S(1)}, bf16[24,1472]{1,0:T(8,128)(2,1)S(1)}, u32[]{:S(2)}, u32[]{:S(2)}) collective-permute-start(bf16[24,1472]{1,0:T(8,128)(2,1)S(1)} %get-tuple-element.127), channel_id=1, source_target_pairs={{0,3},{1,0},{2,1},{3,2},{4,7},{5,4},{6,5},{7,6},{8,11},{9,8},{10,9... | collective-permute-start | bytes 211976 | tf_op jit(solution)/shard_map/ppermute | solution.py:703
  193.4 7.2 %collective-permute-start.24 = (bf16[24,1472]{1,0:T(8,128)(2,1)S(1)}, bf16[24,1472]{1,0:T(8,128)(2,1)S(1)}, u32[]{:S(2)}, u32[]{:S(2)}) collective-permute-start(bf16[24,1472]{1,0:T(8,128)(2,1)S(1)} %get-tuple-element.126), channel_id=1, source_target_pairs={{0,2},{1,3},{2,0},{3,1},{4,6},{5,7},{6,4},{7,5},{8,10},{9,11},{10,... | collective-permute-start | bytes 211976 | tf_op jit(solution)/shard_map/ppermute | solution.py:703
  193.5 7.1 %collective-permute-start.23 = (bf16[24,1472]{1,0:T(8,128)(2,1)S(1)}, bf16[24,1472]{1,0:T(8,128)(2,1)S(1)}, u32[]{:S(2)}, u32[]{:S(2)}) collective-permute-start(bf16[24,1472]{1,0:T(8,128)(2,1)S(1)} %get-tuple-element.125), channel_id=1, source_target_pairs={{0,1},{1,2},{2,3},{3,0},{4,5},{5,6},{6,7},{7,4},{8,9},{9,10},{10,1... | collective-permute-start | bytes 211976 | tf_op jit(solution)/shard_map/ppermute | solution.py:703
  (22 other events, 228.7 us)
